TPU v7x, 128 devices: a whole 4x4x4 slice. The times are simulated.
128 devices in a mesh: lat: 32 (over y, x_lo, z), lon: 4 (over x_hi, core).
Axes of the slice: x: 4 (x_hi: 2, x_lo: 2; x = x_hi * 2 + x_lo), y: 4, z: 4, core: 2. Of those that a mesh axis runs over, the one named last changes fastest.
Arguments:
- obs_feat: bfloat16 [262144, 128], P(('lat', 'lon')), may hold values from -6 to 6
- obs_dest: int32 [262144, 1], P(('lat', 'lon')), may hold values from 0 to 127; in each aligned block of 2048 rows (0 to 2047, 2048 to 4095, ...) at most 32 rows name the same one
- obs_cell: int32 [262144], P(('lat', 'lon')), may hold values from 0 to 3071
- obs_sub: int32 [262144], P(('lat', 'lon')), may hold values from 0 to 255
- background: bfloat16 [768, 512, 512], P('lat', 'lon'), may hold values from -6 to 6
- w_in: bfloat16 [128, 512], replicated, may hold values from -0.5 to 0.5
- dens_vec: float32 [512], replicated, may hold values from -6 to 6
- conv_w: bfloat16 [4, 4, 512, 512], replicated, may hold values from -0.0625 to 0.0625
- conv_b: float32 [512], replicated, may hold values from -3 to 3
- norm_gain: float32 [512], replicated, may hold values from 0.1 to 1.9
- w_qkv: bfloat16 [512, 1536], replicated, may hold values from -0.25 to 0.25
- rel_bias: float32 [8, 13, 13], replicated, may hold values from -6 to 266
- w_out: bfloat16 [512, 512], replicated, may hold values from -0.25 to 0.25
Outputs:
- encoded: bfloat16 [384, 256, 512], P('lat', 'lon')
Inputs may be any that keep to these rules, and one draw needn't show every extreme that they name: `obs_dest`: destination device of each observation, numbered lat index * 4 + lon index; the rows of one device name one destination at most 32 times, and 32 is reached. `obs_cell`: row-major cell inside the destination tile. `obs_sub`: 16 * sub-row + sub-column inside the cell.
All inputs are finite; a program needn't handle non-finite values.
Results may differ from a plain program's by a relative error of at most 0.012.
Values may be sent and summed in bfloat16 or wider, within the bound.
A program may use at most 128 MiB of HBM per device.

v0:
```python
import jax
import jax.numpy as jnp
from jax import lax
from jax.sharding import PartitionSpec as P

HEADS = 8


def extended(x, sides, width, wrap):
    for axis, dim in sides:
        size, length = (lax.axis_size(axis), x.shape[dim])
        up = [(i, (i + 1) % size) for i in range(size if wrap else size - 1)]
        down = [(j, i) for i, j in up]
        last = lax.slice_in_dim(x, length - width, length, axis=dim)
        initial = lax.slice_in_dim(x, 0, width, axis=dim)
        before = lax.ppermute(last, axis, up)
        after = lax.ppermute(initial, axis, down)
        x = jnp.concatenate([before, x, after], axis=dim)
    return x


def kernel_weight(code):
    row_off = (code // 16).astype(jnp.float32)
    col_off = (code % 16).astype(jnp.float32)
    delta_row = (row_off + 0.5) / 16.0 - 0.5
    delta_col = (col_off + 0.5) / 16.0 - 0.5
    return jnp.exp(-(delta_row * delta_row + delta_col * delta_col) / (2.0 * 0.35 * 0.35))


def strided_conv(padded, conv_w, out_rows, out_cols):
    channels = padded.shape[2]
    planes = padded.reshape(out_rows + 1, 2, out_cols + 1, 2, channels)
    total = jnp.zeros((out_rows, out_cols, conv_w.shape[3]), jnp.float32)
    for row_tap in range(4):
        for col_tap in range(4):
            window = planes[
                row_tap // 2 : row_tap // 2 + out_rows,
                row_tap % 2,
                col_tap // 2 : col_tap // 2 + out_cols,
                col_tap % 2,
                :,
            ]
            total = total + jnp.einsum(
                "ijc,cd->ijd", window, conv_w[row_tap, col_tap], preferred_element_type=jnp.float32
            )
    return total.reshape(out_rows * out_cols, conv_w.shape[3])


def attend_rows(query_grid, key_value, row_valid, rel_bias, head_count):
    query_rows, query_cols, channels = query_grid.shape
    window_span = rel_bias.shape[1]
    head_size = channels // head_count
    strip_width = 32
    strip_count = query_cols // strip_width
    key_cols = strip_width + window_span - 1
    col_gap = (
        jnp.arange(key_cols, dtype=jnp.int32)[None, :]
        - jnp.arange(strip_width, dtype=jnp.int32)[:, None]
    )
    col_inside = (col_gap >= 0) & (col_gap < window_span)
    tap_pick = jnp.clip(col_gap, 0, window_span - 1)
    bias_block = jnp.transpose(rel_bias[:, :, tap_pick], (0, 2, 1, 3))
    head_mask = (
        jnp.arange(channels, dtype=jnp.int32)[None, :] // head_size
        == jnp.arange(head_count, dtype=jnp.int32)[:, None]
    )
    head_mask_b = head_mask.astype(jnp.bfloat16)
    head_mask_f = head_mask.astype(jnp.float32)
    scale = head_size ** (-0.5)

    def one_strip(row_at, strip_at):
        zero = jnp.zeros((), jnp.int32)
        col_at = strip_at * strip_width
        query_line = lax.dynamic_slice(
            query_grid, (row_at, col_at, zero), (1, strip_width, channels)
        )[0]
        key_band = lax.dynamic_slice(
            key_value, (row_at, col_at, zero), (window_span, key_cols, 2 * channels)
        )
        valid_band = lax.dynamic_slice(row_valid, (row_at,), (window_span,))
        keys = key_band[:, :, :channels]
        values = key_band[:, :, channels:]
        masked_queries = query_line[None, :, :] * head_mask_b[:, None, :]
        scores = (
            jnp.einsum("hqc,akc->hqak", masked_queries, keys, preferred_element_type=jnp.float32)
            * scale
        )
        scores = scores + bias_block
        inside = col_inside[:, None, :] & valid_band[None, :, None]
        scores = jnp.where(inside[None], scores, -1e30)
        row_peak = jnp.max(scores, axis=(2, 3), keepdims=True)
        exponent = jnp.exp(scores - row_peak)
        weights = (exponent / jnp.sum(exponent, axis=(2, 3), keepdims=True)).astype(jnp.bfloat16)
        blended = jnp.einsum("hqak,akc->hqc", weights, values, preferred_element_type=jnp.float32)
        return jnp.einsum("hqc,hc->qc", blended, head_mask_f).astype(jnp.bfloat16)

    def one_row(row_at):
        strips = lax.map(
            lambda strip_at: one_strip(row_at, strip_at), jnp.arange(strip_count, dtype=jnp.int32)
        )
        return strips.reshape(query_cols, channels)

    rows_out = lax.map(one_row, jnp.arange(query_rows, dtype=jnp.int32))
    return rows_out.reshape(query_rows * query_cols, channels)


def body(
    obs_feat,
    obs_dest,
    obs_cell,
    obs_sub,
    background,
    w_in,
    dens_vec,
    conv_w,
    conv_b,
    norm_gain,
    w_qkv,
    rel_bias,
    w_out,
):
    lat_count = lax.axis_size("lat")
    lon_count = lax.axis_size("lon")
    device_total = lat_count * lon_count
    tile_rows, tile_cols, channels = background.shape
    obs_count, obs_width = obs_feat.shape
    capacity = 2 * obs_count // device_total
    cell_total = tile_rows * tile_cols
    target = obs_dest[:, 0]
    owners = jnp.arange(device_total, dtype=jnp.int32)
    member = (target[:, None] == owners[None, :]).astype(jnp.int32)
    ranking = jnp.sum((jnp.cumsum(member, axis=0) - 1) * member, axis=1)
    position = target * capacity + ranking
    send_feat = (
        jnp.zeros((device_total * capacity, obs_width), jnp.bfloat16).at[position].set(obs_feat)
    )
    send_cell = (
        jnp.full((device_total * capacity,), cell_total, jnp.int32).at[position].set(obs_cell)
    )
    send_code = jnp.zeros((device_total * capacity,), jnp.int32).at[position].set(obs_sub)
    send_meta = jnp.stack(
        [send_cell.reshape(device_total, capacity), send_code.reshape(device_total, capacity)],
        axis=1,
    )
    send_feat = send_feat.reshape(device_total, capacity, obs_width)
    recv_feat, recv_meta = (
        lax.all_to_all(send_feat, ("lat", "lon"), split_axis=0, concat_axis=0, tiled=True),
        lax.all_to_all(send_meta, ("lat", "lon"), split_axis=0, concat_axis=0, tiled=True),
    )
    recv_feat = recv_feat.reshape(device_total * capacity, obs_width)
    recv_cell = recv_meta[:, 0, :].reshape(device_total * capacity)
    recv_code = recv_meta[:, 1, :].reshape(device_total * capacity)
    kernel = kernel_weight(recv_code)
    summed = jax.ops.segment_sum(
        recv_feat.astype(jnp.float32) * kernel[:, None], recv_cell, num_segments=cell_total + 1
    )[:cell_total]
    density = jax.ops.segment_sum(kernel, recv_cell, num_segments=cell_total + 1)[:cell_total]
    normed_obs = (summed / (density[:, None] + 1.0)).astype(jnp.bfloat16)
    lifted = jnp.dot(normed_obs, w_in, preferred_element_type=jnp.float32)
    gridded = (
        background.reshape(cell_total, channels).astype(jnp.float32)
        + lifted
        + density[:, None] * dens_vec[None, :]
    )
    gridded = gridded.astype(jnp.bfloat16).reshape(tile_rows, tile_cols, channels)
    wrapped = extended(gridded, (("lon", 1),), 1, True)
    padded = extended(wrapped, (("lat", 0),), 1, False)
    coarse_rows = tile_rows // 2
    coarse_cols = tile_cols // 2
    conv_sum = strided_conv(padded, conv_w, coarse_rows, coarse_cols) + conv_b[None, :]
    coarse = jax.nn.gelu(conv_sum, approximate=True).astype(jnp.bfloat16)
    coarse_f = coarse.astype(jnp.float32)
    inv_scale = lax.rsqrt(jnp.mean(coarse_f * coarse_f, axis=1, keepdims=True) + 1e-05)
    normed = (coarse_f * inv_scale * norm_gain[None, :]).astype(jnp.bfloat16)
    reach = rel_bias.shape[1] // 2
    projected = jnp.dot(normed, w_qkv, preferred_element_type=jnp.float32).astype(jnp.bfloat16)
    query_flat = projected[:, :channels]
    key_value = projected[:, channels:].reshape(coarse_rows, coarse_cols, 2 * channels)
    key_value = extended(key_value, (("lon", 1),), reach, True)
    key_value = extended(key_value, (("lat", 0),), reach, False)
    global_rows = (
        lax.axis_index("lat") * coarse_rows
        + jnp.arange(coarse_rows + 2 * reach, dtype=jnp.int32)
        - reach
    )
    row_valid = (global_rows >= 0) & (global_rows < lat_count * coarse_rows)
    attended = attend_rows(
        query_flat.reshape(coarse_rows, coarse_cols, channels),
        key_value,
        row_valid,
        rel_bias,
        HEADS,
    )
    encoded = coarse_f + jnp.dot(attended, w_out, preferred_element_type=jnp.float32)
    return encoded.astype(jnp.bfloat16).reshape(coarse_rows, coarse_cols, channels)


def solution(mesh):
    in_specs = (
        P(("lat", "lon"), None),
        P(("lat", "lon"), None),
        P(("lat", "lon")),
        P(("lat", "lon")),
        P("lat", "lon", None),
        P(),
        P(),
        P(),
        P(),
        P(),
        P(),
        P(),
        P(),
    )
    out_specs = P("lat", "lon", None)
    return jax.shard_map(body, mesh=mesh, in_specs=in_specs, out_specs=out_specs, check_vma=False)
```

profile of v0, /device:TPU:9, one launch (start us, length us, event | category | flops | bytes accessed | tf_op | source)
XLA Modules:
  0.0 481.3 jit_solution(12376613610796831408)
XLA Ops:
  2.8 8.2 %scatter_custom_fusion = s32[4096]{0:T(1024)S(1)} fusion(s32[2048]{0:T(1024)S(1)} %bitcast.240, s32[2048]{0:T(1024)} %param.19, s32[]{:T(128)} %constant.145.clone.1), kind=kCustom, calls=%fused_computation.188 | custom fusion | bytes 16896 | tf_op jit(solution)/shard_map/scatter | solution.py:138
  11.1 8.2 %scatter_custom_fusion.1 = s32[4096]{0:T(1024)S(1)} fusion(s32[2048]{0:T(1024)S(1)} %bitcast.241, s32[2048]{0:T(1024)} %param.20, s32[]{:T(128)} %constant.147.clone.1), kind=kCustom, calls=%fused_computation.186 | custom fusion | bytes 16896 | tf_op jit(solution)/shard_map/scatter | solution.py:140
  20.2 10.8 %all-to-all-start = ((s32[128,2,32]{2,1,0:T(2,128)}), s32[128,2,32]{2,1,0:T(2,128)S(1)}, u32[]{:S(2)}, u32[]{:S(2)}) async-start(s32[128,2,32]{2,1,0:T(2,128)} %copy.63), calls=%async_computation | async-start | bytes 262144 | tf_op jit(solution)/shard_map/all_to_all | solution.py:148
  30.9 7.1 %scatter_custom_fusion.2 = bf16[4096,128]{1,0:T(8,128)(2,1)} fusion(s32[2048]{0:T(1024)S(1)} %bitcast.242, bf16[2048,128]{1,0:T(8,128)(2,1)} %param.17, bf16[]{:T(256)} %constant.150.clone.1), kind=kCustom, calls=%fused_computation.146 | custom fusion | bytes 1049088 | tf_op jit(solution)/shard_map/scatter | solution.py:135
  40.0 7.9 %all-to-all-start.1 = ((bf16[128,32,128]{2,1,0:T(8,128)(2,1)}), bf16[128,32,128]{2,1,0:T(8,128)(2,1)S(1)}, u32[]{:S(2)}, u32[]{:S(2)}) async-start(bf16[128,32,128]{2,1,0:T(8,128)(2,1)} %bitcast.21), calls=%async_computation.1 | async-start | bytes 2097152 | tf_op jit(solution)/shard_map/all_to_all | solution.py:147
  48.4 24.7 %scatter_custom_fusion.4 = f32[3073]{0:T(1024)S(1)} fusion(s32[4096]{0:T(1024)S(1)} %reshape.258, f32[4096]{0:T(1024)S(1)} %fusion.110, f32[]{:T(128)} %constant.144.clone.1), kind=kCustom, calls=%fused_computation.184 | custom fusion | flops 4096 | bytes 12296 | tf_op jit(solution)/shard_map/scatter-add | solution.py:157
  73.2 26.7 %scatter_custom_fusion.3 = f32[3073,128]{1,0:T(8,128)} fusion(s32[4096]{0:T(1024)S(1)} %reshape.258, bf16[4096,128]{1,0:T(8,128)(2,1)S(1)} %bitcast.233, f32[4096]{0:T(1024)S(1)} %fusion.110, f32[]{:T(128)} %constant.144.clone.1), kind=kCustom, calls=%fused_computation.43 | custom fusion | flops 1572864 | bytes 2638340 | tf_op jit(solution)/shard_map/scatter-add | solution.py:154
  99.9 4.5 fusion.20
  107.1 4.2 collective-permute-done.1
  111.5 4.6 collective-permute-start.2
  116.1 3.6 collective-permute-start.3
  122.7 3.3 pad_maximum_fusion.1
  126.0 8.0 %reshape.216 = bf16[13,2,65,2,512]{4,3,2,1,0:T(2,128)(2,1)} reshape(bf16[26,130,512]{2,1,0:T(8,128)(2,1)} %pad_maximum_fusion.1) | data formatting | bytes 6922240 | tf_op jit(solution)/shard_map/reshape | solution.py:32
  134.1 35.8 %fusion.130 = (bf16[12,1,64,1,512]{4,3,2,1,0:T(2,128)(2,1)}, bf16[12,1,64,1,512]{4,3,2,1,0:T(2,128)(2,1)S(1)}, bf16[12,1,64,1,512]{4,3,2,1,0:T(2,128)(2,1)S(1)},...) fusion(bf16[13,2,65,2,512]{4,3,2,1,0:T(2,128)(2,1)} %reshape.216), kind=kLoop, calls=%fused_computation.200 | loop fusion | bytes 25165824 | tf_op jit(solution)/shard_map/slice | solution.py:36
  190.9 6.5 %multiply_reduce_fusion = (f32[12,64]{1,0:T(8,128)S(1)}, f32[12,64,512]{2,1,0:T(8,128)}) fusion(f32[512]{0:T(512)S(1)} %copy-done.8, bf16[4,4,512,512]{3,2,1,0:T(8,128)(2,1)S(1)} %bitcast.232, bf16[12,1,64,1,512]{4,3,2,1,0:T(2,128)(2,1)} %get-tuple-element.313, f32[12,64,512]{2,1,0:T(8,128)S(1)} %fusion.49, f32[12,64,512]{2,1,0:T(8,128)S(1)} %fusion.50, ...), kind=kOutput, calls=%fused_computation.69 | convolution fusion | flops 413662464 | bytes 26481664 | tf_op jit(solution)/shard_map/ijc,cd->ijd/dot_general | solution.py:43
  197.4 2.0 fusion.32
  203.2 2.2 collective-permute-start.4
  205.3 2.6 collective-permute-done.4
  208.0 4.2 collective-permute-done.5
  214.4 3.1 collective-permute-start.6
  217.6 5.1 %collective-permute-start.7 = (bf16[6,76,1024]{2,1,0:T(8,128)(2,1)}, bf16[6,76,1024]{2,1,0:T(8,128)(2,1)}, u32[]{:S(2)}, u32[]{:S(2)}) collective-permute-start(bf16[6,76,1024]{2,1,0:T(8,128)(2,1)} %get-tuple-element.334), channel_id=1, source_target_pairs={{4,0},{8,4},{12,8},{16,12},{20,16},{24,20},{28,24},{32,28},{36,32}... | collective-permute-start | bytes 2801672 | tf_op jit(solution)/shard_map/ppermute | solution.py:17
  223.0 5.5 %gather_fusion = f32[1408,8,13]{2,1,0:T(8,128)} fusion(f32[8,13,13]{1,0,2:T(8,128)S(1)} %copy.80, s32[2048]{0:T(1024)S(1)} %pad_clamp_fusion), kind=kCustom, calls=%fused_computation | custom fusion | bytes 1177088 | tf_op jit(solution)/shard_map/gather | solution.py:62
  228.5 4.7 copy.82
  233.3 2.1 slice.228
  235.3 7.3 %collective-permute-done.6 = bf16[6,76,1024]{2,1,0:T(8,128)(2,1)} collective-permute-done((bf16[6,76,1024]{2,1,0:T(8,128)(2,1)}, bf16[6,76,1024]{2,1,0:T(8,128)(2,1)}, u32[]{:S(2)}, u32[]{:S(2)}) %collective-permute-start.6) | collective-permute-done | bytes 933920 | tf_op jit(solution)/shard_map/ppermute | solution.py:16
  243.5 3.8 pad_maximum_fusion
  247.3 230.9 %while.27 = (s32[]{:T(128)}, bf16[12,64,512]{2,1,0:T(8,128)(2,1)}, s32[12]{0:T(128)S(1)}, pred[24]{0:T(512)(128)(4,1)S(1)}, bf16[12,64,512]{2,1,0:T(8,128)(2,1)}...) while((s32[]{:T(128)}, bf16[12,64,512]{2,1,0:T(8,128)(2,1)}, ...), condition=%wide.region_14.15_spmd.clone.clone, body=%wide.region_9.14_spmd.clone.clone.sunk | while | flops 302016384 | bytes 4046547 | solution.py:103
  251.7 14.2 %while.28 = (s32[]{:T(128)}, bf16[2,32,512]{2,1,0:T(8,128)(2,1)S(1)}, pred[32,44]{1,0:T(8,128)(4,1)S(1)}, pred[13]{0:T(512)(128)(4,1)S(1)}, s32[2]{0:T(128)}, /*...) while((s32[]{:T(128)}, ...), condition=%wide.region_13.13_spmd, body=%wide.region_10.12_spmd.sunk | while | flops 301998464 | bytes 3886505 | solution.py:98
  254.5 1.9 fusion.145
  256.9 1.9 fusion.147
  271.0 14.2 %while.28 = (s32[]{:T(128)}, bf16[2,32,512]{2,1,0:T(8,128)(2,1)S(1)}, pred[32,44]{1,0:T(8,128)(4,1)S(1)}, pred[13]{0:T(512)(128)(4,1)S(1)}, s32[2]{0:T(128)}, /*...) while((s32[]{:T(128)}, ...), condition=%wide.region_13.13_spmd, body=%wide.region_10.12_spmd.sunk | while | flops 301998464 | bytes 3886505 | solution.py:98
  273.8 1.9 fusion.145
  276.2 1.9 fusion.147
  290.2 14.2 %while.28 = (s32[]{:T(128)}, bf16[2,32,512]{2,1,0:T(8,128)(2,1)S(1)}, pred[32,44]{1,0:T(8,128)(4,1)S(1)}, pred[13]{0:T(512)(128)(4,1)S(1)}, s32[2]{0:T(128)}, /*...) while((s32[]{:T(128)}, ...), condition=%wide.region_13.13_spmd, body=%wide.region_10.12_spmd.sunk | while | flops 301998464 | bytes 3886505 | solution.py:98
  293.0 1.9 fusion.145
  295.4 1.9 fusion.147
  309.5 14.2 %while.28 = (s32[]{:T(128)}, bf16[2,32,512]{2,1,0:T(8,128)(2,1)S(1)}, pred[32,44]{1,0:T(8,128)(4,1)S(1)}, pred[13]{0:T(512)(128)(4,1)S(1)}, s32[2]{0:T(128)}, /*...) while((s32[]{:T(128)}, ...), condition=%wide.region_13.13_spmd, body=%wide.region_10.12_spmd.sunk | while | flops 301998464 | bytes 3886505 | solution.py:98
  312.3 1.9 fusion.145
  314.6 1.9 fusion.147
  328.7 14.2 %while.28 = (s32[]{:T(128)}, bf16[2,32,512]{2,1,0:T(8,128)(2,1)S(1)}, pred[32,44]{1,0:T(8,128)(4,1)S(1)}, pred[13]{0:T(512)(128)(4,1)S(1)}, s32[2]{0:T(128)}, /*...) while((s32[]{:T(128)}, ...), condition=%wide.region_13.13_spmd, body=%wide.region_10.12_spmd.sunk | while | flops 301998464 | bytes 3886505 | solution.py:98
  331.5 1.9 fusion.145
  333.9 1.9 fusion.147
  348.0 14.2 %while.28 = (s32[]{:T(128)}, bf16[2,32,512]{2,1,0:T(8,128)(2,1)S(1)}, pred[32,44]{1,0:T(8,128)(4,1)S(1)}, pred[13]{0:T(512)(128)(4,1)S(1)}, s32[2]{0:T(128)}, /*...) while((s32[]{:T(128)}, ...), condition=%wide.region_13.13_spmd, body=%wide.region_10.12_spmd.sunk | while | flops 301998464 | bytes 3886505 | solution.py:98
  350.7 1.9 fusion.145
  353.1 1.9 fusion.147
  367.2 14.2 %while.28 = (s32[]{:T(128)}, bf16[2,32,512]{2,1,0:T(8,128)(2,1)S(1)}, pred[32,44]{1,0:T(8,128)(4,1)S(1)}, pred[13]{0:T(512)(128)(4,1)S(1)}, s32[2]{0:T(128)}, /*...) while((s32[]{:T(128)}, ...), condition=%wide.region_13.13_spmd, body=%wide.region_10.12_spmd.sunk | while | flops 301998464 | bytes 3886505 | solution.py:98
  370.0 1.9 fusion.145
  372.3 1.9 fusion.147
  386.4 14.2 %while.28 = (s32[]{:T(128)}, bf16[2,32,512]{2,1,0:T(8,128)(2,1)S(1)}, pred[32,44]{1,0:T(8,128)(4,1)S(1)}, pred[13]{0:T(512)(128)(4,1)S(1)}, s32[2]{0:T(128)}, /*...) while((s32[]{:T(128)}, ...), condition=%wide.region_13.13_spmd, body=%wide.region_10.12_spmd.sunk | while | flops 301998464 | bytes 3886505 | solution.py:98
  389.2 1.9 fusion.145
  391.6 1.9 fusion.147
  405.7 14.2 %while.28 = (s32[]{:T(128)}, bf16[2,32,512]{2,1,0:T(8,128)(2,1)S(1)}, pred[32,44]{1,0:T(8,128)(4,1)S(1)}, pred[13]{0:T(512)(128)(4,1)S(1)}, s32[2]{0:T(128)}, /*...) while((s32[]{:T(128)}, ...), condition=%wide.region_13.13_spmd, body=%wide.region_10.12_spmd.sunk | while | flops 301998464 | bytes 3886505 | solution.py:98
  408.5 1.9 fusion.145
  410.8 1.9 fusion.147
  424.9 14.2 %while.28 = (s32[]{:T(128)}, bf16[2,32,512]{2,1,0:T(8,128)(2,1)S(1)}, pred[32,44]{1,0:T(8,128)(4,1)S(1)}, pred[13]{0:T(512)(128)(4,1)S(1)}, s32[2]{0:T(128)}, /*...) while((s32[]{:T(128)}, ...), condition=%wide.region_13.13_spmd, body=%wide.region_10.12_spmd.sunk | while | flops 301998464 | bytes 3886505 | solution.py:98
  427.7 1.9 fusion.145
  430.1 1.9 fusion.147
  444.2 14.2 %while.28 = (s32[]{:T(128)}, bf16[2,32,512]{2,1,0:T(8,128)(2,1)S(1)}, pred[32,44]{1,0:T(8,128)(4,1)S(1)}, pred[13]{0:T(512)(128)(4,1)S(1)}, s32[2]{0:T(128)}, /*...) while((s32[]{:T(128)}, ...), condition=%wide.region_13.13_spmd, body=%wide.region_10.12_spmd.sunk | while | flops 301998464 | bytes 3886505 | solution.py:98
  447.0 1.9 fusion.145
  449.3 1.9 fusion.147
  463.4 14.2 %while.28 = (s32[]{:T(128)}, bf16[2,32,512]{2,1,0:T(8,128)(2,1)S(1)}, pred[32,44]{1,0:T(8,128)(4,1)S(1)}, pred[13]{0:T(512)(128)(4,1)S(1)}, s32[2]{0:T(128)}, /*...) while((s32[]{:T(128)}, ...), condition=%wide.region_13.13_spmd, body=%wide.region_10.12_spmd.sunk | while | flops 301998464 | bytes 3886505 | solution.py:98
  466.2 1.9 fusion.145
  468.6 1.9 fusion.147
  478.2 3.1 fusion.24
  (316 shorter events, 170.7 us)
Async XLA Ops:
  0.0 200.3 %copy-start = (bf16[512,1536]{1,0:T(8,128)(2,1)S(1)}, bf16[512,1536]{1,0:T(8,128)(2,1)}, u32[]{:S(2)}) copy-start(bf16[512,1536]{1,0:T(8,128)(2,1)} %param.27) | copy-start | bytes 4718596
  1.4 0.7 copy-start.6
  20.2 19.8 %all-to-all-start = ((s32[128,2,32]{2,1,0:T(2,128)}), s32[128,2,32]{2,1,0:T(2,128)S(1)}, u32[]{:S(2)}, u32[]{:S(2)}) async-start(s32[128,2,32]{2,1,0:T(2,128)} %copy.63), calls=%async_computation | async-start | bytes 262144 | tf_op jit(solution)/shard_map/all_to_all | solution.py:148
  40.0 33.2 %all-to-all-start.1 = ((bf16[128,32,128]{2,1,0:T(8,128)(2,1)}), bf16[128,32,128]{2,1,0:T(8,128)(2,1)S(1)}, u32[]{:S(2)}, u32[]{:S(2)}) async-start(bf16[128,32,128]{2,1,0:T(8,128)(2,1)} %bitcast.21), calls=%async_computation.1 | async-start | bytes 2097152 | tf_op jit(solution)/shard_map/all_to_all | solution.py:147
  47.8 52.0 %copy-start.9 = (bf16[128,512]{1,0:T(8,128)(2,1)S(1)}, bf16[128,512]{1,0:T(8,128)(2,1)}, u32[]{:S(2)}) copy-start(bf16[128,512]{1,0:T(8,128)(2,1)} %param.22) | copy-start | bytes 393220
  47.8 52.0 %copy-start.10 = (f32[512]{0:T(512)S(1)}, f32[512]{0:T(512)}, u32[]{:S(2)}) copy-start(f32[512]{0:T(512)} %param.23) | copy-start | bytes 6148
  104.5 2.7 collective-permute-start
  105.9 5.5 %collective-permute-start.1 = (bf16[24,1,512]{2,1,0:T(2,128)(2,1)S(1)}, bf16[24,1,512]{2,1,0:T(2,128)(2,1)S(1)}, u32[]{:S(2)}, u32[]{:S(2)}) collective-permute-start(bf16[24,1,512]{2,1,0:T(2,128)(2,1)S(1)} %get-tuple-element.332), channel_id=1, source_target_pairs={{1,0},{2,1},{3,2},{0,3},{5,4},{6,5},{7,6},{4,7},{9,8},{10,9},{11,1... | collective-permute-start | bytes 73736 | tf_op jit(solution)/shard_map/ppermute | solution.py:17
  111.5 9.8 %collective-permute-start.2 = (bf16[1,130,512]{2,1,0:T(8,128)(2,1)S(1)}, bf16[1,130,512]{2,1,0:T(8,128)(2,1)S(1)}, u32[]{:S(2)}, u32[]{:S(2)}) collective-permute-start(bf16[1,130,512]{2,1,0:T(8,128)(2,1)S(1)} %get-tuple-element.329), channel_id=1, source_target_pairs={{0,4},{4,8},{8,12},{12,16},{16,20},{20,24},{24,28},{28,32},{32,36}... | collective-permute-start | bytes 399368 | tf_op jit(solution)/shard_map/ppermute | solution.py:16
  116.1 6.6 %collective-permute-start.3 = (bf16[1,130,512]{2,1,0:T(8,128)(2,1)S(1)}, bf16[1,130,512]{2,1,0:T(8,128)(2,1)S(1)}, u32[]{:S(2)}, u32[]{:S(2)}) collective-permute-start(bf16[1,130,512]{2,1,0:T(8,128)(2,1)S(1)} %get-tuple-element.330), channel_id=1, source_target_pairs={{4,0},{8,4},{12,8},{16,12},{20,16},{24,20},{28,24},{32,28},{36,32}... | collective-permute-start | bytes 399368 | tf_op jit(solution)/shard_map/ppermute | solution.py:17
  169.9 10.0 %slice-start = ((s8[8388608]{0:T(1024)(128)(4,1)}), s8[4194304]{0:T(1024)(128)(4,1)S(1)}, s32[]{:S(2)}) async-start(s8[8388608]{0:T(1024)(128)(4,1)} %bitcast.231), calls=%async_computation.2 | async-start | bytes 8388608
  174.9 5.0 %slice-start.1 = ((s8[8388608]{0:T(1024)(128)(4,1)}), s8[4194304]{0:T(1024)(128)(4,1)S(1)}, s32[]{:S(2)}) async-start(s8[8388608]{0:T(1024)(128)(4,1)} %bitcast.231), calls=%async_computation.3 | async-start | bytes 8388608
  189.2 1.7 copy-start.8
  197.4 2.9 copy-start.11
  199.4 0.9 copy-start.3
  201.7 1.4 copy-start.2
  203.2 4.8 collective-permute-start.4
  205.3 6.8 %collective-permute-start.5 = (bf16[12,6,1024]{2,1,0:T(8,128)(2,1)S(1)}, bf16[12,6,1024]{2,1,0:T(8,128)(2,1)S(1)}, u32[]{:S(2)}, u32[]{:S(2)}) collective-permute-start(bf16[12,6,1024]{2,1,0:T(8,128)(2,1)S(1)} %get-tuple-element.336), channel_id=1, source_target_pairs={{1,0},{2,1},{3,2},{0,3},{5,4},{6,5},{7,6},{4,7},{9,8},{10,9},{11,1... | collective-permute-start | bytes 442376 | tf_op jit(solution)/shard_map/ppermute | solution.py:17
  208.0 5.0 %copy-start.4 = (bf16[12,6,1024]{2,1,0:T(8,128)(2,1)}, bf16[12,6,1024]{2,1,0:T(8,128)(2,1)S(1)}, u32[]{:S(2)}) copy-start(bf16[12,6,1024]{2,1,0:T(8,128)(2,1)S(1)} %collective-permute-done.4) | copy-start | bytes 442372
  212.2 0.8 copy-start.5
  213.0 9.8 %copy-start.7 = (f32[8,13,13]{2,0,1:T(8,128)S(1)}, f32[8,13,13]{2,0,1:T(8,128)}, u32[]{:S(2)}) copy-start(f32[8,13,13]{2,0,1:T(8,128)} %param.28) | copy-start | bytes 16228
  214.4 28.2 %collective-permute-start.6 = (bf16[6,76,1024]{2,1,0:T(8,128)(2,1)}, bf16[6,76,1024]{2,1,0:T(8,128)(2,1)}, u32[]{:S(2)}, u32[]{:S(2)}) collective-permute-start(bf16[6,76,1024]{2,1,0:T(8,128)(2,1)} %get-tuple-element.333), channel_id=1, source_target_pairs={{0,4},{4,8},{8,12},{12,16},{16,20},{20,24},{24,28},{28,32},{32,36}... | collective-permute-start | bytes 2801672 | tf_op jit(solution)/shard_map/ppermute | solution.py:16
  217.6 25.9 %collective-permute-start.7 = (bf16[6,76,1024]{2,1,0:T(8,128)(2,1)}, bf16[6,76,1024]{2,1,0:T(8,128)(2,1)}, u32[]{:S(2)}, u32[]{:S(2)}) collective-permute-start(bf16[6,76,1024]{2,1,0:T(8,128)(2,1)} %get-tuple-element.334), channel_id=1, source_target_pairs={{4,0},{8,4},{12,8},{16,12},{20,16},{24,20},{28,24},{32,28},{36,32}... | collective-permute-start | bytes 2801672 | tf_op jit(solution)/shard_map/ppermute | solution.py:17
  478.2 3.1 copy-start.1
where the time goes:
time: 489 us; the launch traced here: 481 us
  local copies, waits for them, and re-layouts  160 us (33%)
  matrix products  128 us (26%)
  other arithmetic  75.2 us (15%)
  loops' own time  53.9 us (11%)
  starting transfers between devices  39.4 us (8%)
  waiting for transfers between devices  24.7 us (5%)
    dot_general x24, matrix products, one_strip(): jnp.einsum('hqc,akc->hqak', masked_queries, keys, preferred_element_type=...  46 us
    dot_general x24, matrix products, one_strip(): jnp.einsum('hqak,akc->hqc', weights, values, preferred_element_type=jnp.f...  45.7 us
    another operation x1, loops' own time, attend_rows(): rows_out = lax.map(one_row, jnp.arange(query_rows, dtype=jnp.int32))  37.7 us
    slice x1, local copies, waits for them, and re-layouts, strided_conv(): planes[row_tap // 2:row_tap // 2 + out_rows, row_tap % 2, col_tap // 2:co...  35.8 us
    dynamic_slice x24, local copies, waits for them, and re-layouts, one_row(): lax.map(lambda strip_at: one_strip(row_at, strip_at), jnp.arange(strip_co...  31.1 us
    dot_general x16, matrix products, strided_conv(): jnp.einsum('ijc,cd->ijd', window, conv_w[row_tap, col_tap], preferred_ele...  27.5 us
    scatter-add x1, other arithmetic, body(): jax.ops.segment_sum(recv_feat.astype(jnp.float32) * kernel[:, None], recv...  26.7 us
    scatter-add x1, other arithmetic, body(): jax.ops.segment_sum(kernel, recv_cell, num_segments=cell_total + 1)  24.7 us
  transfers between devices with their start and end apart: 10, of which 9 were waited for; matrix products, arithmetic and copies ran while one was open for 9% of the time, Pallas kernels for 0%

commit v1 on v0

v1 whole, which is shorter than its diff:
```python
import functools

import jax
import jax.numpy as jnp
from jax import lax
from jax.experimental import pallas as pl
from jax.experimental.pallas import tpu as pltpu
from jax.sharding import PartitionSpec as P

HEADS = 8
F32 = jnp.float32
BF16 = jnp.bfloat16
I32 = jnp.int32
NEG = -1e30


def iota(shape, dim):
    return lax.broadcasted_iota(I32, shape, dim)


def pack_kernel(dest_ref, cell_ref, sub_ref, feat_ref, sendf_ref, sendm_ref, pos_ref, wide_ref):
    obs, width = feat_ref.shape
    owners = sendf_ref.shape[0] // 32
    step = 256
    upper = (iota((step, step), 0) < iota((step, step), 1)).astype(F32).astype(BF16)
    running = jnp.zeros((owners, 1), F32)
    for at in range(0, obs, step):
        dest = dest_ref[:, at : at + step]
        member = (iota((owners, step), 0) == dest).astype(F32)
        earlier = jnp.dot(member.astype(BF16), upper, preferred_element_type=F32) + running
        rank = jnp.sum(member * earlier, axis=0, keepdims=True)
        running = running + jnp.sum(member, axis=1, keepdims=True)
        pos_ref[:, at : at + step] = dest * 32 + rank.astype(I32)
        cell = cell_ref[:, at : at + step]
        sub = sub_ref[:, at : at + step]
        line = iota((width, step), 0)
        meta = jnp.where(
            line == 0,
            ((cell >> 7) + 1).astype(F32),
            jnp.where(
                line == 1,
                (cell & 127).astype(F32),
                jnp.where(line == 2, sub.astype(F32), 0.0),
            ),
        )
        wide_ref[at : at + step, width:] = meta.T.astype(BF16)
        wide_ref[at : at + step, :width] = feat_ref[at : at + step, :]

    @pl.loop(0, owners * 32 // step)
    def _(tile):
        local = pos_ref[...] - tile * step
        local = jnp.where((local >= 0) & (local < step), local, -1).astype(F32).astype(BF16)
        slot = iota((step, obs), 0).astype(F32).astype(BF16)
        pick = jnp.where(slot == local, jnp.ones((), BF16), jnp.zeros((), BF16))
        packed = jnp.dot(pick, wide_ref[...], preferred_element_type=F32)
        at = pl.multiple_of(tile * step, step)
        sendf_ref[pl.ds(at, step), :] = packed[:, :width].astype(BF16)
        meta = packed[:, width:].T
        code = (meta[0:1] * 128.0 + meta[1:2]).astype(I32) * 256 + meta[2:3].astype(I32)
        sendm_ref[:, pl.ds(at, step)] = code


def pack_call(dest, cell, sub, feat, owners):
    obs, width = feat.shape
    return pl.pallas_call(
        pack_kernel,
        name="pack",
        out_shape=(
            jax.ShapeDtypeStruct((owners * 32, width), BF16),
            jax.ShapeDtypeStruct((1, owners * 32), I32),
        ),
        scratch_shapes=[pltpu.VMEM((1, obs), I32), pltpu.VMEM((obs, 2 * width), BF16)],
        compiler_params=pltpu.CompilerParams(vmem_limit_bytes=48 << 20),
    )(dest, cell, sub, feat)


def grid_kernel(
    feat_ref, code_ref, back_ref, win_ref, dens_ref, grid_ref, wide_ref, cell_ref, kern_ref
):
    slots, width = feat_ref.shape
    cells = back_ref.shape[0]
    step = 256
    code = code_ref[...]
    sub = code & 255
    cell_ref[...] = (code >> 8) - 128
    row = ((sub >> 4).astype(F32) + 0.5) / 16.0 - 0.5
    col = ((sub & 15).astype(F32) + 0.5) / 16.0 - 0.5
    kern_ref[...] = jnp.exp(-(row * row + col * col) / (2.0 * 0.35 * 0.35))
    wide_ref[:, :width] = feat_ref[...]
    wide_ref[:, width:] = jnp.ones((slots, width), BF16)

    @pl.loop(0, cells // step)
    def _(tile):
        local = cell_ref[...] - tile * step
        local = jnp.where((local >= 0) & (local < step), local, -1).astype(F32).astype(BF16)
        kern = kern_ref[...].astype(BF16)
        line = iota((step, slots), 0).astype(F32).astype(BF16)
        pick = jnp.where(line == local, kern, jnp.zeros((), BF16))
        total = jnp.dot(pick, wide_ref[...], preferred_element_type=F32)
        density = total[:, width : width + 1]
        normed = (total[:, :width] / (density + 1.0)).astype(BF16)
        at = pl.multiple_of(tile * step, step)
        lifted = jnp.dot(normed, win_ref[...], preferred_element_type=F32)
        value = back_ref[pl.ds(at, step), :].astype(F32) + lifted + density * dens_ref[...]
        grid_ref[pl.ds(at, step), :] = value.astype(BF16)


def grid_call(feat, code, back, w_in, dens_vec):
    slots, width = feat.shape
    return pl.pallas_call(
        grid_kernel,
        name="grid",
        out_shape=jax.ShapeDtypeStruct(back.shape, BF16),
        scratch_shapes=[
            pltpu.VMEM((slots, 2 * width), BF16),
            pltpu.VMEM((1, slots), I32),
            pltpu.VMEM((1, slots), F32),
        ],
        compiler_params=pltpu.CompilerParams(vmem_limit_bytes=48 << 20),
    )(feat, code, back, w_in, dens_vec)


def conv_kernel(
    grid_ref, left_ref, right_ref, top_ref, bottom_ref, w_ref, b_ref, gain_ref,
    coarse_ref, normed_ref, line_ref, taps_ref, side_ref,
):
    rows, cols, channels = grid_ref.shape
    side_ref[0] = left_ref[...].astype(F32)
    side_ref[1] = right_ref[...].astype(F32)
    half = cols // 2

    def lay(at, line, left, right):
        for c in range(channels // 128):
            lanes = slice(c * 128, (c + 1) * 128)
            line_ref[c, 8 : 8 + cols, :] = line[:, lanes].astype(F32)
            line_ref[c, 7:8, :] = left[:, lanes].astype(F32)
            line_ref[c, 8 + cols : 9 + cols, :] = right[:, lanes].astype(F32)
            for tap in range(4):
                part = line_ref[c, pl.ds(7 + tap, half, stride=2), :]
                base = tap * channels + c * 128
                taps_ref[at, :, base : base + 128] = part.astype(BF16)

    lay(0, top_ref[:cols, :], top_ref[cols : cols + 1, :], top_ref[cols + 1 : cols + 2, :])
    lay(
        rows + 1,
        bottom_ref[:cols, :],
        bottom_ref[cols : cols + 1, :],
        bottom_ref[cols + 1 : cols + 2, :],
    )

    @pl.loop(0, rows)
    def _(row):
        lay(row + 1, grid_ref[row], side_ref[0, pl.ds(row, 1), :], side_ref[1, pl.ds(row, 1), :])

    @pl.loop(0, rows // 8)
    def _(part):
        total = jnp.zeros((4 * half, channels), F32)
        for tap in range(4):
            window = jnp.concatenate(
                [taps_ref[part * 8 + 2 * i + tap] for i in range(4)], axis=0
            )
            total = total + jnp.dot(window, w_ref[tap], preferred_element_type=F32)
        total = total + b_ref[...]
        inner = 0.7978845608028654 * (total + 0.044715 * total * total * total)
        coarse = (0.5 * total * (1.0 + jnp.tanh(inner))).astype(BF16)
        at = pl.multiple_of(part * 4 * half, 4 * half)
        coarse_ref[pl.ds(at, 4 * half), :] = coarse
        value = coarse.astype(F32)
        scale = lax.rsqrt(jnp.mean(value * value, axis=1, keepdims=True) + 1e-05)
        normed_ref[pl.ds(at, 4 * half), :] = (value * scale * gain_ref[...]).astype(BF16)


def conv_call(grid, left, right, top, bottom, conv_w, conv_b, norm_gain):
    rows, cols, channels = grid.shape
    out = jax.ShapeDtypeStruct((rows // 2 * cols // 2, channels), BF16)
    return pl.pallas_call(
        conv_kernel,
        name="conv",
        out_shape=(out, out),
        scratch_shapes=[
            pltpu.VMEM((channels // 128, cols + 16, 128), F32),
            pltpu.VMEM((rows + 2, cols // 2, 4 * channels), BF16),
            pltpu.VMEM((2, rows, channels), F32),
        ],
        compiler_params=pltpu.CompilerParams(vmem_limit_bytes=56 << 20),
    )(grid, left, right, top, bottom, conv_w, conv_b, norm_gain)


def attend_kernel(
    normed_ref, ext_ref, wqkv_ref, strip_ref, wout_ref, coarse_ref, out_ref,
    query_ref, key_ref, value_ref, bias_ref,
):
    key_rows, key_cols, channels = ext_ref.shape
    rows, cols = key_rows - 12, key_cols - 16
    half = channels // 2
    head = channels // HEADS
    lat, lat_count = lax.axis_index("lat"), lax.axis_size("lat")
    query_ref[...] = (
        jnp.dot(normed_ref[...], wqkv_ref[:, :channels], preferred_element_type=F32)
        .astype(BF16)
        .reshape(rows, cols, channels)
    )

    @pl.loop(0, key_rows // 4)
    def _(part):
        ext = ext_ref[pl.ds(part * 4, 4)].reshape(4 * key_cols, channels)
        both = jnp.dot(ext, wqkv_ref[:, channels:], preferred_element_type=F32).astype(BF16)
        key_ref[pl.ds(part * 4, 4)] = both[:, :channels].reshape(4, key_cols, channels)
        value_ref[pl.ds(part * 4, 4)] = both[:, channels:].reshape(4, key_cols, channels)

    for h in range(HEADS):
        strip = jnp.broadcast_to(strip_ref[h : h + 1, :], (16, 512))
        for r in range(4):
            at = h * 64 + r * 16
            bias_ref[at : at + 16, :] = pltpu.roll(
                strip, 2 + 32 * r, 1, stride=1, stride_axis=0
            )

    lane_head = iota((64, half), 1) // head

    @pl.loop(0, rows // 4)
    def _(down):
        first = lat * rows - 6 + down * 4
        key_row = first + iota((1, 512), 1) // 32
        edge = jnp.where((key_row >= 0) & (key_row < lat_count * rows), 0.0, NEG)

        @pl.loop(0, cols // 16)
        def _(across):
            c0 = pl.multiple_of(across * 16, 16)
            query = query_ref[pl.ds(down * 4, 4), pl.ds(c0, 16), :].reshape(64, channels)
            query = query * 0.125
            parts = []
            for g in range(2):
                lanes = slice(g * half, (g + 1) * half)
                keys = key_ref[pl.ds(down * 4, 16), pl.ds(c0, 32), lanes].reshape(512, half)
                values = value_ref[pl.ds(down * 4, 16), pl.ds(c0, 32), lanes].reshape(512, half)
                wide = query[:, lanes]
                masked = jnp.concatenate(
                    [jnp.where(lane_head == h, wide, jnp.zeros((), BF16)) for h in range(4)],
                    axis=0,
                )
                scores = lax.dot_general(
                    masked, keys, (((1,), (1,)), ((), ())), preferred_element_type=F32
                )
                scores = scores + bias_ref[g * 256 : (g + 1) * 256, :] + edge
                peak = jnp.max(scores, axis=1, keepdims=True)
                weight = jnp.exp(scores - peak)
                norm = jnp.sum(weight, axis=1, keepdims=True)
                mixed = jnp.dot(weight.astype(BF16), values, preferred_element_type=F32) / norm
                total = jnp.zeros((64, half), F32)
                for h in range(4):
                    total = jnp.where(lane_head == h, mixed[h * 64 : (h + 1) * 64], total)
                parts.append(total.astype(BF16))
            attended = jnp.concatenate(parts, axis=1)
            lifted = jnp.dot(attended, wout_ref[...], preferred_element_type=F32)
            base = coarse_ref[pl.ds(down * 4, 4), pl.ds(c0, 16), :].astype(F32)
            result = base + lifted.reshape(4, 16, channels)
            out_ref[pl.ds(down * 4, 4), pl.ds(c0, 16), :] = result.astype(BF16)


def attend_call(normed, ext, w_qkv, strip, w_out, coarse):
    key_rows, key_cols, channels = ext.shape
    rows, cols = key_rows - 12, key_cols - 16
    return pl.pallas_call(
        attend_kernel,
        name="attend",
        out_shape=jax.ShapeDtypeStruct((rows, cols, channels), BF16),
        scratch_shapes=[
            pltpu.VMEM((rows, cols, channels), BF16),
            pltpu.VMEM((key_rows, key_cols, channels), BF16),
            pltpu.VMEM((key_rows, key_cols, channels), BF16),
            pltpu.VMEM((512, 512), F32),
        ],
        compiler_params=pltpu.CompilerParams(vmem_limit_bytes=48 << 20),
    )(normed, ext, w_qkv, strip, w_out, coarse)


def moved(x, axis, step, wrap):
    size = lax.axis_size(axis)
    pairs = [(i, i + step) for i in range(size) if 0 <= i + step < size]
    if wrap:
        pairs = [(i, (i + step) % size) for i in range(size)]
    return lax.ppermute(x, axis, pairs)


def body(
    obs_feat, obs_dest, obs_cell, obs_sub, background, w_in, dens_vec,
    conv_w, conv_b, norm_gain, w_qkv, rel_bias, w_out,
):
    owners = lax.axis_size("lat") * lax.axis_size("lon")
    rows, cols, channels = background.shape
    obs, width = obs_feat.shape
    sendf, sendm = pack_call(
        obs_dest.reshape(1, obs), obs_cell.reshape(1, obs), obs_sub.reshape(1, obs), obs_feat, owners
    )
    both = ("lat", "lon")
    recvf = lax.all_to_all(sendf.reshape(owners, 32, width), both, 0, 0, tiled=True)
    recvm = lax.all_to_all(sendm.reshape(owners, 32), both, 0, 0, tiled=True)
    grid = grid_call(
        recvf.reshape(owners * 32, width),
        recvm.reshape(1, owners * 32),
        background.reshape(rows * cols, channels),
        w_in,
        dens_vec.reshape(1, channels),
    ).reshape(rows, cols, channels)
    left = moved(grid[:, cols - 1, :], "lon", 1, True)
    right = moved(grid[:, 0, :], "lon", -1, True)
    pad = jnp.zeros((14, channels), BF16)
    top = moved(jnp.concatenate([grid[-1], left[-1:], right[-1:], pad]), "lat", 1, False)
    bottom = moved(jnp.concatenate([grid[0], left[:1], right[:1], pad]), "lat", -1, False)
    coarse, normed = conv_call(
        grid, left, right, top, bottom,
        conv_w.reshape(4, 4 * channels, channels),
        conv_b.reshape(1, channels),
        norm_gain.reshape(1, channels),
    )
    normed3 = normed.reshape(rows // 2, cols // 2, channels)
    before = moved(normed3[:, -8:], "lon", 1, True)
    after = moved(normed3[:, :8], "lon", -1, True)
    ext = jnp.concatenate([before, normed3, after], axis=1)
    over = moved(ext[-6:], "lat", 1, False)
    under = moved(ext[:6], "lat", -1, False)
    ext = jnp.concatenate([over, ext, under], axis=0)
    strip = jnp.pad(rel_bias, ((0, 0), (0, 3), (0, 19)), constant_values=NEG).reshape(HEADS, 512)
    return attend_call(
        normed, ext, w_qkv, strip, w_out, coarse.reshape(rows // 2, cols // 2, channels)
    )


def solution(mesh):
    split = P(("lat", "lon"))
    wide = P(("lat", "lon"), None)
    tile = P("lat", "lon", None)
    in_specs = (wide, wide, split, split, tile) + (P(),) * 8
    return jax.shard_map(body, mesh=mesh, in_specs=in_specs, out_specs=tile, check_vma=False)
```

time: 489 us -> 155 us (0.32); the launches traced: 481 us -> 153 us
  local copies, waits for them, and re-layouts: 160 us -> 7.56 us
  matrix products: 128 us -> 0 us
  other arithmetic: 75.2 us -> 4.18 us
  Pallas kernels: 0 us -> 54.7 us
  loops' own time: 53.9 us -> 0 us
  blocking collectives: 0 us -> 19.1 us
  waiting for transfers between devices: 24.7 us -> 41.4 us
  starting transfers between devices: 39.4 us -> 25.5 us
    dot_general x67 -> x0, matrix products: 128 us -> none  [the longest x24 46 us: one_strip(): jnp.einsum('hqc,akc->hqak', masked_queries, keys, preferred_element_type=...]
    pallas_call x0 -> x4, Pallas kernels: none -> 54.7 us  [the longest x1 15.6 us: attend_call(): pl.pallas_call(attend_kernel, name='attend', out_shape=jax.ShapeDtypeStru...]
    another operation x13 -> x0, loops' own time: 53.9 us -> none  [the longest x1 37.7 us: attend_rows(): rows_out = lax.map(one_row, jnp.arange(query_rows, dtype=jnp.int32))]
    scatter-add x2 -> x0, other arithmetic: 51.4 us -> none  [the longest x1 26.7 us: body(): jax.ops.segment_sum(recv_feat.astype(jnp.float32) * kernel[:, None], recv...]
    dynamic_slice x48 -> x0, local copies, waits for them, and re-layouts: 39.7 us -> none  [the longest x24 31.1 us: one_row(): lax.map(lambda strip_at: one_strip(row_at, strip_at), jnp.arange(strip_co...]
    slice x7 -> x6, local copies, waits for them, and re-layouts: 40 us -> 2.17 us  [the longest x1 1.03 us: body(): over = moved(ext[-6:], 'lat', 1, False)]
    scatter x3 -> x0, local copies, waits for them, and re-layouts: 23.6 us -> none  [the longest x1 8.23 us: body(): jnp.zeros((device_total * capacity,), jnp.int32).at[position].set(obs_sub)]
    all_to_all x0 -> x1, blocking collectives: none -> 19.1 us  [body(): recvm = lax.all_to_all(sendm.reshape(owners, 32), both, 0, 0, tiled=True)]
  transfers between devices with their start and end apart: 10 -> 9, of which waited for: 9 -> 9; matrix products, arithmetic and copies ran while one was open for 9% -> 1% of each run, Pallas kernels for 0% -> 0%
where the time goes in v1:
time: 155 us; the launch traced here: 153 us
  Pallas kernels  54.7 us (35%)
  waiting for transfers between devices  41.4 us (27%)
  starting transfers between devices  25.5 us (16%)
  blocking collectives  19.1 us (12%)
  local copies, waits for them, and re-layouts  7.56 us (5%)
  other arithmetic  4.18 us (3%)
    ppermute x8, waiting for transfers between devices, moved(): return lax.ppermute(x, axis, pairs)  24.5 us
    ppermute x8, starting transfers between devices, moved(): return lax.ppermute(x, axis, pairs)  20 us
    all_to_all x1, blocking collectives, body(): recvm = lax.all_to_all(sendm.reshape(owners, 32), both, 0, 0, tiled=True)  19.1 us
    all_to_all x1, waiting for transfers between devices, body(): lax.all_to_all(sendf.reshape(owners, 32, width), both, 0, 0, tiled=True)  16.9 us
    pallas_call x1, Pallas kernels, attend_call(): pl.pallas_call(attend_kernel, name='attend', out_shape=jax.ShapeDtypeStru...  15.6 us
    pallas_call x1, Pallas kernels, conv_call(): pl.pallas_call(conv_kernel, name='conv', out_shape=(out, out), scratch_sh...  15.1 us
    pallas_call x1, Pallas kernels, grid_call(): pl.pallas_call(grid_kernel, name='grid', out_shape=jax.ShapeDtypeStruct(b...  14.8 us
    pallas_call x1, Pallas kernels, pack_call(): pl.pallas_call(pack_kernel, name='pack', out_shape=(jax.ShapeDtypeStruct(...  9.22 us
  transfers between devices with their start and end apart: 9, of which 9 were waited for; matrix products, arithmetic and copies ran while one was open for 1% of the time, Pallas kernels for 0%

profile of v1, /device:TPU:9, one launch (start us, length us, event | category | flops | bytes accessed | tf_op | source)
XLA Modules:
  0.0 152.8 jit_solution(10033176402206625862)
XLA Ops:
  0.0 0.0 copy-start.5
  0.0 1.0 copy-done.5
  1.0 0.0 copy-start.7
  1.0 0.7 copy-done.7
  1.7 0.0 copy-start.8
  1.7 0.7 copy-done.8
  2.4 0.0 copy-start.9
  2.4 0.7 copy-done.9
  3.1 0.0 copy-start.6
  3.1 9.2 %pack.1 = (bf16[4096,128]{1,0:T(8,128)(2,1)}, s32[1,4096]{1,0:T(1,128)S(1)}) custom-call(s32[1,2048]{1,0:T(1,128)S(1)} %bitcast.27, s32[1,2048]{1,0:T(1,128)S(1)} %bitcast.28, s32[1,2048]{1,0:T(1,128)S(1)} %bitcast.29, bf16[2048,128]{1,0:T(8,128)(2,1)S(1)} %copy-done.5), custom_call_target="tpu_custom_call" | custom-call | tf_op jit(solution)/shard_map/pack/pallas_call | solution.py:65
  12.4 0.5 broadcast.11
  12.9 0.7 reduce.6
  13.6 0.1 all_to_all.10
  13.6 19.1 %all_to_all.14 = s32[128,1,32]{2,1,0:T(1,128)S(1)} all-to-all(s32[128,1,32]{2,1,0:T(1,128)S(1)} %bitcast.33), channel_id=1, replica_groups=mesh['lat'=32,'lon'=4] {'lat','lon'}, dimensions={0} | all-to-all | bytes 32768 | tf_op jit(solution)/shard_map/all_to_all | solution.py:298
  32.8 5.5 %all-to-all-start = ((bf16[128,32,128]{2,1,0:T(8,128)(2,1)}), bf16[128,32,128]{2,1,0:T(8,128)(2,1)S(1)}, u32[]{:S(2)}, u32[]{:S(2)}) async-start(bf16[128,32,128]{2,1,0:T(8,128)(2,1)} %bitcast.3), calls=%async_computation | async-start | bytes 2097152 | tf_op jit(solution)/shard_map/all_to_all | solution.py:297
  38.2 0.1 pad.20.clone
  38.3 0.8 reduce.7
  39.1 0.1 reshape.59.code_ref
  39.2 16.9 %all-to-all-done = bf16[128,32,128]{2,1,0:T(8,128)(2,1)S(1)} async-done(((bf16[128,32,128]{2,1,0:T(8,128)(2,1)}), bf16[128,32,128]{2,1,0:T(8,128)(2,1)S(1)}, u32[]{:S(2)}, u32[]{:S(2)}) %all-to-all-start) | async-done | bytes 1048608 | tf_op jit(solution)/shard_map/all_to_all | solution.py:297
  56.2 0.0 copy-done.6
  56.2 0.0 copy-start.10
  56.2 0.7 copy-done.10
  56.8 14.8 %grid.1 = bf16[3072,512]{1,0:T(8,128)(2,1)S(1)} custom-call(bf16[4096,128]{1,0:T(8,128)(2,1)S(1)} %bitcast.25, s32[1,4096]{1,0:T(1,128)S(1)} %reshape.59.code_ref, bf16[3072,512]{1,0:T(8,128)(2,1)} %bitcast.32, bf16[128,512]{1,0:T(8,128)(2,1)S(1)} %copy-done.6, f32[1,512]{1,0:T(1,128)S(1)} %bitcast.30), custom_call_target="tpu_custom_call" | custom-call | tf_op jit(solution)/shard_map/grid/pallas_call | solution.py:110
  71.6 0.0 copy-start
  71.7 0.1 fusion.1
  71.8 1.9 %collective-permute-start = (bf16[24,512]{1,0:T(8,128)(2,1)S(1)}, bf16[24,512]{1,0:T(8,128)(2,1)S(1)}, u32[]{:S(2)}, u32[]{:S(2)}) collective-permute-start(bf16[24,512]{1,0:T(8,128)(2,1)S(1)} %bitcast.34), channel_id=1, source_target_pairs={{0,1},{1,2},{2,3},{3,0},{4,5},{5,6},{6,7},{7,4},{8,9},{9,10},{10,1... | collective-permute-start | bytes 73736 | tf_op jit(solution)/shard_map/ppermute | solution.py:283
  73.7 0.1 collective-permute-start.1
  73.8 0.8 collective-permute-done.left_ref
  74.6 0.0 copy-start.14
  74.7 3.9 %collective-permute-done.1.right_ref = bf16[24,512]{1,0:T(8,128)(2,1)S(1)} collective-permute-done((bf16[24,512]{1,0:T(8,128)(2,1)S(1)}, bf16[24,512]{1,0:T(8,128)(2,1)S(1)}, u32[]{:S(2)}, u32[]{:S(2)}) %collective-permute-start.1) | collective-permute-done | bytes 24608 | tf_op jit(solution)/shard_map/ppermute | solution.py:283
  78.6 0.0 copy-start.15
  78.6 0.1 maximum_maximum_fusion.1
  78.7 2.5 %collective-permute-start.2 = (bf16[144,512]{1,0:T(8,128)(2,1)S(1)}, bf16[144,512]{1,0:T(8,128)(2,1)S(1)}, u32[]{:S(2)}, u32[]{:S(2)}) collective-permute-start(bf16[144,512]{1,0:T(8,128)(2,1)S(1)} %get-tuple-element.26), channel_id=1, source_target_pairs={{0,4},{4,8},{8,12},{12,16},{16,20},{20,24},{24,28},{28,32},{32,36}... | collective-permute-start | bytes 442376 | tf_op jit(solution)/shard_map/ppermute | solution.py:283
  81.2 5.8 %collective-permute-start.3 = (bf16[144,512]{1,0:T(8,128)(2,1)S(1)}, bf16[144,512]{1,0:T(8,128)(2,1)S(1)}, u32[]{:S(2)}, u32[]{:S(2)}) collective-permute-start(bf16[144,512]{1,0:T(8,128)(2,1)S(1)} %get-tuple-element.25), channel_id=1, source_target_pairs={{4,0},{8,4},{12,8},{16,12},{20,16},{24,20},{28,24},{32,28},{36,32}... | collective-permute-start | bytes 442376 | tf_op jit(solution)/shard_map/ppermute | solution.py:283
  87.0 2.0 %collective-permute-done.2.top_ref = bf16[144,512]{1,0:T(8,128)(2,1)S(1)} collective-permute-done((bf16[144,512]{1,0:T(8,128)(2,1)S(1)}, bf16[144,512]{1,0:T(8,128)(2,1)S(1)}, u32[]{:S(2)}, u32[]{:S(2)}) %collective-permute-start.2) | collective-permute-done | bytes 147488 | tf_op jit(solution)/shard_map/ppermute | solution.py:283
  89.0 1.6 %collective-permute-done.3.bottom_ref = bf16[144,512]{1,0:T(8,128)(2,1)S(1)} collective-permute-done((bf16[144,512]{1,0:T(8,128)(2,1)S(1)}, bf16[144,512]{1,0:T(8,128)(2,1)S(1)}, u32[]{:S(2)}, u32[]{:S(2)}) %collective-permute-start.3) | collective-permute-done | bytes 147488 | tf_op jit(solution)/shard_map/ppermute | solution.py:283
  90.6 0.0 copy-done
  90.6 0.0 copy-done.14
  90.6 0.0 copy-done.15
  90.6 0.0 copy-done.11
  90.6 0.6 copy-done.12
  91.3 15.1 %conv.1 = (bf16[768,512]{1,0:T(8,128)(2,1)}, bf16[768,512]{1,0:T(8,128)(2,1)}) custom-call(bf16[24,128,512]{2,1,0:T(8,128)(2,1)} %bitcast.21, bf16[24,512]{1,0:T(8,128)(2,1)} %copy-done.14, bf16[24,512]{1,0:T(8,128)(2,1)} %copy-done.15, bf16[144,512]{1,0:T(8,128)(2,1)} %copy-done.11, bf16[144,512]{1,0:T(8,128)(2,1)} %copy-done.12, ...), custom_call_target="tpu_custom_call" | custom-call | tf_op jit(solution)/shard_map/conv/pallas_call | solution.py:176
  106.3 1.0 fusion.3
  107.3 0.1 collective-permute-start.4
  107.4 0.6 collective-permute-start.5
  108.0 1.1 collective-permute-done.4
  109.1 4.7 %collective-permute-done.5 = bf16[12,8,512]{2,1,0:T(8,128)(2,1)S(1)} collective-permute-done((bf16[12,8,512]{2,1,0:T(8,128)(2,1)S(1)}, bf16[12,8,512]{2,1,0:T(8,128)(2,1)S(1)}, u32[]{:S(2)}, u32[]{:S(2)}) %collective-permute-start.5) | collective-permute-done | bytes 98336 | tf_op jit(solution)/shard_map/ppermute | solution.py:283
  113.8 1.2 pad_maximum_fusion.1
  115.0 0.0 copy-start.2
  115.0 0.0 copy-start.3
  115.1 1.0 fusion.2
  116.1 2.0 %collective-permute-start.6 = (bf16[6,80,512]{2,1,0:T(8,128)(2,1)}, bf16[6,80,512]{2,1,0:T(8,128)(2,1)}, u32[]{:S(2)}, u32[]{:S(2)}) collective-permute-start(bf16[6,80,512]{2,1,0:T(8,128)(2,1)} %get-tuple-element.17), channel_id=1, source_target_pairs={{0,4},{4,8},{8,12},{12,16},{16,20},{20,24},{24,28},{28,32},{32,36}... | collective-permute-start | bytes 1474568 | tf_op jit(solution)/shard_map/ppermute | solution.py:283
  118.1 7.1 %collective-permute-start.7 = (bf16[6,80,512]{2,1,0:T(8,128)(2,1)}, bf16[6,80,512]{2,1,0:T(8,128)(2,1)}, u32[]{:S(2)}, u32[]{:S(2)}) collective-permute-start(bf16[6,80,512]{2,1,0:T(8,128)(2,1)} %get-tuple-element.18), channel_id=1, source_target_pairs={{4,0},{8,4},{12,8},{16,12},{20,16},{24,20},{28,24},{32,28},{36,32}... | collective-permute-start | bytes 1474568 | tf_op jit(solution)/shard_map/ppermute | solution.py:283
  125.2 0.0 copy-done.13
  125.3 0.1 reshape.67.strip_ref
  125.4 0.0 copy-start.4
  125.4 9.5 %collective-permute-done.6 = bf16[6,80,512]{2,1,0:T(8,128)(2,1)} collective-permute-done((bf16[6,80,512]{2,1,0:T(8,128)(2,1)}, bf16[6,80,512]{2,1,0:T(8,128)(2,1)}, u32[]{:S(2)}, u32[]{:S(2)}) %collective-permute-start.6) | collective-permute-done | bytes 491552 | tf_op jit(solution)/shard_map/ppermute | solution.py:283
  134.9 0.9 collective-permute-done.7
  135.8 0.0 copy-done.1
  135.8 1.3 pad_maximum_fusion.ext_ref
  137.1 0.0 copy-done.2
  137.1 0.0 copy-done.3
  137.1 0.0 copy-done.4
  137.1 15.6 %attend.1 = bf16[12,64,512]{2,1,0:T(8,128)(2,1)} custom-call(bf16[768,512]{1,0:T(8,128)(2,1)S(1)} %copy-done.1, bf16[24,80,512]{2,1,0:T(8,128)(2,1)S(1)} %pad_maximum_fusion.ext_ref, bf16[512,1536]{1,0:T(8,128)(2,1)S(1)} %copy-done.2, f32[8,512]{1,0:T(8,128)S(1)} %reshape.67.strip_ref, bf16[512,512]{1,0:T(8,128)(2,1)S(1)} %copy-done.4, ...), custom_call_target="tpu_custom_call" | custom-call | tf_op jit(solution)/shard_map/attend/pallas_call | solution.py:264
  (12 shorter events, 0.1 us)
Async XLA Ops:
  0.0 1.0 copy-start.5
  1.0 0.7 copy-start.7
  1.7 0.7 copy-start.8
  2.4 0.7 copy-start.9
  3.1 53.0 %copy-start.6 = (bf16[128,512]{1,0:T(8,128)(2,1)S(1)}, bf16[128,512]{1,0:T(8,128)(2,1)}, u32[]{:S(2)}) copy-start(bf16[128,512]{1,0:T(8,128)(2,1)} %win_ref.1) | copy-start | bytes 393220
  32.8 23.4 %all-to-all-start = ((bf16[128,32,128]{2,1,0:T(8,128)(2,1)}), bf16[128,32,128]{2,1,0:T(8,128)(2,1)S(1)}, u32[]{:S(2)}, u32[]{:S(2)}) async-start(bf16[128,32,128]{2,1,0:T(8,128)(2,1)} %bitcast.3), calls=%async_computation | async-start | bytes 2097152 | tf_op jit(solution)/shard_map/all_to_all | solution.py:297
  56.2 0.7 copy-start.10
  71.6 18.9 %copy-start = (bf16[3072,512]{1,0:T(8,128)(2,1)}, bf16[3072,512]{1,0:T(8,128)(2,1)S(1)}, u32[]{:S(2)}) copy-start(bf16[3072,512]{1,0:T(8,128)(2,1)S(1)} %grid.1) | copy-start | bytes 9437188
  71.8 2.9 %collective-permute-start = (bf16[24,512]{1,0:T(8,128)(2,1)S(1)}, bf16[24,512]{1,0:T(8,128)(2,1)S(1)}, u32[]{:S(2)}, u32[]{:S(2)}) collective-permute-start(bf16[24,512]{1,0:T(8,128)(2,1)S(1)} %bitcast.34), channel_id=1, source_target_pairs={{0,1},{1,2},{2,3},{3,0},{4,5},{5,6},{6,7},{7,4},{8,9},{9,10},{10,1... | collective-permute-start | bytes 73736 | tf_op jit(solution)/shard_map/ppermute | solution.py:283
  73.7 4.8 %collective-permute-start.1 = (bf16[24,512]{1,0:T(8,128)(2,1)S(1)}, bf16[24,512]{1,0:T(8,128)(2,1)S(1)}, u32[]{:S(2)}, u32[]{:S(2)}) collective-permute-start(bf16[24,512]{1,0:T(8,128)(2,1)S(1)} %bitcast.35), channel_id=1, source_target_pairs={{0,3},{1,0},{2,1},{3,2},{4,7},{5,4},{6,5},{7,6},{8,11},{9,8},{10,9... | collective-permute-start | bytes 73736 | tf_op jit(solution)/shard_map/ppermute | solution.py:283
  74.6 16.0 %copy-start.14 = (bf16[24,512]{1,0:T(8,128)(2,1)}, bf16[24,512]{1,0:T(8,128)(2,1)S(1)}, u32[]{:S(2)}) copy-start(bf16[24,512]{1,0:T(8,128)(2,1)S(1)} %collective-permute-done.left_ref) | copy-start | bytes 73732
  78.6 12.0 %copy-start.15 = (bf16[24,512]{1,0:T(8,128)(2,1)}, bf16[24,512]{1,0:T(8,128)(2,1)S(1)}, u32[]{:S(2)}) copy-start(bf16[24,512]{1,0:T(8,128)(2,1)S(1)} %collective-permute-done.1.right_ref) | copy-start | bytes 73732
  78.7 10.3 %collective-permute-start.2 = (bf16[144,512]{1,0:T(8,128)(2,1)S(1)}, bf16[144,512]{1,0:T(8,128)(2,1)S(1)}, u32[]{:S(2)}, u32[]{:S(2)}) collective-permute-start(bf16[144,512]{1,0:T(8,128)(2,1)S(1)} %get-tuple-element.26), channel_id=1, source_target_pairs={{0,4},{4,8},{8,12},{12,16},{16,20},{20,24},{24,28},{28,32},{32,36}... | collective-permute-start | bytes 442376 | tf_op jit(solution)/shard_map/ppermute | solution.py:283
  81.2 9.4 %collective-permute-start.3 = (bf16[144,512]{1,0:T(8,128)(2,1)S(1)}, bf16[144,512]{1,0:T(8,128)(2,1)S(1)}, u32[]{:S(2)}, u32[]{:S(2)}) collective-permute-start(bf16[144,512]{1,0:T(8,128)(2,1)S(1)} %get-tuple-element.25), channel_id=1, source_target_pairs={{4,0},{8,4},{12,8},{16,12},{20,16},{24,20},{28,24},{32,28},{36,32}... | collective-permute-start | bytes 442376 | tf_op jit(solution)/shard_map/ppermute | solution.py:283
  89.0 1.6 %copy-start.11 = (bf16[144,512]{1,0:T(8,128)(2,1)}, bf16[144,512]{1,0:T(8,128)(2,1)S(1)}, u32[]{:S(2)}) copy-start(bf16[144,512]{1,0:T(8,128)(2,1)S(1)} %collective-permute-done.2.top_ref) | copy-start | bytes 442372
  90.6 0.7 copy-start.12
  106.3 18.9 %copy-start.13 = (f32[8,13,13]{2,0,1:T(8,128)S(1)}, f32[8,13,13]{2,0,1:T(8,128)}, u32[]{:S(2)}) copy-start(f32[8,13,13]{2,0,1:T(8,128)} %param.24) | copy-start | bytes 16228
  106.3 29.5 %copy-start.1 = (bf16[768,512]{1,0:T(8,128)(2,1)S(1)}, bf16[768,512]{1,0:T(8,128)(2,1)}, u32[]{:S(2)}) copy-start(bf16[768,512]{1,0:T(8,128)(2,1)} %get-tuple-element.11.normed_ref) | copy-start | bytes 2359300
  107.3 1.7 %collective-permute-start.4 = (bf16[12,8,512]{2,1,0:T(8,128)(2,1)S(1)}, bf16[12,8,512]{2,1,0:T(8,128)(2,1)S(1)}, u32[]{:S(2)}, u32[]{:S(2)}) collective-permute-start(bf16[12,8,512]{2,1,0:T(8,128)(2,1)S(1)} %get-tuple-element.19), channel_id=1, source_target_pairs={{0,1},{1,2},{2,3},{3,0},{4,5},{5,6},{6,7},{7,4},{8,9},{9,10},{10,1... | collective-permute-start | bytes 294920 | tf_op jit(solution)/shard_map/ppermute | solution.py:283
  107.4 6.4 %collective-permute-start.5 = (bf16[12,8,512]{2,1,0:T(8,128)(2,1)S(1)}, bf16[12,8,512]{2,1,0:T(8,128)(2,1)S(1)}, u32[]{:S(2)}, u32[]{:S(2)}) collective-permute-start(bf16[12,8,512]{2,1,0:T(8,128)(2,1)S(1)} %get-tuple-element.20), channel_id=1, source_target_pairs={{0,3},{1,0},{2,1},{3,2},{4,7},{5,4},{6,5},{7,6},{8,11},{9,8},{10,9... | collective-permute-start | bytes 294920 | tf_op jit(solution)/shard_map/ppermute | solution.py:283
  115.0 22.1 %copy-start.2 = (bf16[512,1536]{1,0:T(8,128)(2,1)S(1)}, bf16[512,1536]{1,0:T(8,128)(2,1)}, u32[]{:S(2)}) copy-start(bf16[512,1536]{1,0:T(8,128)(2,1)} %wqkv_ref.1) | copy-start | bytes 4718596
  115.0 22.1 %copy-start.3 = (bf16[768,512]{1,0:T(8,128)(2,1)S(1)}, bf16[768,512]{1,0:T(8,128)(2,1)}, u32[]{:S(2)}) copy-start(bf16[768,512]{1,0:T(8,128)(2,1)} %get-tuple-element.12) | copy-start | bytes 2359300
  116.1 18.8 %collective-permute-start.6 = (bf16[6,80,512]{2,1,0:T(8,128)(2,1)}, bf16[6,80,512]{2,1,0:T(8,128)(2,1)}, u32[]{:S(2)}, u32[]{:S(2)}) collective-permute-start(bf16[6,80,512]{2,1,0:T(8,128)(2,1)} %get-tuple-element.17), channel_id=1, source_target_pairs={{0,4},{4,8},{8,12},{12,16},{16,20},{20,24},{24,28},{28,32},{32,36}... | collective-permute-start | bytes 1474568 | tf_op jit(solution)/shard_map/ppermute | solution.py:283
  118.1 17.6 %collective-permute-start.7 = (bf16[6,80,512]{2,1,0:T(8,128)(2,1)}, bf16[6,80,512]{2,1,0:T(8,128)(2,1)}, u32[]{:S(2)}, u32[]{:S(2)}) collective-permute-start(bf16[6,80,512]{2,1,0:T(8,128)(2,1)} %get-tuple-element.18), channel_id=1, source_target_pairs={{4,0},{8,4},{12,8},{16,12},{20,16},{24,20},{28,24},{32,28},{36,32}... | collective-permute-start | bytes 1474568 | tf_op jit(solution)/shard_map/ppermute | solution.py:283
  125.4 11.8 %copy-start.4 = (bf16[512,512]{1,0:T(8,128)(2,1)S(1)}, bf16[512,512]{1,0:T(8,128)(2,1)}, u32[]{:S(2)}) copy-start(bf16[512,512]{1,0:T(8,128)(2,1)} %wout_ref.1) | copy-start | bytes 1572868

commit v2 on v1

--- a/solution.py
+++ b/solution.py
@@ -12,16 +12,33 @@
 BF16 = jnp.bfloat16
 I32 = jnp.int32
 NEG = -1e30
+MESH = pl.DeviceIdType.MESH
 
 
 def iota(shape, dim):
     return lax.broadcasted_iota(I32, shape, dim)
 
 
-def pack_kernel(dest_ref, cell_ref, sub_ref, feat_ref, sendf_ref, sendm_ref, pos_ref, wide_ref):
+def route_kernel(
+    dest_ref, cell_ref, sub_ref, feat_ref, recvf_ref, recvm_ref,
+    pos_ref, wide_ref, sendf_ref, sendm_ref, send_sem, recv_sem, own_sem,
+):
     obs, width = feat_ref.shape
-    owners = sendf_ref.shape[0] // 32
+    owners = sendf_ref.shape[0]
     step = 256
+    lon_count = lax.axis_size("lon")
+    lon = lax.axis_index("lon")
+    me = lax.axis_index("lat") * lon_count + lon
+
+    barrier = pltpu.get_barrier_semaphore()
+
+    @pl.loop(1, owners)
+    def _(k):
+        peer = lax.rem(me + k, owners)
+        pl.semaphore_signal(
+            barrier, inc=1, device_id=(peer // lon_count, lax.rem(peer, lon_count)), device_id_type=MESH
+        )
+
     upper = (iota((step, step), 0) < iota((step, step), 1)).astype(F32).astype(BF16)
     running = jnp.zeros((owners, 1), F32)
     for at in range(0, obs, step):
@@ -46,41 +63,108 @@
         wide_ref[at : at + step, width:] = meta.T.astype(BF16)
         wide_ref[at : at + step, :width] = feat_ref[at : at + step, :]
 
-    @pl.loop(0, owners * 32 // step)
-    def _(tile):
+    pl.semaphore_wait(barrier, owners - 1)
+    tiles = owners * 32 // step
+    peers = step // 32
+    near = (lon - iota((peers, 128), 0)) & 3
+    mine = iota((peers, 128), 1) // 32 == lon
+
+    @pl.loop(0, tiles)
+    def _(turn):
+        tile = lax.rem(turn + me // peers, tiles)
         local = pos_ref[...] - tile * step
         local = jnp.where((local >= 0) & (local < step), local, -1).astype(F32).astype(BF16)
         slot = iota((step, obs), 0).astype(F32).astype(BF16)
         pick = jnp.where(slot == local, jnp.ones((), BF16), jnp.zeros((), BF16))
         packed = jnp.dot(pick, wide_ref[...], preferred_element_type=F32)
-        at = pl.multiple_of(tile * step, step)
-        sendf_ref[pl.ds(at, step), :] = packed[:, :width].astype(BF16)
+        first = tile * peers
+        sendf_ref[pl.ds(first, peers)] = packed[:, :width].astype(BF16).reshape(peers, 32, width)
         meta = packed[:, width:].T
         code = (meta[0:1] * 128.0 + meta[1:2]).astype(I32) * 256 + meta[2:3].astype(I32)
-        sendm_ref[:, pl.ds(at, step)] = code
-
-
-def pack_call(dest, cell, sub, feat, owners):
+        lines = jnp.concatenate(
+            [jnp.broadcast_to(code[:, :128], (4, 128)), jnp.broadcast_to(code[:, 128:], (4, 128))], axis=0
+        )
+        placed = jnp.zeros((peers, 128), I32)
+        for k in range(4):
+            placed = jnp.where(near == k, pltpu.roll(lines, 32 * k, 1) if k else lines, placed)
+        placed = jnp.where(mine, placed, 0)
+        for j in range(peers):
+            sendm_ref[first + j] = placed[j : j + 1]
+        for j in range(peers):
+            peer = first + j
+
+            @pl.when(peer != me)
+            def _():
+                there = (peer // lon_count, lax.rem(peer, lon_count))
+                pltpu.make_async_remote_copy(
+                    src_ref=sendf_ref.at[peer],
+                    dst_ref=recvf_ref.at[me],
+                    send_sem=send_sem.at[0],
+                    recv_sem=recv_sem.at[0],
+                    device_id=there,
+                    device_id_type=MESH,
+                ).start()
+                pltpu.make_async_remote_copy(
+                    src_ref=sendm_ref.at[peer],
+                    dst_ref=recvm_ref.at[me],
+                    send_sem=send_sem.at[1],
+                    recv_sem=recv_sem.at[1],
+                    device_id=there,
+                    device_id_type=MESH,
+                ).start()
+
+    own = [
+        pltpu.make_async_copy(sendf_ref.at[me], recvf_ref.at[me], own_sem.at[0]),
+        pltpu.make_async_copy(sendm_ref.at[me], recvm_ref.at[me], own_sem.at[1]),
+    ]
+    for copy in own:
+        copy.start()
+    for copy in own:
+        copy.wait()
+    for sem in (send_sem, recv_sem):
+        for i, (src, dst) in enumerate(((sendf_ref, recvf_ref), (sendm_ref, recvm_ref))):
+            rest = pl.ds(0, owners - 1)
+            pltpu.make_async_copy(src.at[rest], dst.at[rest], sem.at[i]).wait()
+
+
+def route_call(dest, cell, sub, feat, owners):
     obs, width = feat.shape
     return pl.pallas_call(
-        pack_kernel,
-        name="pack",
+        route_kernel,
+        name="route",
         out_shape=(
-            jax.ShapeDtypeStruct((owners * 32, width), BF16),
-            jax.ShapeDtypeStruct((1, owners * 32), I32),
+            jax.ShapeDtypeStruct((owners, 32, width), BF16),
+            jax.ShapeDtypeStruct((owners, 1, 128), I32),
         ),
-        scratch_shapes=[pltpu.VMEM((1, obs), I32), pltpu.VMEM((obs, 2 * width), BF16)],
-        compiler_params=pltpu.CompilerParams(vmem_limit_bytes=48 << 20),
+        in_specs=[pl.BlockSpec(memory_space=pltpu.VMEM)] * 4,
+        out_specs=[pl.BlockSpec(memory_space=pltpu.VMEM)] * 2,
+        scratch_shapes=[
+            pltpu.VMEM((1, obs), I32),
+            pltpu.VMEM((obs, 2 * width), BF16),
+            pltpu.VMEM((owners, 32, width), BF16),
+            pltpu.VMEM((owners, 1, 128), I32),
+            pltpu.SemaphoreType.DMA((2,)),
+            pltpu.SemaphoreType.DMA((2,)),
+            pltpu.SemaphoreType.DMA((2,)),
+        ],
+        compiler_params=pltpu.CompilerParams(
+            collective_id=0, has_side_effects=True, vmem_limit_bytes=40 << 20
+        ),
     )(dest, cell, sub, feat)
 
 
 def grid_kernel(
-    feat_ref, code_ref, back_ref, win_ref, dens_ref, grid_ref, wide_ref, cell_ref, kern_ref
+    feat_ref, code_ref, back_ref, win_ref, dens_ref, grid_ref, wide_ref, cell_ref, kern_ref, codes_ref
 ):
     slots, width = feat_ref.shape
     cells = back_ref.shape[0]
     step = 256
-    code = code_ref[...]
+    for group in range(code_ref.shape[0] // 4):
+        code = code_ref[group * 4]
+        for other in range(1, 4):
+            code = code + code_ref[group * 4 + other]
+        codes_ref[:, group * 128 : group * 128 + 128] = code
+    code = codes_ref[...]
     sub = code & 255
     cell_ref[...] = (code >> 8) - 128
     row = ((sub >> 4).astype(F32) + 0.5) / 16.0 - 0.5
@@ -115,6 +199,7 @@
             pltpu.VMEM((slots, 2 * width), BF16),
             pltpu.VMEM((1, slots), I32),
             pltpu.VMEM((1, slots), F32),
+            pltpu.VMEM((1, slots), I32),
         ],
         compiler_params=pltpu.CompilerParams(vmem_limit_bytes=48 << 20),
     )(feat, code, back, w_in, dens_vec)
@@ -290,15 +375,12 @@
     owners = lax.axis_size("lat") * lax.axis_size("lon")
     rows, cols, channels = background.shape
     obs, width = obs_feat.shape
-    sendf, sendm = pack_call(
+    recvf, recvm = route_call(
         obs_dest.reshape(1, obs), obs_cell.reshape(1, obs), obs_sub.reshape(1, obs), obs_feat, owners
     )
-    both = ("lat", "lon")
-    recvf = lax.all_to_all(sendf.reshape(owners, 32, width), both, 0, 0, tiled=True)
-    recvm = lax.all_to_all(sendm.reshape(owners, 32), both, 0, 0, tiled=True)
     grid = grid_call(
         recvf.reshape(owners * 32, width),
-        recvm.reshape(1, owners * 32),
+        recvm,
         background.reshape(rows * cols, channels),
         w_in,
         dens_vec.reshape(1, channels),

time: 155 us -> 129 us (0.83)
  Pallas kernels: 54.7 us -> 73.9 us
  blocking collectives: 19.1 us -> 0 us
  waiting for transfers between devices: 41.4 us -> 22.9 us
  starting transfers between devices: 25.5 us -> 20.6 us
    pallas_call x1, Pallas kernels: 9.22 us -> 28.4 us  [route_call(): pl.pallas_call(route_kernel, name='route', out_shape=(jax.ShapeDtypeStruc...]
    all_to_all x1 -> x0, blocking collectives: 19.1 us -> none  [body(): recvm = lax.all_to_all(sendm.reshape(owners, 32), both, 0, 0, tiled=True)]
    all_to_all x1 -> x0, waiting for transfers between devices: 16.9 us -> none  [body(): lax.all_to_all(sendf.reshape(owners, 32, width), both, 0, 0, tiled=True)]
    all_to_all x1 -> x0, starting transfers between devices: 5.46 us -> none  [body(): lax.all_to_all(sendf.reshape(owners, 32, width), both, 0, 0, tiled=True)]
    ppermute x8, waiting for transfers between devices: 24.5 us -> 22.9 us  [moved(): return lax.ppermute(x, axis, pairs)]
  transfers between devices with their start and end apart: 9 -> 8, of which waited for: 9 -> 8; matrix products, arithmetic and copies ran while one was open for 1% -> 0% of each run, Pallas kernels for 0% -> 0%
where the time goes in v2:
time: 129 us; the launch traced here: 128 us
  Pallas kernels  73.9 us (57%)
  waiting for transfers between devices  22.9 us (18%)
  starting transfers between devices  20.6 us (16%)
  local copies, waits for them, and re-layouts  7.76 us (6%)
  other arithmetic  2.69 us (2%)
    pallas_call x1, Pallas kernels, route_call(): pl.pallas_call(route_kernel, name='route', out_shape=(jax.ShapeDtypeStruc...  28.4 us
    ppermute x8, waiting for transfers between devices, moved(): return lax.ppermute(x, axis, pairs)  22.9 us
    ppermute x8, starting transfers between devices, moved(): return lax.ppermute(x, axis, pairs)  20.6 us
    pallas_call x1, Pallas kernels, attend_call(): pl.pallas_call(attend_kernel, name='attend', out_shape=jax.ShapeDtypeStru...  15.6 us
    pallas_call x1, Pallas kernels, conv_call(): pl.pallas_call(conv_kernel, name='conv', out_shape=(out, out), scratch_sh...  15.1 us
    pallas_call x1, Pallas kernels, grid_call(): pl.pallas_call(grid_kernel, name='grid', out_shape=jax.ShapeDtypeStruct(b...  14.8 us
    unnamed x35, local copies, waits for them, and re-layouts  5.42 us
  transfers between devices with their start and end apart: 8, of which 8 were waited for; matrix products, arithmetic and copies ran while one was open for 0% of the time, Pallas kernels for 0%

profile of v2, /device:TPU:9, one launch (start us, length us, event | category | flops | bytes accessed | tf_op | source)
XLA Modules:
  0.0 128.0 jit_solution(4129532558232447713)
XLA Ops:
  0.0 0.0 copy-start.5
  0.0 1.0 copy-done.5
  1.0 0.0 copy-start.7
  1.0 0.7 copy-done.7
  1.7 0.0 copy-start.8
  1.7 0.7 copy-done.8
  2.4 0.0 copy-start.9
  2.4 0.7 copy-done.9
  3.1 28.4 %route.1 = (bf16[128,32,128]{2,1,0:T(8,128)(2,1)S(1)}, s32[128,1,128]{2,1,0:T(1,128)S(1)}) custom-call(s32[1,2048]{1,0:T(1,128)S(1)} %bitcast.25, s32[1,2048]{1,0:T(1,128)S(1)} %bitcast.26, s32[1,2048]{1,0:T(1,128)S(1)} %bitcast.27, bf16[2048,128]{1,0:T(8,128)(2,1)S(1)} %copy-done.5), custom_call_target="tpu_custom_call" | custom-call | tf_op jit(solution)/shard_map/route/pallas_call | solution.py:132
  31.5 0.0 copy-start.6
  31.6 0.9 copy-done.6
  32.5 0.0 copy-start.10
  32.5 0.7 copy-done.10
  33.1 14.8 %grid.1 = bf16[3072,512]{1,0:T(8,128)(2,1)S(1)} custom-call(bf16[4096,128]{1,0:T(8,128)(2,1)S(1)} %bitcast.23, s32[128,1,128]{2,1,0:T(1,128)S(1)} %get-tuple-element.10.code_ref, bf16[3072,512]{1,0:T(8,128)(2,1)} %bitcast.30, bf16[128,512]{1,0:T(8,128)(2,1)S(1)} %copy-done.6, f32[1,512]{1,0:T(1,128)S(1)} %bitcast.28), custom_call_target="tpu_custom_call" | custom-call | tf_op jit(solution)/shard_map/grid/pallas_call | solution.py:194
  48.0 0.0 copy-start
  48.0 0.1 fusion.1
  48.1 2.3 %collective-permute-start = (bf16[24,512]{1,0:T(8,128)(2,1)S(1)}, bf16[24,512]{1,0:T(8,128)(2,1)S(1)}, u32[]{:S(2)}, u32[]{:S(2)}) collective-permute-start(bf16[24,512]{1,0:T(8,128)(2,1)S(1)} %bitcast.31), channel_id=1, source_target_pairs={{0,1},{1,2},{2,3},{3,0},{4,5},{5,6},{6,7},{7,4},{8,9},{9,10},{10,1... | collective-permute-start | bytes 73736 | tf_op jit(solution)/shard_map/ppermute | solution.py:368
  50.4 0.0 collective-permute-start.1
  50.5 0.1 pad.20.clone
  50.5 0.8 collective-permute-done.left_ref
  51.4 0.0 copy-start.14
  51.4 3.8 %collective-permute-done.1.right_ref = bf16[24,512]{1,0:T(8,128)(2,1)S(1)} collective-permute-done((bf16[24,512]{1,0:T(8,128)(2,1)S(1)}, bf16[24,512]{1,0:T(8,128)(2,1)S(1)}, u32[]{:S(2)}, u32[]{:S(2)}) %collective-permute-start.1) | collective-permute-done | bytes 24608 | tf_op jit(solution)/shard_map/ppermute | solution.py:368
  55.2 0.0 copy-start.15
  55.2 0.1 maximum_maximum_fusion.1
  55.3 2.1 %collective-permute-start.2 = (bf16[144,512]{1,0:T(8,128)(2,1)S(1)}, bf16[144,512]{1,0:T(8,128)(2,1)S(1)}, u32[]{:S(2)}, u32[]{:S(2)}) collective-permute-start(bf16[144,512]{1,0:T(8,128)(2,1)S(1)} %get-tuple-element.26), channel_id=1, source_target_pairs={{0,4},{4,8},{8,12},{12,16},{16,20},{20,24},{24,28},{28,32},{32,36}... | collective-permute-start | bytes 442376 | tf_op jit(solution)/shard_map/ppermute | solution.py:368
  57.4 6.2 %collective-permute-start.3 = (bf16[144,512]{1,0:T(8,128)(2,1)S(1)}, bf16[144,512]{1,0:T(8,128)(2,1)S(1)}, u32[]{:S(2)}, u32[]{:S(2)}) collective-permute-start(bf16[144,512]{1,0:T(8,128)(2,1)S(1)} %get-tuple-element.25), channel_id=1, source_target_pairs={{4,0},{8,4},{12,8},{16,12},{20,16},{24,20},{28,24},{32,28},{36,32}... | collective-permute-start | bytes 442376 | tf_op jit(solution)/shard_map/ppermute | solution.py:368
  63.6 0.8 collective-permute-done.2.top_ref
  64.4 0.0 copy-start.11
  64.4 1.8 %collective-permute-done.3.bottom_ref = bf16[144,512]{1,0:T(8,128)(2,1)S(1)} collective-permute-done((bf16[144,512]{1,0:T(8,128)(2,1)S(1)}, bf16[144,512]{1,0:T(8,128)(2,1)S(1)}, u32[]{:S(2)}, u32[]{:S(2)}) %collective-permute-start.3) | collective-permute-done | bytes 147488 | tf_op jit(solution)/shard_map/ppermute | solution.py:368
  66.2 0.0 copy-start.12
  66.2 0.0 copy-done
  66.2 0.0 copy-done.14
  66.2 0.0 copy-done.15
  66.2 0.0 copy-done.11
  66.2 0.6 copy-done.12
  66.8 15.1 %conv.1 = (bf16[768,512]{1,0:T(8,128)(2,1)}, bf16[768,512]{1,0:T(8,128)(2,1)}) custom-call(bf16[24,128,512]{2,1,0:T(8,128)(2,1)} %bitcast.19, bf16[24,512]{1,0:T(8,128)(2,1)} %copy-done.14, bf16[24,512]{1,0:T(8,128)(2,1)} %copy-done.15, bf16[144,512]{1,0:T(8,128)(2,1)} %copy-done.11, bf16[144,512]{1,0:T(8,128)(2,1)} %copy-done.12, ...), custom_call_target="tpu_custom_call" | custom-call | tf_op jit(solution)/shard_map/conv/pallas_call | solution.py:261
  81.9 0.0 copy-start.13
  81.9 0.0 copy-start.1
  81.9 1.0 fusion.3
  82.9 1.4 %collective-permute-start.4 = (bf16[12,8,512]{2,1,0:T(8,128)(2,1)S(1)}, bf16[12,8,512]{2,1,0:T(8,128)(2,1)S(1)}, u32[]{:S(2)}, u32[]{:S(2)}) collective-permute-start(bf16[12,8,512]{2,1,0:T(8,128)(2,1)S(1)} %get-tuple-element.19), channel_id=1, source_target_pairs={{0,1},{1,2},{2,3},{3,0},{4,5},{5,6},{6,7},{7,4},{8,9},{9,10},{10,1... | collective-permute-start | bytes 294920 | tf_op jit(solution)/shard_map/ppermute | solution.py:368
  84.3 0.0 collective-permute-start.5
  84.3 1.6 %collective-permute-done.4 = bf16[12,8,512]{2,1,0:T(8,128)(2,1)S(1)} collective-permute-done((bf16[12,8,512]{2,1,0:T(8,128)(2,1)S(1)}, bf16[12,8,512]{2,1,0:T(8,128)(2,1)S(1)}, u32[]{:S(2)}, u32[]{:S(2)}) %collective-permute-start.4) | collective-permute-done | bytes 98336 | tf_op jit(solution)/shard_map/ppermute | solution.py:368
  86.0 3.9 %collective-permute-done.5 = bf16[12,8,512]{2,1,0:T(8,128)(2,1)S(1)} collective-permute-done((bf16[12,8,512]{2,1,0:T(8,128)(2,1)S(1)}, bf16[12,8,512]{2,1,0:T(8,128)(2,1)S(1)}, u32[]{:S(2)}, u32[]{:S(2)}) %collective-permute-start.5) | collective-permute-done | bytes 98336 | tf_op jit(solution)/shard_map/ppermute | solution.py:368
  89.9 1.2 pad_maximum_fusion.1
  91.1 0.0 copy-start.2
  91.1 0.0 copy-start.3
  91.1 1.0 fusion.2
  92.2 3.0 %collective-permute-start.6 = (bf16[6,80,512]{2,1,0:T(8,128)(2,1)}, bf16[6,80,512]{2,1,0:T(8,128)(2,1)}, u32[]{:S(2)}, u32[]{:S(2)}) collective-permute-start(bf16[6,80,512]{2,1,0:T(8,128)(2,1)} %get-tuple-element.17), channel_id=1, source_target_pairs={{0,4},{4,8},{8,12},{12,16},{16,20},{20,24},{24,28},{28,32},{32,36}... | collective-permute-start | bytes 1474568 | tf_op jit(solution)/shard_map/ppermute | solution.py:368
  95.2 5.5 %collective-permute-start.7 = (bf16[6,80,512]{2,1,0:T(8,128)(2,1)}, bf16[6,80,512]{2,1,0:T(8,128)(2,1)}, u32[]{:S(2)}, u32[]{:S(2)}) collective-permute-start(bf16[6,80,512]{2,1,0:T(8,128)(2,1)} %get-tuple-element.18), channel_id=1, source_target_pairs={{4,0},{8,4},{12,8},{16,12},{20,16},{24,20},{28,24},{32,28},{36,32}... | collective-permute-start | bytes 1474568 | tf_op jit(solution)/shard_map/ppermute | solution.py:368
  100.7 0.0 copy-done.13
  100.8 0.1 reshape.54.strip_ref
  100.9 0.0 copy-start.4
  100.9 8.4 %collective-permute-done.6 = bf16[6,80,512]{2,1,0:T(8,128)(2,1)} collective-permute-done((bf16[6,80,512]{2,1,0:T(8,128)(2,1)}, bf16[6,80,512]{2,1,0:T(8,128)(2,1)}, u32[]{:S(2)}, u32[]{:S(2)}) %collective-permute-start.6) | collective-permute-done | bytes 491552 | tf_op jit(solution)/shard_map/ppermute | solution.py:368
  109.3 1.8 %collective-permute-done.7 = bf16[6,80,512]{2,1,0:T(8,128)(2,1)} collective-permute-done((bf16[6,80,512]{2,1,0:T(8,128)(2,1)}, bf16[6,80,512]{2,1,0:T(8,128)(2,1)}, u32[]{:S(2)}, u32[]{:S(2)}) %collective-permute-start.7) | collective-permute-done | bytes 491552 | tf_op jit(solution)/shard_map/ppermute | solution.py:368
  111.0 0.0 copy-done.1
  111.0 1.3 %pad_maximum_fusion.ext_ref = bf16[24,80,512]{2,1,0:T(8,128)(2,1)S(1)} fusion(bf16[6,80,512]{2,1,0:T(8,128)(2,1)} %collective-permute-done.7, bf16[12,8,512]{2,1,0:T(8,128)(2,1)S(1)} %collective-permute-done.5, bf16[12,64,512]{2,1,0:T(8,128)(2,1)S(1)} %bitcast.22, bf16[12,8,512]{2,1,0:T(8,128)(2,1)S(1)} %collective-permute-done.4, ...), kind=kLoop, calls=%fused_computation | loop fusion | flops 9830400 | bytes 3932160 | tf_op jit(solution)/shard_map/concatenate | solution.py:405
  112.4 0.0 copy-done.2
  112.4 0.0 copy-done.3
  112.4 0.0 copy-done.4
  112.4 15.6 %attend.1 = bf16[12,64,512]{2,1,0:T(8,128)(2,1)} custom-call(bf16[768,512]{1,0:T(8,128)(2,1)S(1)} %copy-done.1, bf16[24,80,512]{2,1,0:T(8,128)(2,1)S(1)} %pad_maximum_fusion.ext_ref, bf16[512,1536]{1,0:T(8,128)(2,1)S(1)} %copy-done.2, f32[8,512]{1,0:T(8,128)S(1)} %reshape.54.strip_ref, bf16[512,512]{1,0:T(8,128)(2,1)S(1)} %copy-done.4, ...), custom_call_target="tpu_custom_call" | custom-call | tf_op jit(solution)/shard_map/attend/pallas_call | solution.py:349
  (8 shorter events, 0.1 us)
Async XLA Ops:
  0.0 1.0 copy-start.5
  1.0 0.7 copy-start.7
  1.7 0.7 copy-start.8
  2.4 0.7 copy-start.9
  31.5 0.9 copy-start.6
  32.5 0.7 copy-start.10
  48.0 18.2 %copy-start = (bf16[3072,512]{1,0:T(8,128)(2,1)}, bf16[3072,512]{1,0:T(8,128)(2,1)S(1)}, u32[]{:S(2)}) copy-start(bf16[3072,512]{1,0:T(8,128)(2,1)S(1)} %grid.1) | copy-start | bytes 9437188
  48.1 3.3 %collective-permute-start = (bf16[24,512]{1,0:T(8,128)(2,1)S(1)}, bf16[24,512]{1,0:T(8,128)(2,1)S(1)}, u32[]{:S(2)}, u32[]{:S(2)}) collective-permute-start(bf16[24,512]{1,0:T(8,128)(2,1)S(1)} %bitcast.31), channel_id=1, source_target_pairs={{0,1},{1,2},{2,3},{3,0},{4,5},{5,6},{6,7},{7,4},{8,9},{9,10},{10,1... | collective-permute-start | bytes 73736 | tf_op jit(solution)/shard_map/ppermute | solution.py:368
  50.4 4.8 %collective-permute-start.1 = (bf16[24,512]{1,0:T(8,128)(2,1)S(1)}, bf16[24,512]{1,0:T(8,128)(2,1)S(1)}, u32[]{:S(2)}, u32[]{:S(2)}) collective-permute-start(bf16[24,512]{1,0:T(8,128)(2,1)S(1)} %bitcast.32), channel_id=1, source_target_pairs={{0,3},{1,0},{2,1},{3,2},{4,7},{5,4},{6,5},{7,6},{8,11},{9,8},{10,9... | collective-permute-start | bytes 73736 | tf_op jit(solution)/shard_map/ppermute | solution.py:368
  51.4 14.8 %copy-start.14 = (bf16[24,512]{1,0:T(8,128)(2,1)}, bf16[24,512]{1,0:T(8,128)(2,1)S(1)}, u32[]{:S(2)}) copy-start(bf16[24,512]{1,0:T(8,128)(2,1)S(1)} %collective-permute-done.left_ref) | copy-start | bytes 73732
  55.2 11.0 %copy-start.15 = (bf16[24,512]{1,0:T(8,128)(2,1)}, bf16[24,512]{1,0:T(8,128)(2,1)S(1)}, u32[]{:S(2)}) copy-start(bf16[24,512]{1,0:T(8,128)(2,1)S(1)} %collective-permute-done.1.right_ref) | copy-start | bytes 73732
  55.3 9.1 %collective-permute-start.2 = (bf16[144,512]{1,0:T(8,128)(2,1)S(1)}, bf16[144,512]{1,0:T(8,128)(2,1)S(1)}, u32[]{:S(2)}, u32[]{:S(2)}) collective-permute-start(bf16[144,512]{1,0:T(8,128)(2,1)S(1)} %get-tuple-element.26), channel_id=1, source_target_pairs={{0,4},{4,8},{8,12},{12,16},{16,20},{20,24},{24,28},{28,32},{32,36}... | collective-permute-start | bytes 442376 | tf_op jit(solution)/shard_map/ppermute | solution.py:368
  57.4 8.7 %collective-permute-start.3 = (bf16[144,512]{1,0:T(8,128)(2,1)S(1)}, bf16[144,512]{1,0:T(8,128)(2,1)S(1)}, u32[]{:S(2)}, u32[]{:S(2)}) collective-permute-start(bf16[144,512]{1,0:T(8,128)(2,1)S(1)} %get-tuple-element.25), channel_id=1, source_target_pairs={{4,0},{8,4},{12,8},{16,12},{20,16},{24,20},{28,24},{32,28},{36,32}... | collective-permute-start | bytes 442376 | tf_op jit(solution)/shard_map/ppermute | solution.py:368
  64.4 1.8 %copy-start.11 = (bf16[144,512]{1,0:T(8,128)(2,1)}, bf16[144,512]{1,0:T(8,128)(2,1)S(1)}, u32[]{:S(2)}) copy-start(bf16[144,512]{1,0:T(8,128)(2,1)S(1)} %collective-permute-done.2.top_ref) | copy-start | bytes 442372
  66.2 0.7 copy-start.12
  81.9 18.8 %copy-start.13 = (f32[8,13,13]{2,0,1:T(8,128)S(1)}, f32[8,13,13]{2,0,1:T(8,128)}, u32[]{:S(2)}) copy-start(f32[8,13,13]{2,0,1:T(8,128)} %param.24) | copy-start | bytes 16228
  81.9 29.2 %copy-start.1 = (bf16[768,512]{1,0:T(8,128)(2,1)S(1)}, bf16[768,512]{1,0:T(8,128)(2,1)}, u32[]{:S(2)}) copy-start(bf16[768,512]{1,0:T(8,128)(2,1)} %get-tuple-element.11.normed_ref) | copy-start | bytes 2359300
  82.9 3.1 %collective-permute-start.4 = (bf16[12,8,512]{2,1,0:T(8,128)(2,1)S(1)}, bf16[12,8,512]{2,1,0:T(8,128)(2,1)S(1)}, u32[]{:S(2)}, u32[]{:S(2)}) collective-permute-start(bf16[12,8,512]{2,1,0:T(8,128)(2,1)S(1)} %get-tuple-element.19), channel_id=1, source_target_pairs={{0,1},{1,2},{2,3},{3,0},{4,5},{5,6},{6,7},{7,4},{8,9},{9,10},{10,1... | collective-permute-start | bytes 294920 | tf_op jit(solution)/shard_map/ppermute | solution.py:368
  84.3 5.5 %collective-permute-start.5 = (bf16[12,8,512]{2,1,0:T(8,128)(2,1)S(1)}, bf16[12,8,512]{2,1,0:T(8,128)(2,1)S(1)}, u32[]{:S(2)}, u32[]{:S(2)}) collective-permute-start(bf16[12,8,512]{2,1,0:T(8,128)(2,1)S(1)} %get-tuple-element.20), channel_id=1, source_target_pairs={{0,3},{1,0},{2,1},{3,2},{4,7},{5,4},{6,5},{7,6},{8,11},{9,8},{10,9... | collective-permute-start | bytes 294920 | tf_op jit(solution)/shard_map/ppermute | solution.py:368
  91.1 21.3 %copy-start.2 = (bf16[512,1536]{1,0:T(8,128)(2,1)S(1)}, bf16[512,1536]{1,0:T(8,128)(2,1)}, u32[]{:S(2)}) copy-start(bf16[512,1536]{1,0:T(8,128)(2,1)} %wqkv_ref.1) | copy-start | bytes 4718596
  91.1 21.3 %copy-start.3 = (bf16[768,512]{1,0:T(8,128)(2,1)S(1)}, bf16[768,512]{1,0:T(8,128)(2,1)}, u32[]{:S(2)}) copy-start(bf16[768,512]{1,0:T(8,128)(2,1)} %get-tuple-element.12) | copy-start | bytes 2359300
  92.2 17.1 %collective-permute-start.6 = (bf16[6,80,512]{2,1,0:T(8,128)(2,1)}, bf16[6,80,512]{2,1,0:T(8,128)(2,1)}, u32[]{:S(2)}, u32[]{:S(2)}) collective-permute-start(bf16[6,80,512]{2,1,0:T(8,128)(2,1)} %get-tuple-element.17), channel_id=1, source_target_pairs={{0,4},{4,8},{8,12},{12,16},{16,20},{20,24},{24,28},{28,32},{32,36}... | collective-permute-start | bytes 1474568 | tf_op jit(solution)/shard_map/ppermute | solution.py:368
  95.2 15.9 %collective-permute-start.7 = (bf16[6,80,512]{2,1,0:T(8,128)(2,1)}, bf16[6,80,512]{2,1,0:T(8,128)(2,1)}, u32[]{:S(2)}, u32[]{:S(2)}) collective-permute-start(bf16[6,80,512]{2,1,0:T(8,128)(2,1)} %get-tuple-element.18), channel_id=1, source_target_pairs={{4,0},{8,4},{12,8},{16,12},{20,16},{24,20},{28,24},{32,28},{36,32}... | collective-permute-start | bytes 1474568 | tf_op jit(solution)/shard_map/ppermute | solution.py:368
  100.9 11.6 %copy-start.4 = (bf16[512,512]{1,0:T(8,128)(2,1)S(1)}, bf16[512,512]{1,0:T(8,128)(2,1)}, u32[]{:S(2)}) copy-start(bf16[512,512]{1,0:T(8,128)(2,1)} %wout_ref.1) | copy-start | bytes 1572868

commit v3 on v1

v3 whole, which is shorter than its diff:
```python
import jax
import jax.numpy as jnp
from jax import lax
from jax.experimental import pallas as pl
from jax.experimental.pallas import tpu as pltpu
from jax.sharding import PartitionSpec as P

HEADS = 8
F32 = jnp.float32
BF16 = jnp.bfloat16
I32 = jnp.int32
NEG = -1e30
MESH = pl.DeviceIdType.MESH
WAYS = ((-1, 0), (1, 0), (0, -1), (0, 1), (-1, -1), (-1, 1), (1, -1), (1, 1))


def iota(shape, dim):
    return lax.broadcasted_iota(I32, shape, dim)


def narrow(x):
    return x.astype(F32).astype(BF16)


def dot(x, y):
    return jnp.dot(x, y, preferred_element_type=F32)


def dot_t(x, y):
    return lax.dot_general(x, y, (((1,), (1,)), ((), ())), preferred_element_type=F32)


def column(row):
    return jnp.broadcast_to(row.astype(F32), (128, 128)).T.astype(BF16)


def one_hot(place_ref, index, value):
    for part in range(place_ref.shape[0] // 256):
        local = index - part * 256
        local = narrow(jnp.where((local >= 0) & (local < 256), local, -1))
        line = narrow(iota((256, index.shape[1]), 0))
        place_ref[part * 256 : part * 256 + 256, :] = jnp.where(
            line == local, value, jnp.zeros((), BF16)
        )


def main_kernel(
    dest_ref, cell_ref, sub_ref, feat_ref, back_hbm, win_ref, dens_ref, conv_hbm, bias_in_ref,
    gain_ref, wqkv_hbm, strip_ref, wout_hbm,
    out_ref,
    back_ref, conv_ref, wqkv_ref, wout_ref,
    sendf_ref, sendm_ref, recvf_ref, recvm_ref, pick_ref, group_ref, local_ref,
    edge_ref, brow_ref, bside_ref, line_ref, taps_ref, acc_ref, comp_ref,
    codes_ref, spread_ref, sums_ref, oedge_ref, oline_ref, orow_ref, oside_ref, otaps_ref,
    own_ref, coarse_ref, vert_ref, side_ref, query_ref, key_ref, value_ref, bias_ref,
    load_sem, route_sem, own_sem, halo_send, halo_recv,
):
    obs, width = feat_ref.shape
    owners = sendf_ref.shape[0]
    slots = owners * 32
    rows, cols, channels = back_ref.shape
    half = cols // 2
    out_rows = rows // 2
    both = 2 * width
    lat_count, lon_count = lax.axis_size("lat"), lax.axis_size("lon")
    lat, lon = lax.axis_index("lat"), lax.axis_index("lon")
    me = lat * lon_count + lon

    loads = [
        pltpu.make_async_copy(src, dst, load_sem.at[i])
        for i, (src, dst) in enumerate(
            ((back_hbm, back_ref), (conv_hbm, conv_ref), (wqkv_hbm, wqkv_ref), (wout_hbm, wout_ref))
        )
    ]
    for load in loads:
        load.start()

    barrier = pltpu.get_barrier_semaphore()

    @pl.loop(1, owners)
    def _(k):
        peer = lax.rem(me + k, owners)
        pl.semaphore_signal(
            barrier, inc=1, device_id=(peer // lon_count, lax.rem(peer, lon_count)), device_id_type=MESH
        )

    def inside(da):
        return (lat + da >= 0) & (lat + da < lat_count)

    def halo(base, parts):
        copies = []
        for i, ((da, db), (src, dst)) in enumerate(zip(WAYS, parts)):
            copies.append(
                (
                    da,
                    pltpu.make_async_remote_copy(
                        src_ref=src,
                        dst_ref=dst,
                        send_sem=halo_send.at[base + i],
                        recv_sem=halo_recv.at[base + i],
                        device_id=(lat + da, lax.rem(lon + db + lon_count, lon_count)),
                        device_id_type=MESH,
                    ),
                )
            )
        return copies

    def halo_start(copies):
        for da, copy in copies:
            pl.when(inside(da))(copy.start)

    def halo_arrive(copies):
        for da, copy in copies:
            pl.when(inside(-da))(copy.wait_recv)

    def halo_sent(copies):
        for da, copy in copies:
            pl.when(inside(da))(copy.wait_send)

    step = 256
    upper = (iota((step, step), 0) < iota((step, step), 1)).astype(F32).astype(BF16)
    running = jnp.zeros((owners, 1), F32)
    for at in range(0, obs, step):
        dest = dest_ref[:, at : at + step]
        member = (iota((owners, step), 0) == dest).astype(F32)
        earlier = dot(member.astype(BF16), upper) + running
        rank = jnp.sum(member * earlier, axis=0, keepdims=True)
        running = running + jnp.sum(member, axis=1, keepdims=True)
        local_ref[:, at : at + step] = (dest & 15) * 32 + rank.astype(I32)
        for more in range(0, step, 128):
            group_ref[at + more : at + more + 128, :] = column(dest[:, more : more + 128] >> 4)
    one_hot(pick_ref, local_ref[...], jnp.ones((), BF16))

    dest, cell, sub = dest_ref[...], cell_ref[...], sub_ref[...]
    same = iota((8, obs), 0) == (dest >> 4)
    meta = jnp.concatenate(
        [jnp.where(same, value, 0) for value in ((cell >> 7) + 1, cell & 127, sub, dest * 0)], axis=0
    )
    meta = dot_t(narrow(meta), pick_ref[...])
    code = (meta[0:8] * 128.0 + meta[8:16]).astype(I32) * 256 + meta[16:24].astype(I32)
    mine = iota((8, 128), 1) // 32 == lon
    for c in range(4):
        chunk = code[:, c * 128 : c * 128 + 128]
        turned = [chunk] + [pltpu.roll(chunk, 32 * k, 1) for k in range(1, 4)]
        for j in range(4):
            near = (lon - j) & 3
            placed = jnp.where(
                near < 2,
                jnp.where(near == 0, turned[0], turned[1]),
                jnp.where(near == 2, turned[2], turned[3]),
            )
            placed = jnp.where(mine, placed, 0)
            for g in range(8):
                sendm_ref[g * 16 + c * 4 + j] = placed[g : g + 1]

    loads[0].wait()
    for row in range(rows):
        tile = back_ref[row, 0:16, :].astype(F32)
        edge_ref[0, row : row + 1, :] = tile[0:1]
        tile = back_ref[row, cols - 16 : cols, :].astype(F32)
        edge_ref[1, row : row + 1, :] = tile[15:16]

    pl.semaphore_wait(barrier, owners - 1)

    def fine_parts(first, last, edge, row, side):
        top, bottom = pl.ds(0, 8), pl.ds(rows - 8, 8)
        return (
            (first, row.at[1]),
            (last, row.at[0]),
            (edge.at[0], side.at[1, pl.ds(8, rows)]),
            (edge.at[1], side.at[0, pl.ds(8, rows)]),
            (edge.at[0, top], side.at[1, pl.ds(8 + rows, 8)]),
            (edge.at[1, top], side.at[0, pl.ds(8 + rows, 8)]),
            (edge.at[0, bottom], side.at[1, pl.ds(0, 8)]),
            (edge.at[1, bottom], side.at[0, pl.ds(0, 8)]),
        )

    halo_back = halo(0, fine_parts(back_ref.at[0], back_ref.at[rows - 1], edge_ref, brow_ref, bside_ref))
    halo_start(halo_back)

    @pl.loop(0, owners // 32)
    def _(turn):
        part = lax.rem(turn + me // 32, owners // 32)
        group = group_ref[...]
        feat = feat_ref[...]
        wide = jnp.concatenate(
            [
                jnp.where(
                    group == jnp.full((1, 1), 2 * part + i, I32).astype(F32).astype(BF16),
                    feat,
                    jnp.zeros((), BF16),
                )
                for i in range(2)
            ],
            axis=1,
        )
        packed = dot(pick_ref[...], wide).astype(BF16)
        for i in range(2):
            sendf_ref[pl.ds(part * 32 + i * 16, 16)] = packed[:, i * width : (i + 1) * width].reshape(
                16, 32, width
            )

        @pl.loop(0, 32)
        def _(k):
            peer = part * 32 + k

            @pl.when(peer != me)
            def _():
                there = (peer // lon_count, lax.rem(peer, lon_count))
                for i, (src, dst) in enumerate(((sendf_ref, recvf_ref), (sendm_ref, recvm_ref))):
                    pltpu.make_async_remote_copy(
                        src_ref=src.at[peer],
                        dst_ref=dst.at[me],
                        send_sem=route_sem.at[i],
                        recv_sem=route_sem.at[2 + i],
                        device_id=there,
                        device_id_type=MESH,
                    ).start()

    own_copies = [
        pltpu.make_async_copy(src.at[me], dst.at[me], own_sem.at[i])
        for i, (src, dst) in enumerate(((sendf_ref, recvf_ref), (sendm_ref, recvm_ref)))
    ]
    for copy in own_copies:
        copy.start()

    @pl.when(lat == 0)
    def _():
        brow_ref[0] = jnp.zeros((cols, channels), BF16)
        bside_ref[:, 0:8, :] = jnp.zeros((2, 8, channels), F32)
        orow_ref[0] = jnp.zeros((cols, both), BF16)
        oside_ref[:, 0:8, :] = jnp.zeros((2, 8, both), F32)
        vert_ref[0] = jnp.zeros((6, half, channels), BF16)
        side_ref[:, 0:6] = jnp.zeros((2, 6, 16, channels), BF16)

    @pl.when(lat == lat_count - 1)
    def _():
        brow_ref[1] = jnp.zeros((cols, channels), BF16)
        bside_ref[:, 8 + rows :, :] = jnp.zeros((2, 8, channels), F32)
        orow_ref[1] = jnp.zeros((cols, both), BF16)
        oside_ref[:, 8 + rows :, :] = jnp.zeros((2, 8, both), F32)
        vert_ref[1] = jnp.zeros((6, half, channels), BF16)
        side_ref[:, 18:24] = jnp.zeros((2, 6, 16, channels), BF16)

    halo_arrive(halo_back)

    def lay(taps, buffer, slot, at, line, left, right):
        size = line.shape[1]
        for c in range(size // 128):
            lanes = slice(c * 128, (c + 1) * 128)
            spot = slot * (size // 128) + c
            buffer[spot, 8 : 8 + cols, :] = line[:, lanes].astype(F32)
            if left is not None:
                buffer[spot, 7:8, :] = left[:, lanes]
                buffer[spot, 8 + cols : 9 + cols, :] = right[:, lanes]
            for tap in range(4):
                part = buffer[spot, pl.ds(7 + tap, half, stride=2), :]
                base = tap * size + c * 128
                taps[at, :, base : base + 128] = part.astype(BF16)

    for i, at in ((0, 0), (1, rows + 1)):
        lay(
            taps_ref, line_ref, i, at, brow_ref[i],
            bside_ref[0, at + 7 : at + 8, :], bside_ref[1, at + 7 : at + 8, :],
        )

    @pl.loop(0, rows // 2)
    def _(pair):
        for i in range(2):
            row = pair * 2 + i
            lay(
                taps_ref, line_ref, i, row + 1, back_ref[row],
                bside_ref[0, pl.ds(row + 8, 1), :], bside_ref[1, pl.ds(row + 8, 1), :],
            )

    loads[1].wait()
    block = 4 * half

    def window(taps, part, tap):
        return taps[pl.ds(part * 4 + tap // 2, 4), tap % 2].reshape(block, taps.shape[3])

    taps4 = taps_ref.reshape(rows // 2 + 1, 2, half, 4 * channels)
    otaps4 = otaps_ref.reshape(rows // 2 + 1, 2, half, 4 * both)

    @pl.loop(0, out_rows // 4)
    def _(part):
        total = jnp.broadcast_to(bias_in_ref[...], (block, channels))
        for tap in range(4):
            total = total + dot(window(taps4, part, tap), conv_ref[tap])
        acc_ref[pl.ds(pl.multiple_of(part * block, block), block), :] = total

    dens = jnp.broadcast_to(dens_ref[...], (16, channels))
    dens_hi = dens.astype(BF16)
    dens_lo = (dens - dens_hi.astype(F32)).astype(BF16)
    line16 = iota((16, channels), 0)
    tail = jnp.where(
        line16 == 0, dens_hi.astype(F32), jnp.where(line16 == 1, dens_lo.astype(F32), 0.0)
    ).astype(BF16)
    lift = jnp.concatenate([win_ref[...], tail], axis=0)

    @pl.loop(0, 4)
    def _(tap):
        for s in range(4):
            made = dot(lift, conv_ref[tap, s * channels : (s + 1) * channels, :])
            base = s * both
            comp_ref[tap, base : base + width, :] = made[:width].astype(BF16)
            whole = made[width : width + 1] + made[width + 1 : width + 2]
            upper_part = whole.astype(BF16).astype(F32)
            rest = jnp.where(
                line16 < 2, upper_part, jnp.where(line16 == 2, whole - upper_part, 0.0)
            ).astype(BF16)
            comp_ref[tap, base + width : base + width + 16, :] = rest
            comp_ref[tap, base + width + 16 : base + both, :] = jnp.zeros(
                (width - 16, channels), BF16
            )

    for h in range(HEADS):
        strip = jnp.broadcast_to(strip_ref[h : h + 1, :], (16, 512))
        for r in range(4):
            at = h * 64 + r * 16
            bias_ref[at : at + 16, :] = pltpu.roll(strip, 2 + 32 * r, 1, stride=1, stride_axis=0)

    for copy in own_copies:
        copy.wait()
    rest = pl.ds(0, owners - 1)
    for i, (src, dst) in enumerate(((sendf_ref, recvf_ref), (sendm_ref, recvm_ref))):
        pltpu.make_async_copy(src.at[rest], dst.at[rest], route_sem.at[i]).wait()
        pltpu.make_async_copy(src.at[rest], dst.at[rest], route_sem.at[2 + i]).wait()
    for group in range(owners // 4):
        code = recvm_ref[group * 4]
        for other in range(1, 4):
            code = code + recvm_ref[group * 4 + other]
        codes_ref[:, group * 128 : group * 128 + 128] = code

    chunk = spread_ref.shape[0]
    lane = narrow(iota((128, 128), 1))
    for c in range(slots // chunk):
        code = codes_ref[:, c * chunk : (c + 1) * chunk]
        sub = code & 255
        cell = (code >> 8) - 128
        row_off = ((sub >> 4).astype(F32) + 0.5) / 16.0 - 0.5
        col_off = ((sub & 15).astype(F32) + 0.5) / 16.0 - 0.5
        kern = jnp.exp(-(row_off * row_off + col_off * col_off) / (2.0 * 0.35 * 0.35))
        one_hot(pick_ref, cell & 511, kern.astype(BF16))
        band = cell >> 9
        for b in range(chunk // 128):
            spot = column(band[:, b * 128 : b * 128 + 128])
            first = (c * chunk + b * 128) // 32
            feat = recvf_ref[first : first + 4].reshape(128, width)
            lines = slice(b * 128, b * 128 + 128)
            for g in range(rows // 4):
                here = jnp.full((1, 1), g, F32).astype(BF16)
                spread_ref[lines, g * width : (g + 1) * width] = jnp.where(
                    spot == here, feat, jnp.zeros((), BF16)
                )
            spread_ref[lines, rows // 4 * width :] = jnp.where(
                spot == lane, jnp.ones((), BF16), jnp.zeros((), BF16)
            )
        part = dot(pick_ref[...], spread_ref[...])
        sums_ref[...] = part if c == 0 else sums_ref[...] + part

    lane_f = iota((cols, width), 1)
    for g in range(rows // 4):
        for r in range(4):
            row = g * 4 + r
            lines = slice(r * cols, (r + 1) * cols)
            density = sums_ref[lines, rows // 4 * width + g : rows // 4 * width + g + 1]
            normed = sums_ref[lines, g * width : (g + 1) * width] / (density + 1.0)
            high = density.astype(BF16).astype(F32)
            marks = jnp.where(
                (lane_f == 0) | (lane_f == 2), high, jnp.where(lane_f == 1, density - high, 0.0)
            )
            line = jnp.concatenate([normed, marks], axis=1)
            oedge_ref[0, row : row + 1, :] = line[0:1]
            oedge_ref[1, row : row + 1, :] = line[cols - 1 : cols]
            if row == 0:
                orow_ref[2] = line.astype(BF16)
            if row == rows - 1:
                orow_ref[3] = line.astype(BF16)
            lay(otaps_ref, oline_ref, row % 2, row + 1, line, None, None)

    halo_obs = halo(8, fine_parts(orow_ref.at[2], orow_ref.at[3], oedge_ref, orow_ref, oside_ref))
    halo_start(halo_obs)
    halo_arrive(halo_obs)
    for i, at in ((0, 0), (1, rows + 1)):
        lay(otaps_ref, oline_ref, i, at, orow_ref[i], None, None)
    first_line = iota((16, both), 0) == 0
    last_line = iota((16, both), 0) == 15
    for at in range(rows + 2):
        old = otaps_ref[at, 0:16, 0:both].astype(F32)
        otaps_ref[at, 0:16, 0:both] = jnp.where(
            first_line, oside_ref[0, at + 7 : at + 8, :], old
        ).astype(BF16)
        old = otaps_ref[at, half - 16 : half, 3 * both :].astype(F32)
        otaps_ref[at, half - 16 : half, 3 * both :] = jnp.where(
            last_line, oside_ref[1, at + 7 : at + 8, :], old
        ).astype(BF16)

    loads[2].wait()
    loads[3].wait()

    @pl.loop(0, out_rows // 4)
    def _(part):
        at = pl.multiple_of(part * block, block)
        total = acc_ref[pl.ds(at, block), :]
        for tap in range(4):
            total = total + dot(window(otaps4, part, tap), comp_ref[tap])
        inner = 0.7978845608028654 * (total + 0.044715 * total * total * total)
        coarse = (0.5 * total * (1.0 + jnp.tanh(inner))).astype(BF16)
        coarse_ref[pl.ds(part * 4, 4)] = coarse.reshape(4, half, channels)
        value = coarse.astype(F32)
        scale = lax.rsqrt(jnp.mean(value * value, axis=1, keepdims=True) + 1e-05)
        normed = (value * scale * gain_ref[...]).astype(BF16)
        own_ref[pl.ds(part * 4, 4)] = normed.reshape(4, half, channels)

    upside, downside = pl.ds(0, 6), pl.ds(out_rows - 6, 6)
    lower, higher = pl.ds(0, 16), pl.ds(half - 16, 16)
    middle, before, after = pl.ds(6, out_rows), pl.ds(0, 6), pl.ds(6 + out_rows, 6)
    halo_norm = halo(
        16,
        (
            (own_ref.at[upside], vert_ref.at[1]),
            (own_ref.at[downside], vert_ref.at[0]),
            (own_ref.at[:, lower], side_ref.at[1, middle]),
            (own_ref.at[:, higher], side_ref.at[0, middle]),
            (own_ref.at[upside, lower], side_ref.at[1, after]),
            (own_ref.at[upside, higher], side_ref.at[0, after]),
            (own_ref.at[downside, lower], side_ref.at[1, before]),
            (own_ref.at[downside, higher], side_ref.at[0, before]),
        ),
    )
    halo_start(halo_norm)

    def keys_values(x, lead):
        made = dot(x.reshape(lead * x.shape[1], channels), wqkv_ref[:, channels:])
        made = made.reshape(lead, x.shape[1], 2 * channels)
        return made[:, :, :channels], made[:, :, channels:]

    @pl.loop(0, out_rows // 4)
    def _(part):
        own = own_ref[pl.ds(part * 4, 4)]
        query = dot(own.reshape(block, channels), wqkv_ref[:, :channels]).astype(BF16) * 0.125
        query_ref[pl.ds(part * 4, 4)] = query.astype(BF16).reshape(4, half, channels)
        key, value = keys_values(own, 4)
        key_ref[pl.ds(part * 4 + 6, 4), 8 : 8 + half, :] = key.astype(BF16)
        value_ref[pl.ds(part * 4 + 6, 4), 8 : 8 + half, :] = value.astype(BF16)

    halo_arrive(halo_norm)
    for i, at in ((0, 0), (1, 6 + out_rows)):
        key, value = keys_values(vert_ref[i], 6)
        key_ref[at : at + 6, 8 : 8 + half, :] = key.astype(BF16)
        value_ref[at : at + 6, 8 : 8 + half, :] = value.astype(BF16)
    for i, at, cut in ((0, 0, slice(8, 16)), (1, 8 + half, slice(0, 8))):
        key, value = keys_values(side_ref[i], out_rows + 12)
        key_ref[:, at : at + 8, :] = key[:, cut].astype(BF16)
        value_ref[:, at : at + 8, :] = value[:, cut].astype(BF16)

    half_ch = channels // 2
    lane_head = iota((64, half_ch), 1) // (channels // HEADS)

    @pl.loop(0, out_rows // 4)
    def _(down):
        first = lat * out_rows - 6 + down * 4
        key_row = first + iota((1, 512), 1) // 32
        beyond = jnp.where((key_row >= 0) & (key_row < lat_count * out_rows), 0.0, NEG)

        @pl.loop(0, half // 16)
        def _(across):
            c0 = pl.multiple_of(across * 16, 16)
            query = query_ref[pl.ds(down * 4, 4), pl.ds(c0, 16), :].reshape(64, channels)
            parts = []
            for g in range(2):
                lanes = slice(g * half_ch, (g + 1) * half_ch)
                keys = key_ref[pl.ds(down * 4, 16), pl.ds(c0, 32), lanes].reshape(512, half_ch)
                values = value_ref[pl.ds(down * 4, 16), pl.ds(c0, 32), lanes].reshape(512, half_ch)
                wide = query[:, lanes]
                masked = jnp.concatenate(
                    [jnp.where(lane_head == h, wide, jnp.zeros((), BF16)) for h in range(4)], axis=0
                )
                scores = dot_t(masked, keys)
                scores = scores + bias_ref[g * 256 : (g + 1) * 256, :] + beyond
                peak = jnp.max(scores, axis=1, keepdims=True)
                weight = jnp.exp(scores - peak)
                norm = jnp.sum(weight, axis=1, keepdims=True)
                mixed = dot(weight.astype(BF16), values) / norm
                total = jnp.zeros((64, half_ch), F32)
                for h in range(4):
                    total = jnp.where(lane_head == h, mixed[h * 64 : (h + 1) * 64], total)
                parts.append(total.astype(BF16))
            attended = jnp.concatenate(parts, axis=1)
            lifted = dot(attended, wout_ref[...])
            base = coarse_ref[pl.ds(down * 4, 4), pl.ds(c0, 16), :].astype(F32)
            result = base + lifted.reshape(4, 16, channels)
            out_ref[pl.ds(down * 4, 4), pl.ds(c0, 16), :] = result.astype(BF16)

    for copies in (halo_back, halo_obs, halo_norm):
        halo_sent(copies)


def body(
    obs_feat, obs_dest, obs_cell, obs_sub, background, w_in, dens_vec,
    conv_w, conv_b, norm_gain, w_qkv, rel_bias, w_out,
):
    owners = lax.axis_size("lat") * lax.axis_size("lon")
    rows, cols, channels = background.shape
    obs, width = obs_feat.shape
    half, out_rows, both = cols // 2, rows // 2, 2 * width
    strip = jnp.pad(rel_bias, ((0, 0), (0, 3), (0, 19)), constant_values=NEG).reshape(HEADS, 512)
    vmem = pl.BlockSpec(memory_space=pltpu.VMEM)
    hbm = pl.BlockSpec(memory_space=pl.ANY)
    scratch = [
        ((rows, cols, channels), BF16),
        ((4, 4 * channels, channels), BF16),
        ((channels, 3 * channels), BF16),
        ((channels, channels), BF16),
        ((owners, 32, width), BF16),
        ((owners, 1, 128), I32),
        ((owners, 32, width), BF16),
        ((owners, 1, 128), I32),
        ((512, obs), BF16),
        ((obs, width), BF16),
        ((1, obs), I32),
        ((2, rows, channels), F32),
        ((2, cols, channels), BF16),
        ((2, rows + 16, channels), F32),
        ((2 * channels // 128, cols + 16, 128), F32),
        ((rows + 2, half, 4 * channels), BF16),
        ((half * out_rows, channels), F32),
        ((4, 4 * both, channels), BF16),
        ((1, owners * 32), I32),
        ((obs, rows // 4 * width + 128), BF16),
        ((512, rows // 4 * width + 128), F32),
        ((2, rows, both), F32),
        ((2 * both // 128, cols + 16, 128), F32),
        ((4, cols, both), BF16),
        ((2, rows + 16, both), F32),
        ((rows + 2, half, 4 * both), BF16),
        ((out_rows, half, channels), BF16),
        ((out_rows, half, channels), BF16),
        ((2, 6, half, channels), BF16),
        ((2, out_rows + 12, 16, channels), BF16),
        ((out_rows, half, channels), BF16),
        ((out_rows + 12, half + 16, channels), BF16),
        ((out_rows + 12, half + 16, channels), BF16),
        ((HEADS * 64, 512), F32),
    ]
    sems = [pltpu.SemaphoreType.DMA((n,)) for n in (4, 4, 2, 24, 24)]
    return pl.pallas_call(
        main_kernel,
        name="main",
        out_shape=jax.ShapeDtypeStruct((out_rows, half, channels), BF16),
        in_specs=[vmem, vmem, vmem, vmem, hbm, vmem, vmem, hbm, vmem, vmem, hbm, vmem, hbm],
        out_specs=vmem,
        scratch_shapes=[pltpu.VMEM(shape, dtype) for shape, dtype in scratch] + sems,
        compiler_params=pltpu.CompilerParams(
            collective_id=0, has_side_effects=True, vmem_limit_bytes=62 << 20
        ),
    )(
        obs_dest.reshape(1, obs),
        obs_cell.reshape(1, obs),
        obs_sub.reshape(1, obs),
        obs_feat,
        background,
        w_in,
        dens_vec.reshape(1, channels),
        conv_w.reshape(4, 4 * channels, channels),
        conv_b.reshape(1, channels),
        norm_gain.reshape(1, channels),
        w_qkv,
        strip,
        w_out,
    )


def solution(mesh):
    split = P(("lat", "lon"))
    wide = P(("lat", "lon"), None)
    tile = P("lat", "lon", None)
    in_specs = (wide, wide, split, split, tile) + (P(),) * 8
    return jax.shard_map(body, mesh=mesh, in_specs=in_specs, out_specs=tile, check_vma=False)
```

time: 155 us -> 91.9 us (0.59)
  waiting for transfers between devices: 41.4 us -> 0 us
  Pallas kernels: 54.7 us -> 87.4 us
  starting transfers between devices: 25.5 us -> 0 us
  blocking collectives: 19.1 us -> 0 us
  other arithmetic: 4.18 us -> 0 us
  local copies, waits for them, and re-layouts: 7.56 us -> 3.59 us
    pallas_call x4 -> x1, Pallas kernels: 54.7 us -> 87.4 us  [body(): pl.pallas_call(main_kernel, name='main', out_shape=jax.ShapeDtypeStruct((...]
    ppermute x8 -> x0, waiting for transfers between devices: 24.5 us -> none  [moved(): return lax.ppermute(x, axis, pairs)]
    ppermute x8 -> x0, starting transfers between devices: 20 us -> none  [moved(): return lax.ppermute(x, axis, pairs)]
    all_to_all x1 -> x0, blocking collectives: 19.1 us -> none  [body(): recvm = lax.all_to_all(sendm.reshape(owners, 32), both, 0, 0, tiled=True)]
    all_to_all x1 -> x0, waiting for transfers between devices: 16.9 us -> none  [body(): lax.all_to_all(sendf.reshape(owners, 32, width), both, 0, 0, tiled=True)]
    all_to_all x1 -> x0, starting transfers between devices: 5.46 us -> none  [body(): lax.all_to_all(sendf.reshape(owners, 32, width), both, 0, 0, tiled=True)]
    concatenate x3 -> x0, other arithmetic: 2.69 us -> none  [the longest x1 1.34 us: body(): ext = jnp.concatenate([over, ext, under], axis=0)]
    slice x6 -> x0, local copies, waits for them, and re-layouts: 2.17 us -> none  [the longest x1 1.03 us: body(): over = moved(ext[-6:], 'lat', 1, False)]
  transfers between devices with their start and end apart: 9 -> 0, of which waited for: 9 -> 0; matrix products, arithmetic and copies ran while one was open for 1% -> 0% of each run, Pallas kernels for 0% -> 0%
where the time goes in v3:
time: 91.9 us; the launch traced here: 91 us
  Pallas kernels  87.4 us (95%)
  local copies, waits for them, and re-layouts  3.59 us (4%)
    pallas_call x1, Pallas kernels, body(): pl.pallas_call(main_kernel, name='main', out_shape=jax.ShapeDtypeStruct((...  87.4 us
    unnamed x2, local copies, waits for them, and re-layouts  2.89 us

profile of v3, /device:TPU:9, one launch (start us, length us, event | category | flops | bytes accessed | tf_op | source)
XLA Modules:
  0.0 91.0 jit_solution(9485432833331306775)
XLA Ops:
  0.0 0.8 copy.15
  0.8 0.7 reshape.31.strip_ref
  1.5 87.4 %main.1 = bf16[12,64,512]{2,1,0:T(8,128)(2,1)} custom-call(s32[1,2048]{1,0:T(1,128)} %bitcast.8, s32[1,2048]{1,0:T(1,128)} %bitcast.9, s32[1,2048]{1,0:T(1,128)} %bitcast.10, bf16[2048,128]{1,0:T(8,128)(2,1)} %feat_ref.1, bf16[24,128,512]{2,1,0:T(8,128)(2,1)} %back_hbm.1, bf16[128,512]{1,0:T(8,128)(2,1)} %win_ref.1, f32[1,512]{1,0:T(1,128)} %bitcast.11, ...), custom_call_target="tpu_custom_call" | custom-call | tf_op jit(solution)/shard_map/main/pallas_call | solution.py:548
  88.9 2.1 %copy.17 = bf16[12,64,512]{2,1,0:T(8,128)(2,1)} copy(bf16[12,64,512]{2,1,0:T(8,128)(2,1)} %main.1) | data formatting | bytes 1572864
  (1 shorter events, 0.0 us)

commit v4 on v3

--- a/solution.py
+++ b/solution.py
@@ -52,8 +52,8 @@
     sendf_ref, sendm_ref, recvf_ref, recvm_ref, pick_ref, group_ref, local_ref,
     edge_ref, brow_ref, bside_ref, line_ref, taps_ref, acc_ref, comp_ref,
     codes_ref, spread_ref, sums_ref, oedge_ref, oline_ref, orow_ref, oside_ref, otaps_ref,
-    own_ref, coarse_ref, vert_ref, side_ref, query_ref, key_ref, value_ref, bias_ref,
-    load_sem, route_sem, own_sem, halo_send, halo_recv,
+    own_ref, coarse_ref, vert_ref, side_ref, sside_ref, query_ref, key_ref, value_ref, bias_ref,
+    load_sem, route_sem, own_sem, halo_send, halo_recv, meet_sem,
 ):
     obs, width = feat_ref.shape
     owners = sendf_ref.shape[0]
@@ -75,21 +75,34 @@
     for load in loads:
         load.start()
 
-    barrier = pltpu.get_barrier_semaphore()
-
-    @pl.loop(1, owners)
-    def _(k):
-        peer = lax.rem(me + k, owners)
-        pl.semaphore_signal(
-            barrier, inc=1, device_id=(peer // lon_count, lax.rem(peer, lon_count)), device_id_type=MESH
-        )
-
     def inside(da):
         return (lat + da >= 0) & (lat + da < lat_count)
 
+    def place(device):
+        return device // lon_count, lax.rem(device, lon_count)
+
+    barrier = pltpu.get_barrier_semaphore()
+    rounds = owners.bit_length() - 1
+
+    def greet(where):
+        pl.semaphore_signal(barrier, inc=1, device_id=where, device_id_type=MESH)
+
+    for da, db in WAYS:
+        there = (lat + da, lax.rem(lon + db + lon_count, lon_count))
+        if da == 0:
+            greet(there)
+        else:
+            pl.when(inside(da))(lambda: greet(there))
+    for k in range(rounds):
+        greet(place(me ^ (1 << k)))
+
+    def meet(k):
+        pl.semaphore_signal(meet_sem.at[k], inc=1, device_id=place(me ^ (1 << k)), device_id_type=MESH)
+        pl.semaphore_wait(meet_sem.at[k], 1)
+
     def halo(base, parts):
         copies = []
-        for i, ((da, db), (src, dst)) in enumerate(zip(WAYS, parts)):
+        for i, ((da, db), src, dst) in enumerate(parts):
             copies.append(
                 (
                     da,
@@ -117,6 +130,32 @@
         for da, copy in copies:
             pl.when(inside(da))(copy.wait_send)
 
+    loads[0].wait()
+    for row in range(rows):
+        tile = back_ref[row, 0:16, :].astype(F32)
+        edge_ref[0, row : row + 1, :] = tile[0:1]
+        tile = back_ref[row, cols - 16 : cols, :].astype(F32)
+        edge_ref[1, row : row + 1, :] = tile[15:16]
+
+    neighbours = 2 + 3 * (inside(-1).astype(I32) + inside(1).astype(I32))
+    pl.semaphore_wait(barrier, rounds + neighbours)
+
+    def fine_parts(first, last, edge, row, side):
+        top, bottom = pl.ds(0, 8), pl.ds(rows - 8, 8)
+        return (
+            ((-1, 0), first, row.at[1]),
+            ((1, 0), last, row.at[0]),
+            ((0, -1), edge.at[0], side.at[1, pl.ds(8, rows)]),
+            ((0, 1), edge.at[1], side.at[0, pl.ds(8, rows)]),
+            ((-1, -1), edge.at[0, top], side.at[1, pl.ds(8 + rows, 8)]),
+            ((-1, 1), edge.at[1, top], side.at[0, pl.ds(8 + rows, 8)]),
+            ((1, -1), edge.at[0, bottom], side.at[1, pl.ds(0, 8)]),
+            ((1, 1), edge.at[1, bottom], side.at[0, pl.ds(0, 8)]),
+        )
+
+    halo_back = halo(0, fine_parts(back_ref.at[0], back_ref.at[rows - 1], edge_ref, brow_ref, bside_ref))
+    halo_start(halo_back)
+
     step = 256
     upper = (iota((step, step), 0) < iota((step, step), 1)).astype(F32).astype(BF16)
     running = jnp.zeros((owners, 1), F32)
@@ -129,6 +168,8 @@
         local_ref[:, at : at + step] = (dest & 15) * 32 + rank.astype(I32)
         for more in range(0, step, 128):
             group_ref[at + more : at + more + 128, :] = column(dest[:, more : more + 128] >> 4)
+        if at // step < rounds:
+            meet(at // step)
     one_hot(pick_ref, local_ref[...], jnp.ones((), BF16))
 
     dest, cell, sub = dest_ref[...], cell_ref[...], sub_ref[...]
@@ -153,30 +194,8 @@
             for g in range(8):
                 sendm_ref[g * 16 + c * 4 + j] = placed[g : g + 1]
 
-    loads[0].wait()
-    for row in range(rows):
-        tile = back_ref[row, 0:16, :].astype(F32)
-        edge_ref[0, row : row + 1, :] = tile[0:1]
-        tile = back_ref[row, cols - 16 : cols, :].astype(F32)
-        edge_ref[1, row : row + 1, :] = tile[15:16]
-
-    pl.semaphore_wait(barrier, owners - 1)
-
-    def fine_parts(first, last, edge, row, side):
-        top, bottom = pl.ds(0, 8), pl.ds(rows - 8, 8)
-        return (
-            (first, row.at[1]),
-            (last, row.at[0]),
-            (edge.at[0], side.at[1, pl.ds(8, rows)]),
-            (edge.at[1], side.at[0, pl.ds(8, rows)]),
-            (edge.at[0, top], side.at[1, pl.ds(8 + rows, 8)]),
-            (edge.at[1, top], side.at[0, pl.ds(8 + rows, 8)]),
-            (edge.at[0, bottom], side.at[1, pl.ds(0, 8)]),
-            (edge.at[1, bottom], side.at[0, pl.ds(0, 8)]),
-        )
-
-    halo_back = halo(0, fine_parts(back_ref.at[0], back_ref.at[rows - 1], edge_ref, brow_ref, bside_ref))
-    halo_start(halo_back)
+    for k in range(obs // step, rounds):
+        meet(k)
 
     @pl.loop(0, owners // 32)
     def _(turn):
@@ -231,7 +250,7 @@
         orow_ref[0] = jnp.zeros((cols, both), BF16)
         oside_ref[:, 0:8, :] = jnp.zeros((2, 8, both), F32)
         vert_ref[0] = jnp.zeros((6, half, channels), BF16)
-        side_ref[:, 0:6] = jnp.zeros((2, 6, 16, channels), BF16)
+        side_ref[:, 0:3] = jnp.zeros((2, 3, 16, channels), BF16)
 
     @pl.when(lat == lat_count - 1)
     def _():
@@ -240,7 +259,7 @@
         orow_ref[1] = jnp.zeros((cols, both), BF16)
         oside_ref[:, 8 + rows :, :] = jnp.zeros((2, 8, both), F32)
         vert_ref[1] = jnp.zeros((6, half, channels), BF16)
-        side_ref[:, 18:24] = jnp.zeros((2, 6, 16, channels), BF16)
+        side_ref[:, 9:12] = jnp.zeros((2, 3, 16, channels), BF16)
 
     halo_arrive(halo_back)
 
@@ -313,12 +332,6 @@
             comp_ref[tap, base + width + 16 : base + both, :] = jnp.zeros(
                 (width - 16, channels), BF16
             )
-
-    for h in range(HEADS):
-        strip = jnp.broadcast_to(strip_ref[h : h + 1, :], (16, 512))
-        for r in range(4):
-            at = h * 64 + r * 16
-            bias_ref[at : at + 16, :] = pltpu.roll(strip, 2 + 32 * r, 1, stride=1, stride_axis=0)
 
     for copy in own_copies:
         copy.wait()
@@ -381,6 +394,27 @@
 
     halo_obs = halo(8, fine_parts(orow_ref.at[2], orow_ref.at[3], oedge_ref, orow_ref, oside_ref))
     halo_start(halo_obs)
+
+    middle = slice(both, 3 * both)
+    for part in (1, 0, 2):
+        lines = slice(part * block, (part + 1) * block)
+        total = acc_ref[lines, :]
+        for tap in range(4):
+            if (part, tap) not in ((0, 0), (out_rows // 4 - 1, 3)):
+                total = total + dot(window(otaps4, part, tap)[:, middle], comp_ref[tap, middle, :])
+        acc_ref[lines, :] = total
+
+    for down in range(out_rows // 4):
+        key_row = lat * out_rows - 6 + down * 4 + iota((1, 512), 1) // 32
+        beyond = jnp.where((key_row >= 0) & (key_row < lat_count * out_rows), 0.0, NEG)
+        for h in range(HEADS):
+            strip = jnp.broadcast_to(strip_ref[h : h + 1, :], (16, 512))
+            for r in range(4):
+                at = h * 64 + r * 16
+                bias_ref[down, at : at + 16, :] = (
+                    pltpu.roll(strip, 2 + 32 * r, 1, stride=1, stride_axis=0) + beyond
+                )
+
     halo_arrive(halo_obs)
     for i, at in ((0, 0), (1, rows + 1)):
         lay(otaps_ref, oline_ref, i, at, orow_ref[i], None, None)
@@ -399,37 +433,79 @@
     loads[2].wait()
     loads[3].wait()
 
-    @pl.loop(0, out_rows // 4)
-    def _(part):
-        at = pl.multiple_of(part * block, block)
-        total = acc_ref[pl.ds(at, block), :]
+    outer = (slice(0, both), slice(3 * both, 4 * both))
+
+    def finish(part):
+        lines = slice(part * block, (part + 1) * block)
+        total = acc_ref[lines, :]
         for tap in range(4):
-            total = total + dot(window(otaps4, part, tap), comp_ref[tap])
+            view = window(otaps4, part, tap)
+            if (part, tap) in ((0, 0), (out_rows // 4 - 1, 3)):
+                total = total + dot(view, comp_ref[tap])
+            else:
+                for lanes in outer:
+                    total = total + dot(view[:, lanes], comp_ref[tap, lanes, :])
         inner = 0.7978845608028654 * (total + 0.044715 * total * total * total)
         coarse = (0.5 * total * (1.0 + jnp.tanh(inner))).astype(BF16)
-        coarse_ref[pl.ds(part * 4, 4)] = coarse.reshape(4, half, channels)
+        coarse_ref[part * 4 : part * 4 + 4] = coarse.reshape(4, half, channels)
         value = coarse.astype(F32)
         scale = lax.rsqrt(jnp.mean(value * value, axis=1, keepdims=True) + 1e-05)
-        normed = (value * scale * gain_ref[...]).astype(BF16)
-        own_ref[pl.ds(part * 4, 4)] = normed.reshape(4, half, channels)
-
-    upside, downside = pl.ds(0, 6), pl.ds(out_rows - 6, 6)
-    lower, higher = pl.ds(0, 16), pl.ds(half - 16, 16)
-    middle, before, after = pl.ds(6, out_rows), pl.ds(0, 6), pl.ds(6 + out_rows, 6)
-    halo_norm = halo(
+        normed = value * scale * gain_ref[...]
+        own_ref[part * 4 : part * 4 + 4] = normed.astype(BF16).reshape(4, half, channels)
+        for side, at in ((0, 0), (1, half - 8)):
+            for pair in range(2):
+                first = pair * 2 * half + at
+                both_rows = jnp.concatenate(
+                    [normed[first : first + 8], normed[first + half : first + half + 8]], axis=0
+                )
+                sside_ref[side, part * 2 + pair] = both_rows.astype(BF16)
+
+    def rim(first, count, side):
+        return sside_ref.at[side, pl.ds(first, count)]
+
+    def gap(first, count, side):
+        return side_ref.at[side, pl.ds(first, count)]
+
+    finish(0)
+    halo_first = halo(
         16,
         (
-            (own_ref.at[upside], vert_ref.at[1]),
-            (own_ref.at[downside], vert_ref.at[0]),
-            (own_ref.at[:, lower], side_ref.at[1, middle]),
-            (own_ref.at[:, higher], side_ref.at[0, middle]),
-            (own_ref.at[upside, lower], side_ref.at[1, after]),
-            (own_ref.at[upside, higher], side_ref.at[0, after]),
-            (own_ref.at[downside, lower], side_ref.at[1, before]),
-            (own_ref.at[downside, higher], side_ref.at[0, before]),
+            ((-1, 0), own_ref.at[pl.ds(0, 4)], vert_ref.at[1, pl.ds(0, 4)]),
+            ((0, -1), rim(0, 2, 0), gap(3, 2, 1)),
+            ((0, 1), rim(0, 2, 1), gap(3, 2, 0)),
+            ((-1, -1), rim(0, 2, 0), gap(9, 2, 1)),
+            ((-1, 1), rim(0, 2, 1), gap(9, 2, 0)),
         ),
     )
-    halo_start(halo_norm)
+    halo_start(halo_first)
+    finish(2)
+    halo_second = halo(
+        21,
+        (
+            ((1, 0), own_ref.at[pl.ds(8, 4)], vert_ref.at[0, pl.ds(2, 4)]),
+            ((0, -1), rim(4, 2, 0), gap(7, 2, 1)),
+            ((0, 1), rim(4, 2, 1), gap(7, 2, 0)),
+            ((1, -1), rim(4, 2, 0), gap(1, 2, 1)),
+            ((1, 1), rim(4, 2, 1), gap(1, 2, 0)),
+        ),
+    )
+    halo_start(halo_second)
+    finish(1)
+    halo_third = halo(
+        26,
+        (
+            ((-1, 0), own_ref.at[pl.ds(4, 2)], vert_ref.at[1, pl.ds(4, 2)]),
+            ((1, 0), own_ref.at[pl.ds(6, 2)], vert_ref.at[0, pl.ds(0, 2)]),
+            ((0, -1), rim(2, 2, 0), gap(5, 2, 1)),
+            ((0, 1), rim(2, 2, 1), gap(5, 2, 0)),
+            ((-1, -1), rim(2, 1, 0), gap(11, 1, 1)),
+            ((-1, 1), rim(2, 1, 1), gap(11, 1, 0)),
+            ((1, -1), rim(3, 1, 0), gap(0, 1, 1)),
+            ((1, 1), rim(3, 1, 1), gap(0, 1, 0)),
+        ),
+    )
+    halo_start(halo_third)
+    halo_norm = halo_first + halo_second + halo_third
 
     def keys_values(x, lead):
         made = dot(x.reshape(lead * x.shape[1], channels), wqkv_ref[:, channels:])
@@ -450,20 +526,17 @@
         key, value = keys_values(vert_ref[i], 6)
         key_ref[at : at + 6, 8 : 8 + half, :] = key.astype(BF16)
         value_ref[at : at + 6, 8 : 8 + half, :] = value.astype(BF16)
-    for i, at, cut in ((0, 0, slice(8, 16)), (1, 8 + half, slice(0, 8))):
-        key, value = keys_values(side_ref[i], out_rows + 12)
-        key_ref[:, at : at + 8, :] = key[:, cut].astype(BF16)
-        value_ref[:, at : at + 8, :] = value[:, cut].astype(BF16)
+    for i, at in ((0, 0), (1, 8 + half)):
+        key, value = keys_values(side_ref[i], out_rows // 2 + 6)
+        shape = (out_rows + 12, 8, channels)
+        key_ref[:, at : at + 8, :] = key.reshape(shape).astype(BF16)
+        value_ref[:, at : at + 8, :] = value.reshape(shape).astype(BF16)
 
     half_ch = channels // 2
     lane_head = iota((64, half_ch), 1) // (channels // HEADS)
 
     @pl.loop(0, out_rows // 4)
     def _(down):
-        first = lat * out_rows - 6 + down * 4
-        key_row = first + iota((1, 512), 1) // 32
-        beyond = jnp.where((key_row >= 0) & (key_row < lat_count * out_rows), 0.0, NEG)
-
         @pl.loop(0, half // 16)
         def _(across):
             c0 = pl.multiple_of(across * 16, 16)
@@ -478,11 +551,11 @@
                     [jnp.where(lane_head == h, wide, jnp.zeros((), BF16)) for h in range(4)], axis=0
                 )
                 scores = dot_t(masked, keys)
-                scores = scores + bias_ref[g * 256 : (g + 1) * 256, :] + beyond
+                scores = scores + bias_ref[down, g * 256 : (g + 1) * 256, :]
                 peak = jnp.max(scores, axis=1, keepdims=True)
                 weight = jnp.exp(scores - peak)
                 norm = jnp.sum(weight, axis=1, keepdims=True)
-                mixed = dot(weight.astype(BF16), values) / norm
+                mixed = dot(weight.astype(BF16), values) * (1.0 / norm)
                 total = jnp.zeros((64, half_ch), F32)
                 for h in range(4):
                     total = jnp.where(lane_head == h, mixed[h * 64 : (h + 1) * 64], total)
@@ -538,13 +611,15 @@
         ((out_rows, half, channels), BF16),
         ((out_rows, half, channels), BF16),
         ((2, 6, half, channels), BF16),
-        ((2, out_rows + 12, 16, channels), BF16),
+        ((2, out_rows // 2 + 6, 16, channels), BF16),
+        ((2, out_rows // 2, 16, channels), BF16),
         ((out_rows, half, channels), BF16),
         ((out_rows + 12, half + 16, channels), BF16),
         ((out_rows + 12, half + 16, channels), BF16),
-        ((HEADS * 64, 512), F32),
+        ((out_rows // 4, HEADS * 64, 512), F32),
     ]
-    sems = [pltpu.SemaphoreType.DMA((n,)) for n in (4, 4, 2, 24, 24)]
+    sems = [pltpu.SemaphoreType.DMA((n,)) for n in (4, 4, 2, 34, 34)]
+    sems.append(pltpu.SemaphoreType.REGULAR((owners.bit_length() - 1,)))
     return pl.pallas_call(
         main_kernel,
         name="main",

time: 91.9 us -> 84.3 us (0.917)
  Pallas kernels: 87.4 us -> 80.4 us
    pallas_call x1, Pallas kernels: 87.4 us -> 80.4 us  [body(): pl.pallas_call(main_kernel, name='main', out_shape=jax.ShapeDtypeStruct((...]
where the time goes in v4:
time: 84.3 us; the launch traced here: 84 us
  Pallas kernels  80.4 us (95%)
  local copies, waits for them, and re-layouts  3.59 us (4%)
    pallas_call x1, Pallas kernels, body(): pl.pallas_call(main_kernel, name='main', out_shape=jax.ShapeDtypeStruct((...  80.4 us
    unnamed x2, local copies, waits for them, and re-layouts  2.89 us

profile of v4, /device:TPU:9, one launch (start us, length us, event | category | flops | bytes accessed | tf_op | source)
XLA Modules:
  0.0 84.0 jit_solution(16480363527021546234)
XLA Ops:
  0.0 0.8 copy.15
  0.8 0.7 reshape.31.strip_ref
  1.5 80.4 %main.1 = bf16[12,64,512]{2,1,0:T(8,128)(2,1)} custom-call(s32[1,2048]{1,0:T(1,128)} %bitcast.8, s32[1,2048]{1,0:T(1,128)} %bitcast.9, s32[1,2048]{1,0:T(1,128)} %bitcast.10, bf16[2048,128]{1,0:T(8,128)(2,1)} %feat_ref.1, bf16[24,128,512]{2,1,0:T(8,128)(2,1)} %back_hbm.1, bf16[128,512]{1,0:T(8,128)(2,1)} %win_ref.1, f32[1,512]{1,0:T(1,128)} %bitcast.11, ...), custom_call_target="tpu_custom_call" | custom-call | tf_op jit(solution)/shard_map/main/pallas_call | solution.py:623
  82.0 2.1 %copy.17 = bf16[12,64,512]{2,1,0:T(8,128)(2,1)} copy(bf16[12,64,512]{2,1,0:T(8,128)(2,1)} %main.1) | data formatting | bytes 1572864
  (1 shorter events, 0.0 us)

commit v5 on v4

--- a/solution.py
+++ b/solution.py
@@ -52,7 +52,8 @@
     sendf_ref, sendm_ref, recvf_ref, recvm_ref, pick_ref, group_ref, local_ref,
     edge_ref, brow_ref, bside_ref, line_ref, taps_ref, acc_ref, comp_ref,
     codes_ref, spread_ref, sums_ref, oedge_ref, oline_ref, orow_ref, oside_ref, otaps_ref,
-    own_ref, coarse_ref, vert_ref, side_ref, sside_ref, query_ref, key_ref, value_ref, bias_ref,
+    own_ref, coarse_ref, vert_ref, side_ref, sside_ref, query_ref, ext_ref, bias_ref, rim_ref,
+    far_ref, turned_ref, held_ref, stat_ref,
     load_sem, route_sem, own_sem, halo_send, halo_recv, meet_sem,
 ):
     obs, width = feat_ref.shape
@@ -82,7 +83,8 @@
         return device // lon_count, lax.rem(device, lon_count)
 
     barrier = pltpu.get_barrier_semaphore()
-    rounds = owners.bit_length() - 1
+    near = [me ^ j for j in range(1, 16)]
+    far = [me ^ (16 * j) for j in range(1, owners // 16)]
 
     def greet(where):
         pl.semaphore_signal(barrier, inc=1, device_id=where, device_id_type=MESH)
@@ -93,12 +95,8 @@
             greet(there)
         else:
             pl.when(inside(da))(lambda: greet(there))
-    for k in range(rounds):
-        greet(place(me ^ (1 << k)))
-
-    def meet(k):
-        pl.semaphore_signal(meet_sem.at[k], inc=1, device_id=place(me ^ (1 << k)), device_id_type=MESH)
-        pl.semaphore_wait(meet_sem.at[k], 1)
+    for device in near + far:
+        greet(place(device))
 
     def halo(base, parts):
         copies = []
@@ -138,7 +136,9 @@
         edge_ref[1, row : row + 1, :] = tile[15:16]
 
     neighbours = 2 + 3 * (inside(-1).astype(I32) + inside(1).astype(I32))
-    pl.semaphore_wait(barrier, rounds + neighbours)
+    pl.semaphore_wait(barrier, len(near) + len(far) + neighbours)
+    for device in far:
+        pl.semaphore_signal(meet_sem, inc=1, device_id=place(device), device_id_type=MESH)
 
     def fine_parts(first, last, edge, row, side):
         top, bottom = pl.ds(0, 8), pl.ds(rows - 8, 8)
@@ -165,15 +165,13 @@
         earlier = dot(member.astype(BF16), upper) + running
         rank = jnp.sum(member * earlier, axis=0, keepdims=True)
         running = running + jnp.sum(member, axis=1, keepdims=True)
-        local_ref[:, at : at + step] = (dest & 15) * 32 + rank.astype(I32)
+        local_ref[:, at : at + step] = (dest >> 3) * 32 + rank.astype(I32)
         for more in range(0, step, 128):
-            group_ref[at + more : at + more + 128, :] = column(dest[:, more : more + 128] >> 4)
-        if at // step < rounds:
-            meet(at // step)
+            group_ref[at + more : at + more + 128, :] = column(dest[:, more : more + 128] & 7)
     one_hot(pick_ref, local_ref[...], jnp.ones((), BF16))
 
     dest, cell, sub = dest_ref[...], cell_ref[...], sub_ref[...]
-    same = iota((8, obs), 0) == (dest >> 4)
+    same = iota((8, obs), 0) == (dest & 7)
     meta = jnp.concatenate(
         [jnp.where(same, value, 0) for value in ((cell >> 7) + 1, cell & 127, sub, dest * 0)], axis=0
     )
@@ -194,12 +192,11 @@
             for g in range(8):
                 sendm_ref[g * 16 + c * 4 + j] = placed[g : g + 1]
 
-    for k in range(obs // step, rounds):
-        meet(k)
+    pl.semaphore_wait(meet_sem, len(far))
 
     @pl.loop(0, owners // 32)
     def _(turn):
-        part = lax.rem(turn + me // 32, owners // 32)
+        part = lax.rem(turn + me + me // 4, owners // 32)
         group = group_ref[...]
         feat = feat_ref[...]
         wide = jnp.concatenate(
@@ -215,20 +212,23 @@
         )
         packed = dot(pick_ref[...], wide).astype(BF16)
         for i in range(2):
-            sendf_ref[pl.ds(part * 32 + i * 16, 16)] = packed[:, i * width : (i + 1) * width].reshape(
+            sendf_ref[pl.ds((part * 2 + i) * 16, 16)] = packed[:, i * width : (i + 1) * width].reshape(
                 16, 32, width
             )
 
         @pl.loop(0, 32)
         def _(k):
-            peer = part * 32 + k
+            turned = lax.rem(k * 5 + me, 32)
+            group = part * 2 + lax.rem(turned, 2)
+            peer = (turned // 2) * 8 + group
 
             @pl.when(peer != me)
             def _():
-                there = (peer // lon_count, lax.rem(peer, lon_count))
+                there = place(peer)
+                slot = group * 16 + turned // 2
                 for i, (src, dst) in enumerate(((sendf_ref, recvf_ref), (sendm_ref, recvm_ref))):
                     pltpu.make_async_remote_copy(
-                        src_ref=src.at[peer],
+                        src_ref=src.at[slot],
                         dst_ref=dst.at[me],
                         send_sem=route_sem.at[i],
                         recv_sem=route_sem.at[2 + i],
@@ -237,7 +237,7 @@
                     ).start()
 
     own_copies = [
-        pltpu.make_async_copy(src.at[me], dst.at[me], own_sem.at[i])
+        pltpu.make_async_copy(src.at[lax.rem(me, 8) * 16 + me // 8], dst.at[me], own_sem.at[i])
         for i, (src, dst) in enumerate(((sendf_ref, recvf_ref), (sendm_ref, recvm_ref)))
     ]
     for copy in own_copies:
@@ -332,6 +332,39 @@
             comp_ref[tap, base + width + 16 : base + both, :] = jnp.zeros(
                 (width - 16, channels), BF16
             )
+
+    loads[2].wait()
+    loads[3].wait()
+    turned_ref[...] = wqkv_ref[:, 2 * channels :].astype(F32).T.astype(BF16)
+
+    no_up = jnp.where(lat == 0, NEG, 0.0)
+    no_down = jnp.where(lat == lat_count - 1, NEG, 0.0)
+    lane256 = iota((16, 256), 1)
+    for pair in range(HEADS // 2):
+        places = slice(pair * 128, pair * 128 + 128)
+        for down in range(out_rows // 4):
+            inner_part, outer_part = [], []
+            for h in (2 * pair, 2 * pair + 1):
+                strip = jnp.broadcast_to(strip_ref[h : h + 1, :], (16, 640))
+                for r in range(4):
+
+                    def shifted(first_row, lead, size):
+                        amount = (2 + 32 * (r + 4 * down - first_row) + lead) % 640
+                        return pltpu.roll(strip, amount, 1, stride=1, stride_axis=0)[:, :size]
+
+                    inner_part.append(shifted(6, 0, 384))
+                    if down == 0:
+                        outer_part.append(shifted(0, 0, 256) + no_up)
+                    elif down == 1:
+                        outer_part.append(
+                            jnp.where(
+                                lane256 < 64, shifted(4, 0, 256) + no_up, shifted(18, 64, 256) + no_down
+                            )
+                        )
+                    else:
+                        outer_part.append(jnp.where(lane256 < 64, NEG, shifted(18, 64, 256) + no_down))
+            bias_ref[down, :, places] = jnp.concatenate(inner_part, axis=0).T
+            rim_ref[down, :, places] = jnp.concatenate(outer_part, axis=0).T
 
     for copy in own_copies:
         copy.wait()
@@ -404,17 +437,6 @@
                 total = total + dot(window(otaps4, part, tap)[:, middle], comp_ref[tap, middle, :])
         acc_ref[lines, :] = total
 
-    for down in range(out_rows // 4):
-        key_row = lat * out_rows - 6 + down * 4 + iota((1, 512), 1) // 32
-        beyond = jnp.where((key_row >= 0) & (key_row < lat_count * out_rows), 0.0, NEG)
-        for h in range(HEADS):
-            strip = jnp.broadcast_to(strip_ref[h : h + 1, :], (16, 512))
-            for r in range(4):
-                at = h * 64 + r * 16
-                bias_ref[down, at : at + 16, :] = (
-                    pltpu.roll(strip, 2 + 32 * r, 1, stride=1, stride_axis=0) + beyond
-                )
-
     halo_arrive(halo_obs)
     for i, at in ((0, 0), (1, rows + 1)):
         lay(otaps_ref, oline_ref, i, at, orow_ref[i], None, None)
@@ -430,8 +452,6 @@
             last_line, oside_ref[1, at + 7 : at + 8, :], old
         ).astype(BF16)
 
-    loads[2].wait()
-    loads[3].wait()
 
     outer = (slice(0, both), slice(3 * both, 4 * both))
 
@@ -452,6 +472,7 @@
         scale = lax.rsqrt(jnp.mean(value * value, axis=1, keepdims=True) + 1e-05)
         normed = value * scale * gain_ref[...]
         own_ref[part * 4 : part * 4 + 4] = normed.astype(BF16).reshape(4, half, channels)
+        ext_ref[part * 4 : part * 4 + 4, 8 : 8 + half, :] = normed.reshape(4, half, channels).astype(BF16)
         for side, at in ((0, 0), (1, half - 8)):
             for pair in range(2):
                 first = pair * 2 * half + at
@@ -470,11 +491,11 @@
     halo_first = halo(
         16,
         (
-            ((-1, 0), own_ref.at[pl.ds(0, 4)], vert_ref.at[1, pl.ds(0, 4)]),
             ((0, -1), rim(0, 2, 0), gap(3, 2, 1)),
             ((0, 1), rim(0, 2, 1), gap(3, 2, 0)),
             ((-1, -1), rim(0, 2, 0), gap(9, 2, 1)),
             ((-1, 1), rim(0, 2, 1), gap(9, 2, 0)),
+            ((-1, 0), own_ref.at[pl.ds(0, 4)], vert_ref.at[1, pl.ds(0, 4)]),
         ),
     )
     halo_start(halo_first)
@@ -482,11 +503,11 @@
     halo_second = halo(
         21,
         (
-            ((1, 0), own_ref.at[pl.ds(8, 4)], vert_ref.at[0, pl.ds(2, 4)]),
             ((0, -1), rim(4, 2, 0), gap(7, 2, 1)),
             ((0, 1), rim(4, 2, 1), gap(7, 2, 0)),
             ((1, -1), rim(4, 2, 0), gap(1, 2, 1)),
             ((1, 1), rim(4, 2, 1), gap(1, 2, 0)),
+            ((1, 0), own_ref.at[pl.ds(8, 4)], vert_ref.at[0, pl.ds(2, 4)]),
         ),
     )
     halo_start(halo_second)
@@ -494,77 +515,108 @@
     halo_third = halo(
         26,
         (
-            ((-1, 0), own_ref.at[pl.ds(4, 2)], vert_ref.at[1, pl.ds(4, 2)]),
-            ((1, 0), own_ref.at[pl.ds(6, 2)], vert_ref.at[0, pl.ds(0, 2)]),
             ((0, -1), rim(2, 2, 0), gap(5, 2, 1)),
             ((0, 1), rim(2, 2, 1), gap(5, 2, 0)),
             ((-1, -1), rim(2, 1, 0), gap(11, 1, 1)),
             ((-1, 1), rim(2, 1, 1), gap(11, 1, 0)),
             ((1, -1), rim(3, 1, 0), gap(0, 1, 1)),
             ((1, 1), rim(3, 1, 1), gap(0, 1, 0)),
+            ((-1, 0), own_ref.at[pl.ds(4, 2)], vert_ref.at[1, pl.ds(4, 2)]),
+            ((1, 0), own_ref.at[pl.ds(6, 2)], vert_ref.at[0, pl.ds(0, 2)]),
         ),
     )
     halo_start(halo_third)
     halo_norm = halo_first + halo_second + halo_third
-
-    def keys_values(x, lead):
-        made = dot(x.reshape(lead * x.shape[1], channels), wqkv_ref[:, channels:])
-        made = made.reshape(lead, x.shape[1], 2 * channels)
-        return made[:, :, :channels], made[:, :, channels:]
+    halo_side = halo_first[:2] + halo_second[:2] + halo_third[:2]
+    halo_far = halo_first[2:] + halo_second[2:] + halo_third[2:]
 
     @pl.loop(0, out_rows // 4)
     def _(part):
-        own = own_ref[pl.ds(part * 4, 4)]
-        query = dot(own.reshape(block, channels), wqkv_ref[:, :channels]).astype(BF16) * 0.125
+        own = own_ref[pl.ds(part * 4, 4)].reshape(block, channels)
+        query = dot(own, wqkv_ref[:, :channels]).astype(BF16) * 0.125
         query_ref[pl.ds(part * 4, 4)] = query.astype(BF16).reshape(4, half, channels)
-        key, value = keys_values(own, 4)
-        key_ref[pl.ds(part * 4 + 6, 4), 8 : 8 + half, :] = key.astype(BF16)
-        value_ref[pl.ds(part * 4 + 6, 4), 8 : 8 + half, :] = value.astype(BF16)
-
-    halo_arrive(halo_norm)
-    for i, at in ((0, 0), (1, 6 + out_rows)):
-        key, value = keys_values(vert_ref[i], 6)
-        key_ref[at : at + 6, 8 : 8 + half, :] = key.astype(BF16)
-        value_ref[at : at + 6, 8 : 8 + half, :] = value.astype(BF16)
-    for i, at in ((0, 0), (1, 8 + half)):
-        key, value = keys_values(side_ref[i], out_rows // 2 + 6)
-        shape = (out_rows + 12, 8, channels)
-        key_ref[:, at : at + 8, :] = key.reshape(shape).astype(BF16)
-        value_ref[:, at : at + 8, :] = value.reshape(shape).astype(BF16)
 
     half_ch = channels // 2
     lane_head = iota((64, half_ch), 1) // (channels // HEADS)
-
-    @pl.loop(0, out_rows // 4)
-    def _(down):
-        @pl.loop(0, half // 16)
-        def _(across):
-            c0 = pl.multiple_of(across * 16, 16)
-            query = query_ref[pl.ds(down * 4, 4), pl.ds(c0, 16), :].reshape(64, channels)
+    same_half = iota((128, 128), 0) // 64 == iota((128, 128), 1) // 64
+
+    def keys_values(x):
+        keys = dot(x, wqkv_ref[:, channels : 2 * channels]).astype(BF16)
+        return keys, dot_t(turned_ref[...], x).astype(BF16)
+
+    def queries(down, c0, lanes):
+        wide = query_ref[down * 4 : down * 4 + 4, pl.ds(c0, 16), lanes].reshape(64, half_ch)
+        return jnp.concatenate(
+            [jnp.where(lane_head == h, wide, jnp.zeros((), BF16)) for h in range(4)], axis=0
+        )
+
+    def attend_near(across):
+        c0 = pl.multiple_of(across * 16, 16)
+        keys, values = keys_values(ext_ref[:, pl.ds(c0, 32), :].reshape(32 * out_rows, channels))
+        for down in range(out_rows // 4):
+            spot = down * (half // 16) + across
+            for g in range(2):
+                lanes = slice(g * half_ch, (g + 1) * half_ch)
+                scores = dot_t(keys[:, lanes], queries(down, c0, lanes)) + bias_ref[down, :, lanes]
+                peak = jnp.max(scores, axis=0, keepdims=True)
+                weight = jnp.exp(scores - peak)
+                stat_ref[spot, 0:1, lanes] = peak
+                stat_ref[spot, 1:2, lanes] = jnp.sum(weight, axis=0, keepdims=True)
+                mixed = dot(values[lanes], weight.astype(BF16))
+                for p in range(2):
+                    cut = slice(p * 128, p * 128 + 128)
+                    held_ref[spot, g * half_ch + p * 128 : g * half_ch + p * 128 + 128, :] = mixed[cut, cut]
+
+    @pl.loop(1, half // 16 - 1)
+    def _(across):
+        attend_near(across)
+
+    halo_arrive(halo_side)
+    for i, at in ((0, 0), (1, 8 + half)):
+        x = side_ref[i, 3 : 3 + out_rows // 2].astype(F32).reshape(out_rows, 8, channels)
+        ext_ref[:, at : at + 8, :] = x.astype(BF16)
+
+    @pl.loop(0, 2)
+    def _(end):
+        attend_near(end * (half // 16 - 1))
+
+    halo_arrive(halo_far)
+    for i in range(2):
+        seg = slice(0, 3) if i == 0 else slice(3 + out_rows // 2, 6 + out_rows // 2)
+        far_ref[i, :, 8 : 8 + half, :] = vert_ref[i].astype(F32).astype(BF16)
+        for j, at in ((0, 0), (1, 8 + half)):
+            x = side_ref[j, seg].astype(F32).reshape(6, 8, channels)
+            far_ref[i, :, at : at + 8, :] = x.astype(BF16)
+
+    @pl.loop(0, half // 16)
+    def _(across):
+        c0 = pl.multiple_of(across * 16, 16)
+        above = far_ref[0, :, pl.ds(c0, 32), :].reshape(192, channels)
+        below = far_ref[1, :, pl.ds(c0, 32), :].reshape(192, channels)
+        keys, values = keys_values(jnp.concatenate([above[128:], below[:64], above, below], axis=0))
+        for down, seg in ((0, slice(128, 320)), (1, slice(0, 128)), (2, slice(256, 512))):
+            spot = down * (half // 16) + across
+            count = seg.stop - seg.start
             parts = []
             for g in range(2):
                 lanes = slice(g * half_ch, (g + 1) * half_ch)
-                keys = key_ref[pl.ds(down * 4, 16), pl.ds(c0, 32), lanes].reshape(512, half_ch)
-                values = value_ref[pl.ds(down * 4, 16), pl.ds(c0, 32), lanes].reshape(512, half_ch)
-                wide = query[:, lanes]
-                masked = jnp.concatenate(
-                    [jnp.where(lane_head == h, wide, jnp.zeros((), BF16)) for h in range(4)], axis=0
-                )
-                scores = dot_t(masked, keys)
-                scores = scores + bias_ref[down, g * 256 : (g + 1) * 256, :]
-                peak = jnp.max(scores, axis=1, keepdims=True)
+                scores = dot_t(keys[seg, lanes], queries(down, c0, lanes)) + rim_ref[down, :count, lanes]
+                old_peak, old_norm = stat_ref[spot, 0:1, lanes], stat_ref[spot, 1:2, lanes]
+                peak = jnp.maximum(old_peak, jnp.max(scores, axis=0, keepdims=True))
                 weight = jnp.exp(scores - peak)
-                norm = jnp.sum(weight, axis=1, keepdims=True)
-                mixed = dot(weight.astype(BF16), values) * (1.0 / norm)
-                total = jnp.zeros((64, half_ch), F32)
-                for h in range(4):
-                    total = jnp.where(lane_head == h, mixed[h * 64 : (h + 1) * 64], total)
-                parts.append(total.astype(BF16))
-            attended = jnp.concatenate(parts, axis=1)
-            lifted = dot(attended, wout_ref[...])
-            base = coarse_ref[pl.ds(down * 4, 4), pl.ds(c0, 16), :].astype(F32)
-            result = base + lifted.reshape(4, 16, channels)
-            out_ref[pl.ds(down * 4, 4), pl.ds(c0, 16), :] = result.astype(BF16)
+                fade = jnp.exp(old_peak - peak)
+                inverse = 1.0 / (old_norm * fade + jnp.sum(weight, axis=0, keepdims=True))
+                fade = fade * inverse
+                mixed = dot(values[lanes, seg], weight.astype(BF16))
+                for p in range(2):
+                    cut = slice(p * 128, p * 128 + 128)
+                    held = held_ref[spot, g * half_ch + p * 128 : g * half_ch + p * 128 + 128, :]
+                    total = held * fade[:, cut] + mixed[cut, cut] * inverse[:, cut]
+                    parts.append(jnp.where(same_half, total, 0.0).T.astype(BF16))
+            lifted = dot(jnp.concatenate(parts, axis=1), wout_ref[...])
+            base = coarse_ref[down * 4 : down * 4 + 4, pl.ds(c0, 16), :].astype(F32)
+            result = base + (lifted[:64] + lifted[64:]).reshape(4, 16, channels)
+            out_ref[down * 4 : down * 4 + 4, pl.ds(c0, 16), :] = result.astype(BF16)
 
     for copies in (halo_back, halo_obs, halo_norm):
         halo_sent(copies)
@@ -578,7 +630,7 @@
     rows, cols, channels = background.shape
     obs, width = obs_feat.shape
     half, out_rows, both = cols // 2, rows // 2, 2 * width
-    strip = jnp.pad(rel_bias, ((0, 0), (0, 3), (0, 19)), constant_values=NEG).reshape(HEADS, 512)
+    strip = jnp.pad(rel_bias, ((0, 0), (0, 7), (0, 19)), constant_values=NEG).reshape(HEADS, 640)
     vmem = pl.BlockSpec(memory_space=pltpu.VMEM)
     hbm = pl.BlockSpec(memory_space=pl.ANY)
     scratch = [
@@ -614,12 +666,16 @@
         ((2, out_rows // 2 + 6, 16, channels), BF16),
         ((2, out_rows // 2, 16, channels), BF16),
         ((out_rows, half, channels), BF16),
-        ((out_rows + 12, half + 16, channels), BF16),
-        ((out_rows + 12, half + 16, channels), BF16),
-        ((out_rows // 4, HEADS * 64, 512), F32),
+        ((out_rows, half + 16, channels), BF16),
+        ((out_rows // 4, 384, HEADS * 64), F32),
+        ((out_rows // 4, 256, HEADS * 64), F32),
+        ((2, 6, half + 16, channels), BF16),
+        ((channels, channels), BF16),
+        ((out_rows * half // 64, channels, 128), F32),
+        ((out_rows * half // 64, 8, channels), F32),
     ]
     sems = [pltpu.SemaphoreType.DMA((n,)) for n in (4, 4, 2, 34, 34)]
-    sems.append(pltpu.SemaphoreType.REGULAR((owners.bit_length() - 1,)))
+    sems.append(pltpu.SemaphoreType.REGULAR)
     return pl.pallas_call(
         main_kernel,
         name="main",

time: 84.3 us -> 78.9 us (0.936)
  Pallas kernels: 80.4 us -> 75.1 us
    pallas_call x1, Pallas kernels: 80.4 us -> 75.1 us  [body(): pl.pallas_call(main_kernel, name='main', out_shape=jax.ShapeDtypeStruct((...]
where the time goes in v5:
time: 78.9 us; the launch traced here: 78.7 us
  Pallas kernels  75.1 us (95%)
  local copies, waits for them, and re-layouts  3.59 us (5%)
    pallas_call x1, Pallas kernels, body(): pl.pallas_call(main_kernel, name='main', out_shape=jax.ShapeDtypeStruct((...  75.1 us
    unnamed x2, local copies, waits for them, and re-layouts  2.89 us

profile of v5, /device:TPU:9, one launch (start us, length us, event | category | flops | bytes accessed | tf_op | source)
XLA Modules:
  0.0 78.7 jit_solution(6852572837241057789)
XLA Ops:
  0.0 0.8 %copy.16 = f32[8,13,13]{2,1,0:T(8,128)S(1)} copy(f32[8,13,13]{2,0,1:T(8,128)} %param.24) | data formatting | bytes 10816
  0.8 0.7 reshape.31.strip_ref
  1.5 75.1 %main.1 = bf16[12,64,512]{2,1,0:T(8,128)(2,1)} custom-call(s32[1,2048]{1,0:T(1,128)} %bitcast.8, s32[1,2048]{1,0:T(1,128)} %bitcast.9, s32[1,2048]{1,0:T(1,128)} %bitcast.10, bf16[2048,128]{1,0:T(8,128)(2,1)} %feat_ref.1, bf16[24,128,512]{2,1,0:T(8,128)(2,1)} %back_hbm.1, bf16[128,512]{1,0:T(8,128)(2,1)} %win_ref.1, f32[1,512]{1,0:T(1,128)} %bitcast.11, ...), custom_call_target="tpu_custom_call" | custom-call | tf_op jit(solution)/shard_map/main/pallas_call | solution.py:679
  76.6 2.1 %copy.18 = bf16[12,64,512]{2,1,0:T(8,128)(2,1)} copy(bf16[12,64,512]{2,1,0:T(8,128)(2,1)} %main.1) | data formatting | bytes 1572864
  (1 shorter events, 0.0 us)

commit v6 on v5

--- a/solution.py
+++ b/solution.py
@@ -46,15 +46,15 @@
 
 def main_kernel(
     dest_ref, cell_ref, sub_ref, feat_ref, back_hbm, win_ref, dens_ref, conv_hbm, bias_in_ref,
-    gain_ref, wqkv_hbm, strip_ref, wout_hbm,
+    gain_ref, wqkv_hbm, rel_ref, wout_hbm,
     out_ref,
     back_ref, conv_ref, wqkv_ref, wout_ref,
     sendf_ref, sendm_ref, recvf_ref, recvm_ref, pick_ref, group_ref, local_ref,
     edge_ref, brow_ref, bside_ref, line_ref, taps_ref, acc_ref, comp_ref,
     codes_ref, spread_ref, sums_ref, oedge_ref, oline_ref, orow_ref, oside_ref, otaps_ref,
     own_ref, coarse_ref, vert_ref, side_ref, sside_ref, query_ref, ext_ref, bias_ref, rim_ref,
-    far_ref, turned_ref, held_ref, stat_ref,
-    load_sem, route_sem, own_sem, halo_send, halo_recv, meet_sem,
+    far_ref, turned_ref, held_ref, stat_ref, strip_ref,
+    load_sem, route_sem, arrive_sem, own_sem, halo_send, halo_recv, meet_sem,
 ):
     obs, width = feat_ref.shape
     owners = sendf_ref.shape[0]
@@ -177,12 +177,13 @@
     )
     meta = dot_t(narrow(meta), pick_ref[...])
     code = (meta[0:8] * 128.0 + meta[8:16]).astype(I32) * 256 + meta[16:24].astype(I32)
-    mine = iota((8, 128), 1) // 32 == lon
+    spread_by = lax.rem(lat, 4)
+    mine = iota((8, 128), 1) // 32 == spread_by
     for c in range(4):
         chunk = code[:, c * 128 : c * 128 + 128]
         turned = [chunk] + [pltpu.roll(chunk, 32 * k, 1) for k in range(1, 4)]
         for j in range(4):
-            near = (lon - j) & 3
+            near = lax.rem(spread_by - j + 4, 4)
             placed = jnp.where(
                 near < 2,
                 jnp.where(near == 0, turned[0], turned[1]),
@@ -194,9 +195,12 @@
 
     pl.semaphore_wait(meet_sem, len(far))
 
+    kind = lax.rem(lat + lon, 4)
+    home = kind * 32 + lat
+
     @pl.loop(0, owners // 32)
     def _(turn):
-        part = lax.rem(turn + me + me // 4, owners // 32)
+        part = lax.rem(turn + kind, 4)
         group = group_ref[...]
         feat = feat_ref[...]
         wide = jnp.concatenate(
@@ -229,15 +233,15 @@
                 for i, (src, dst) in enumerate(((sendf_ref, recvf_ref), (sendm_ref, recvm_ref))):
                     pltpu.make_async_remote_copy(
                         src_ref=src.at[slot],
-                        dst_ref=dst.at[me],
+                        dst_ref=dst.at[home],
                         send_sem=route_sem.at[i],
-                        recv_sem=route_sem.at[2 + i],
+                        recv_sem=arrive_sem.at[2 * turn + i],
                         device_id=there,
                         device_id_type=MESH,
                     ).start()
 
     own_copies = [
-        pltpu.make_async_copy(src.at[lax.rem(me, 8) * 16 + me // 8], dst.at[me], own_sem.at[i])
+        pltpu.make_async_copy(src.at[lax.rem(me, 8) * 16 + me // 8], dst.at[home], own_sem.at[i])
         for i, (src, dst) in enumerate(((sendf_ref, recvf_ref), (sendm_ref, recvm_ref)))
     ]
     for copy in own_copies:
@@ -337,62 +341,46 @@
     loads[3].wait()
     turned_ref[...] = wqkv_ref[:, 2 * channels :].astype(F32).T.astype(BF16)
 
-    no_up = jnp.where(lat == 0, NEG, 0.0)
-    no_down = jnp.where(lat == lat_count - 1, NEG, 0.0)
-    lane256 = iota((16, 256), 1)
-    for pair in range(HEADS // 2):
-        places = slice(pair * 128, pair * 128 + 128)
-        for down in range(out_rows // 4):
-            inner_part, outer_part = [], []
-            for h in (2 * pair, 2 * pair + 1):
-                strip = jnp.broadcast_to(strip_ref[h : h + 1, :], (16, 640))
-                for r in range(4):
-
-                    def shifted(first_row, lead, size):
-                        amount = (2 + 32 * (r + 4 * down - first_row) + lead) % 640
-                        return pltpu.roll(strip, amount, 1, stride=1, stride_axis=0)[:, :size]
-
-                    inner_part.append(shifted(6, 0, 384))
-                    if down == 0:
-                        outer_part.append(shifted(0, 0, 256) + no_up)
-                    elif down == 1:
-                        outer_part.append(
-                            jnp.where(
-                                lane256 < 64, shifted(4, 0, 256) + no_up, shifted(18, 64, 256) + no_down
-                            )
-                        )
-                    else:
-                        outer_part.append(jnp.where(lane256 < 64, NEG, shifted(18, 64, 256) + no_down))
-            bias_ref[down, :, places] = jnp.concatenate(inner_part, axis=0).T
-            rim_ref[down, :, places] = jnp.concatenate(outer_part, axis=0).T
-
-    for copy in own_copies:
-        copy.wait()
-    rest = pl.ds(0, owners - 1)
-    for i, (src, dst) in enumerate(((sendf_ref, recvf_ref), (sendm_ref, recvm_ref))):
-        pltpu.make_async_copy(src.at[rest], dst.at[rest], route_sem.at[i]).wait()
-        pltpu.make_async_copy(src.at[rest], dst.at[rest], route_sem.at[2 + i]).wait()
-    for group in range(owners // 4):
-        code = recvm_ref[group * 4]
-        for other in range(1, 4):
-            code = code + recvm_ref[group * 4 + other]
-        codes_ref[:, group * 128 : group * 128 + 128] = code
-
     chunk = spread_ref.shape[0]
     lane = narrow(iota((128, 128), 1))
-    for c in range(slots // chunk):
-        code = codes_ref[:, c * chunk : (c + 1) * chunk]
+    sums_ref[...] = jnp.zeros(sums_ref.shape, F32)
+
+    @pl.loop(0, 4)
+    def _(turn):
+        senders = lax.rem(lax.rem(me, 8) // 2 - turn + 4, 4)
+        first = senders * 32
+
+        def arrive(count):
+            some = pl.ds(0, count)
+            for i, (src, dst) in enumerate(((sendf_ref, recvf_ref), (sendm_ref, recvm_ref))):
+                pltpu.make_async_copy(src.at[some], dst.at[some], arrive_sem.at[2 * turn + i]).wait()
+
+        @pl.when(senders == kind)
+        def _():
+            arrive(31)
+            for copy in own_copies:
+                copy.wait()
+
+        @pl.when(senders != kind)
+        def _():
+            arrive(32)
+
+        for group in range(8):
+            code = recvm_ref[first + group * 4]
+            for other in range(1, 4):
+                code = code + recvm_ref[first + group * 4 + other]
+            codes_ref[:, group * 128 : group * 128 + 128] = code
+        code = codes_ref[...]
         sub = code & 255
         cell = (code >> 8) - 128
         row_off = ((sub >> 4).astype(F32) + 0.5) / 16.0 - 0.5
         col_off = ((sub & 15).astype(F32) + 0.5) / 16.0 - 0.5
         kern = jnp.exp(-(row_off * row_off + col_off * col_off) / (2.0 * 0.35 * 0.35))
-        one_hot(pick_ref, cell & 511, kern.astype(BF16))
+        one_hot(pick_ref.at[:, 0:chunk], cell & 511, kern.astype(BF16))
         band = cell >> 9
         for b in range(chunk // 128):
             spot = column(band[:, b * 128 : b * 128 + 128])
-            first = (c * chunk + b * 128) // 32
-            feat = recvf_ref[first : first + 4].reshape(128, width)
+            feat = recvf_ref[pl.ds(first + b * 4, 4)].reshape(128, width)
             lines = slice(b * 128, b * 128 + 128)
             for g in range(rows // 4):
                 here = jnp.full((1, 1), g, F32).astype(BF16)
@@ -402,8 +390,7 @@
             spread_ref[lines, rows // 4 * width :] = jnp.where(
                 spot == lane, jnp.ones((), BF16), jnp.zeros((), BF16)
             )
-        part = dot(pick_ref[...], spread_ref[...])
-        sums_ref[...] = part if c == 0 else sums_ref[...] + part
+        sums_ref[...] += dot(pick_ref[:, 0:chunk], spread_ref[...])
 
     lane_f = iota((cols, width), 1)
     for g in range(rows // 4):
@@ -436,6 +423,38 @@
             if (part, tap) not in ((0, 0), (out_rows // 4 - 1, 3)):
                 total = total + dot(window(otaps4, part, tap)[:, middle], comp_ref[tap, middle, :])
         acc_ref[lines, :] = total
+
+    no_up = jnp.where(lat == 0, NEG, 0.0)
+    no_down = jnp.where(lat == lat_count - 1, NEG, 0.0)
+    strip_ref[...] = jnp.full(strip_ref.shape, NEG, F32)
+    for r in range(rel_ref.shape[1]):
+        strip_ref[:, r * 32 : r * 32 + rel_ref.shape[2]] = rel_ref[:, r, :]
+    lane256 = iota((16, 256), 1)
+    for pair in range(HEADS // 2):
+        places = slice(pair * 128, pair * 128 + 128)
+        for down in range(out_rows // 4):
+            inner_part, outer_part = [], []
+            for h in (2 * pair, 2 * pair + 1):
+                strip = jnp.broadcast_to(strip_ref[h : h + 1, :], (16, 640))
+                for r in range(4):
+
+                    def shifted(first_row, lead, size):
+                        amount = (2 + 32 * (r + 4 * down - first_row) + lead) % 640
+                        return pltpu.roll(strip, amount, 1, stride=1, stride_axis=0)[:, :size]
+
+                    inner_part.append(shifted(6, 0, 384))
+                    if down == 0:
+                        outer_part.append(shifted(0, 0, 256) + no_up)
+                    elif down == 1:
+                        outer_part.append(
+                            jnp.where(
+                                lane256 < 64, shifted(4, 0, 256) + no_up, shifted(18, 64, 256) + no_down
+                            )
+                        )
+                    else:
+                        outer_part.append(jnp.where(lane256 < 64, NEG, shifted(18, 64, 256) + no_down))
+            bias_ref[down, :, places] = jnp.concatenate(inner_part, axis=0).T
+            rim_ref[down, :, places] = jnp.concatenate(outer_part, axis=0).T
 
     halo_arrive(halo_obs)
     for i, at in ((0, 0), (1, rows + 1)):
@@ -493,8 +512,6 @@
         (
             ((0, -1), rim(0, 2, 0), gap(3, 2, 1)),
             ((0, 1), rim(0, 2, 1), gap(3, 2, 0)),
-            ((-1, -1), rim(0, 2, 0), gap(9, 2, 1)),
-            ((-1, 1), rim(0, 2, 1), gap(9, 2, 0)),
             ((-1, 0), own_ref.at[pl.ds(0, 4)], vert_ref.at[1, pl.ds(0, 4)]),
         ),
     )
@@ -505,8 +522,6 @@
         (
             ((0, -1), rim(4, 2, 0), gap(7, 2, 1)),
             ((0, 1), rim(4, 2, 1), gap(7, 2, 0)),
-            ((1, -1), rim(4, 2, 0), gap(1, 2, 1)),
-            ((1, 1), rim(4, 2, 1), gap(1, 2, 0)),
             ((1, 0), own_ref.at[pl.ds(8, 4)], vert_ref.at[0, pl.ds(2, 4)]),
         ),
     )
@@ -517,10 +532,6 @@
         (
             ((0, -1), rim(2, 2, 0), gap(5, 2, 1)),
             ((0, 1), rim(2, 2, 1), gap(5, 2, 0)),
-            ((-1, -1), rim(2, 1, 0), gap(11, 1, 1)),
-            ((-1, 1), rim(2, 1, 1), gap(11, 1, 0)),
-            ((1, -1), rim(3, 1, 0), gap(0, 1, 1)),
-            ((1, 1), rim(3, 1, 1), gap(0, 1, 0)),
             ((-1, 0), own_ref.at[pl.ds(4, 2)], vert_ref.at[1, pl.ds(4, 2)]),
             ((1, 0), own_ref.at[pl.ds(6, 2)], vert_ref.at[0, pl.ds(0, 2)]),
         ),
@@ -572,6 +583,15 @@
         attend_near(across)
 
     halo_arrive(halo_side)
+    halo_corner = halo(
+        34,
+        [
+            ((way, 0), side_ref.at[i, pl.ds(start, 3)], side_ref.at[i, pl.ds(stop, 3)])
+            for i in range(2)
+            for way, start, stop in ((-1, 3, 9), (1, 6, 0))
+        ],
+    )
+    halo_start(halo_corner)
     for i, at in ((0, 0), (1, 8 + half)):
         x = side_ref[i, 3 : 3 + out_rows // 2].astype(F32).reshape(out_rows, 8, channels)
         ext_ref[:, at : at + 8, :] = x.astype(BF16)
@@ -580,7 +600,7 @@
     def _(end):
         attend_near(end * (half // 16 - 1))
 
-    halo_arrive(halo_far)
+    halo_arrive(halo_far + halo_corner)
     for i in range(2):
         seg = slice(0, 3) if i == 0 else slice(3 + out_rows // 2, 6 + out_rows // 2)
         far_ref[i, :, 8 : 8 + half, :] = vert_ref[i].astype(F32).astype(BF16)
@@ -618,7 +638,10 @@
             result = base + (lifted[:64] + lifted[64:]).reshape(4, 16, channels)
             out_ref[down * 4 : down * 4 + 4, pl.ds(c0, 16), :] = result.astype(BF16)
 
-    for copies in (halo_back, halo_obs, halo_norm):
+    rest = pl.ds(0, owners - 1)
+    for i, (src, dst) in enumerate(((sendf_ref, recvf_ref), (sendm_ref, recvm_ref))):
+        pltpu.make_async_copy(src.at[rest], dst.at[rest], route_sem.at[i]).wait()
+    for copies in (halo_back, halo_obs, halo_norm, halo_corner):
         halo_sent(copies)
 
 
@@ -630,7 +653,6 @@
     rows, cols, channels = background.shape
     obs, width = obs_feat.shape
     half, out_rows, both = cols // 2, rows // 2, 2 * width
-    strip = jnp.pad(rel_bias, ((0, 0), (0, 7), (0, 19)), constant_values=NEG).reshape(HEADS, 640)
     vmem = pl.BlockSpec(memory_space=pltpu.VMEM)
     hbm = pl.BlockSpec(memory_space=pl.ANY)
     scratch = [
@@ -652,8 +674,8 @@
         ((rows + 2, half, 4 * channels), BF16),
         ((half * out_rows, channels), F32),
         ((4, 4 * both, channels), BF16),
-        ((1, owners * 32), I32),
-        ((obs, rows // 4 * width + 128), BF16),
+        ((1, owners * 8), I32),
+        ((owners * 8, rows // 4 * width + 128), BF16),
         ((512, rows // 4 * width + 128), F32),
         ((2, rows, both), F32),
         ((2 * both // 128, cols + 16, 128), F32),
@@ -673,8 +695,9 @@
         ((channels, channels), BF16),
         ((out_rows * half // 64, channels, 128), F32),
         ((out_rows * half // 64, 8, channels), F32),
+        ((HEADS, 640), F32),
     ]
-    sems = [pltpu.SemaphoreType.DMA((n,)) for n in (4, 4, 2, 34, 34)]
+    sems = [pltpu.SemaphoreType.DMA((n,)) for n in (4, 2, 8, 2, 38, 38)]
     sems.append(pltpu.SemaphoreType.REGULAR)
     return pl.pallas_call(
         main_kernel,
@@ -698,7 +721,7 @@
         conv_b.reshape(1, channels),
         norm_gain.reshape(1, channels),
         w_qkv,
-        strip,
+        rel_bias,
         w_out,
     )
 

time: 78.9 us -> 76.9 us (0.975)
  Pallas kernels: 75.1 us -> 73.2 us
    pallas_call x1, Pallas kernels: 75.1 us -> 73.2 us  [body(): pl.pallas_call(main_kernel, name='main', out_shape=jax.ShapeDtypeStruct((...]
where the time goes in v6:
time: 76.9 us; the launch traced here: 76.7 us
  Pallas kernels  73.2 us (95%)
  local copies, waits for them, and re-layouts  3.51 us (5%)
    pallas_call x1, Pallas kernels, body(): pl.pallas_call(main_kernel, name='main', out_shape=jax.ShapeDtypeStruct((...  73.2 us
    unnamed x2, local copies, waits for them, and re-layouts  3.51 us

profile of v6, /device:TPU:9, one launch (start us, length us, event | category | flops | bytes accessed | tf_op | source)
XLA Modules:
  0.0 76.7 jit_solution(2711026342259294419)
XLA Ops:
  0.0 1.5 %copy.14.rel_ref = f32[8,13,13]{2,1,0:T(8,128)} copy(f32[8,13,13]{2,0,1:T(8,128)} %param.24) | data formatting | bytes 10816 | tf_op args[11]
  1.5 73.2 %main.1 = bf16[12,64,512]{2,1,0:T(8,128)(2,1)} custom-call(s32[1,2048]{1,0:T(1,128)} %bitcast.8, s32[1,2048]{1,0:T(1,128)} %bitcast.9, s32[1,2048]{1,0:T(1,128)} %bitcast.10, bf16[2048,128]{1,0:T(8,128)(2,1)} %feat_ref.1, bf16[24,128,512]{2,1,0:T(8,128)(2,1)} %back_hbm.1, bf16[128,512]{1,0:T(8,128)(2,1)} %win_ref.1, f32[1,512]{1,0:T(1,128)} %bitcast.11, ...), custom_call_target="tpu_custom_call" | custom-call | tf_op jit(solution)/shard_map/main/pallas_call | solution.py:702
  74.6 2.1 %copy.16 = bf16[12,64,512]{2,1,0:T(8,128)(2,1)} copy(bf16[12,64,512]{2,1,0:T(8,128)(2,1)} %main.1) | data formatting | bytes 1572864

commit v7 on v6

--- a/solution.py
+++ b/solution.py
@@ -10,6 +10,7 @@
 BF16 = jnp.bfloat16
 I32 = jnp.int32
 NEG = -1e30
+LOG2E = 1.4426950408889634
 MESH = pl.DeviceIdType.MESH
 WAYS = ((-1, 0), (1, 0), (0, -1), (0, 1), (-1, -1), (-1, 1), (1, -1), (1, 1))
 
@@ -45,16 +46,16 @@
 
 
 def main_kernel(
-    dest_ref, cell_ref, sub_ref, feat_ref, back_hbm, win_ref, dens_ref, conv_hbm, bias_in_ref,
+    dest_ref, cell_ref, sub_ref, feat_hbm, back_hbm, win_hbm, dens_ref, conv_hbm, bias_in_ref,
     gain_ref, wqkv_hbm, rel_ref, wout_hbm,
-    out_ref,
-    back_ref, conv_ref, wqkv_ref, wout_ref,
+    out_hbm,
+    feat_ref, win_ref, out_ref, back_ref, conv_ref, wqkv_ref, wout_ref,
     sendf_ref, sendm_ref, recvf_ref, recvm_ref, pick_ref, group_ref, local_ref,
     edge_ref, brow_ref, bside_ref, line_ref, taps_ref, acc_ref, comp_ref,
     codes_ref, spread_ref, sums_ref, oedge_ref, oline_ref, orow_ref, oside_ref, otaps_ref,
     own_ref, coarse_ref, vert_ref, side_ref, sside_ref, query_ref, ext_ref, bias_ref, rim_ref,
-    far_ref, turned_ref, held_ref, stat_ref, strip_ref,
-    load_sem, route_sem, arrive_sem, own_sem, halo_send, halo_recv, meet_sem,
+    far_ref, turned_ref, held_ref, stat_ref, strip_ref, keys_ref, values_ref,
+    load_sem, route_sem, arrive_sem, own_sem, out_sem, halo_send, halo_recv, meet_sem,
 ):
     obs, width = feat_ref.shape
     owners = sendf_ref.shape[0]
@@ -70,11 +71,18 @@
     loads = [
         pltpu.make_async_copy(src, dst, load_sem.at[i])
         for i, (src, dst) in enumerate(
-            ((back_hbm, back_ref), (conv_hbm, conv_ref), (wqkv_hbm, wqkv_ref), (wout_hbm, wout_ref))
+            (
+                (back_hbm, back_ref),
+                (conv_hbm, conv_ref),
+                (wqkv_hbm, wqkv_ref),
+                (wout_hbm, wout_ref),
+                (feat_hbm, feat_ref),
+                (win_hbm, win_ref),
+            )
         )
     ]
-    for load in loads:
-        load.start()
+    for i in (0, 4, 5, 1, 2, 3):
+        loads[i].start()
 
     def inside(da):
         return (lat + da >= 0) & (lat + da < lat_count)
@@ -129,11 +137,10 @@
             pl.when(inside(da))(copy.wait_send)
 
     loads[0].wait()
-    for row in range(rows):
-        tile = back_ref[row, 0:16, :].astype(F32)
-        edge_ref[0, row : row + 1, :] = tile[0:1]
-        tile = back_ref[row, cols - 16 : cols, :].astype(F32)
-        edge_ref[1, row : row + 1, :] = tile[15:16]
+    @pl.loop(0, rows)
+    def _(row):
+        edge_ref[0, pl.ds(row, 1), :] = back_ref[row, 0:16, :].astype(F32)[0:1]
+        edge_ref[1, pl.ds(row, 1), :] = back_ref[row, cols - 16 : cols, :].astype(F32)[15:16]
 
     neighbours = 2 + 3 * (inside(-1).astype(I32) + inside(1).astype(I32))
     pl.semaphore_wait(barrier, len(near) + len(far) + neighbours)
@@ -198,6 +205,8 @@
     kind = lax.rem(lat + lon, 4)
     home = kind * 32 + lat
 
+    loads[4].wait()
+
     @pl.loop(0, owners // 32)
     def _(turn):
         part = lax.rem(turn + kind, 4)
@@ -319,6 +328,7 @@
     tail = jnp.where(
         line16 == 0, dens_hi.astype(F32), jnp.where(line16 == 1, dens_lo.astype(F32), 0.0)
     ).astype(BF16)
+    loads[5].wait()
     lift = jnp.concatenate([win_ref[...], tail], axis=0)
 
     @pl.loop(0, 4)
@@ -427,15 +437,17 @@
     no_up = jnp.where(lat == 0, NEG, 0.0)
     no_down = jnp.where(lat == lat_count - 1, NEG, 0.0)
     strip_ref[...] = jnp.full(strip_ref.shape, NEG, F32)
-    for r in range(rel_ref.shape[1]):
-        strip_ref[:, r * 32 : r * 32 + rel_ref.shape[2]] = rel_ref[:, r, :]
+    for r in range(rel_ref.shape[0]):
+        strip_ref[:, r * 32 : r * 32 + rel_ref.shape[2]] = rel_ref[r] * LOG2E
     lane256 = iota((16, 256), 1)
-    for pair in range(HEADS // 2):
-        places = slice(pair * 128, pair * 128 + 128)
+
+    @pl.loop(0, HEADS // 2)
+    def _(pair):
+        places = pl.ds(pl.multiple_of(pair * 128, 128), 128)
         for down in range(out_rows // 4):
             inner_part, outer_part = [], []
-            for h in (2 * pair, 2 * pair + 1):
-                strip = jnp.broadcast_to(strip_ref[h : h + 1, :], (16, 640))
+            for i in range(2):
+                strip = jnp.broadcast_to(strip_ref[pl.ds(2 * pair + i, 1), :], (16, 640))
                 for r in range(4):
 
                     def shifted(first_row, lead, size):
@@ -444,15 +456,16 @@
 
                     inner_part.append(shifted(6, 0, 384))
                     if down == 0:
-                        outer_part.append(shifted(0, 0, 256) + no_up)
+                        found = jnp.where(lane256 < 192, shifted(0, 0, 256) + no_up, NEG)
                     elif down == 1:
-                        outer_part.append(
-                            jnp.where(
-                                lane256 < 64, shifted(4, 0, 256) + no_up, shifted(18, 64, 256) + no_down
-                            )
+                        found = jnp.where(
+                            lane256 < 64,
+                            shifted(4, 0, 256) + no_up,
+                            jnp.where(lane256 < 128, shifted(18, 64, 256) + no_down, NEG),
                         )
                     else:
-                        outer_part.append(jnp.where(lane256 < 64, NEG, shifted(18, 64, 256) + no_down))
+                        found = jnp.where(lane256 < 64, NEG, shifted(18, 64, 256) + no_down)
+                    outer_part.append(found)
             bias_ref[down, :, places] = jnp.concatenate(inner_part, axis=0).T
             rim_ref[down, :, places] = jnp.concatenate(outer_part, axis=0).T
 
@@ -461,16 +474,16 @@
         lay(otaps_ref, oline_ref, i, at, orow_ref[i], None, None)
     first_line = iota((16, both), 0) == 0
     last_line = iota((16, both), 0) == 15
-    for at in range(rows + 2):
+    @pl.loop(0, rows + 2)
+    def _(at):
         old = otaps_ref[at, 0:16, 0:both].astype(F32)
         otaps_ref[at, 0:16, 0:both] = jnp.where(
-            first_line, oside_ref[0, at + 7 : at + 8, :], old
+            first_line, oside_ref[0, pl.ds(at + 7, 1), :], old
         ).astype(BF16)
         old = otaps_ref[at, half - 16 : half, 3 * both :].astype(F32)
         otaps_ref[at, half - 16 : half, 3 * both :] = jnp.where(
-            last_line, oside_ref[1, at + 7 : at + 8, :], old
+            last_line, oside_ref[1, pl.ds(at + 7, 1), :], old
         ).astype(BF16)
-
 
     outer = (slice(0, both), slice(3 * both, 4 * both))
 
@@ -544,7 +557,7 @@
     @pl.loop(0, out_rows // 4)
     def _(part):
         own = own_ref[pl.ds(part * 4, 4)].reshape(block, channels)
-        query = dot(own, wqkv_ref[:, :channels]).astype(BF16) * 0.125
+        query = dot(own, wqkv_ref[:, :channels]) * (0.125 * LOG2E)
         query_ref[pl.ds(part * 4, 4)] = query.astype(BF16).reshape(4, half, channels)
 
     half_ch = channels // 2
@@ -556,49 +569,56 @@
         return keys, dot_t(turned_ref[...], x).astype(BF16)
 
     def queries(down, c0, lanes):
-        wide = query_ref[down * 4 : down * 4 + 4, pl.ds(c0, 16), lanes].reshape(64, half_ch)
+        wide = query_ref[pl.ds(down * 4, 4), pl.ds(c0, 16), lanes].reshape(64, half_ch)
         return jnp.concatenate(
             [jnp.where(lane_head == h, wide, jnp.zeros((), BF16)) for h in range(4)], axis=0
         )
 
-    def attend_near(across):
+    corners = [
+        ((way, 0), side_ref.at[i, pl.ds(start, 3)], side_ref.at[i, pl.ds(stop, 3)])
+        for i in range(2)
+        for way, start, stop in ((-1, 3, 9), (1, 6, 0))
+    ]
+
+    tall = 32 * out_rows
+
+    @pl.loop(0, half // 16)
+    def _(turn):
+        across = lax.rem(turn + 1, half // 16)
+
+        @pl.when(turn == half // 16 - 2)
+        def _():
+            halo_arrive(halo_side)
+            halo_start(halo(34, corners))
+            for i, at in ((0, 0), (1, 8 + half)):
+                x = side_ref[i, 3 : 3 + out_rows // 2].astype(F32).reshape(out_rows, 8, channels)
+                ext_ref[:, at : at + 8, :] = x.astype(BF16)
+
         c0 = pl.multiple_of(across * 16, 16)
-        keys, values = keys_values(ext_ref[:, pl.ds(c0, 32), :].reshape(32 * out_rows, channels))
-        for down in range(out_rows // 4):
+        keys, values = keys_values(ext_ref[:, pl.ds(c0, 32), :].reshape(tall, channels))
+        keys_ref[0:tall, :] = keys
+        values_ref[:, 0:tall] = values
+
+        @pl.loop(0, out_rows // 4)
+        def _(down):
             spot = down * (half // 16) + across
             for g in range(2):
                 lanes = slice(g * half_ch, (g + 1) * half_ch)
-                scores = dot_t(keys[:, lanes], queries(down, c0, lanes)) + bias_ref[down, :, lanes]
+                scores = dot_t(keys_ref[0:tall, lanes], queries(down, c0, lanes)) + bias_ref[down, :, lanes]
                 peak = jnp.max(scores, axis=0, keepdims=True)
-                weight = jnp.exp(scores - peak)
+                weight = jnp.exp2(scores - peak)
                 stat_ref[spot, 0:1, lanes] = peak
                 stat_ref[spot, 1:2, lanes] = jnp.sum(weight, axis=0, keepdims=True)
-                mixed = dot(values[lanes], weight.astype(BF16))
+                mixed = dot(values_ref[lanes, 0:tall], weight.astype(BF16))
                 for p in range(2):
                     cut = slice(p * 128, p * 128 + 128)
                     held_ref[spot, g * half_ch + p * 128 : g * half_ch + p * 128 + 128, :] = mixed[cut, cut]
 
-    @pl.loop(1, half // 16 - 1)
-    def _(across):
-        attend_near(across)
-
-    halo_arrive(halo_side)
-    halo_corner = halo(
-        34,
-        [
-            ((way, 0), side_ref.at[i, pl.ds(start, 3)], side_ref.at[i, pl.ds(stop, 3)])
-            for i in range(2)
-            for way, start, stop in ((-1, 3, 9), (1, 6, 0))
-        ],
-    )
-    halo_start(halo_corner)
-    for i, at in ((0, 0), (1, 8 + half)):
-        x = side_ref[i, 3 : 3 + out_rows // 2].astype(F32).reshape(out_rows, 8, channels)
-        ext_ref[:, at : at + 8, :] = x.astype(BF16)
-
-    @pl.loop(0, 2)
-    def _(end):
-        attend_near(end * (half // 16 - 1))
+    halo_corner = halo(34, corners)
+
+    def out_copy(across):
+        some = pl.ds(pl.multiple_of(across * 16, 16), 16)
+        return pltpu.make_async_copy(out_ref.at[:, some], out_hbm.at[:, some], out_sem.at[across])
 
     halo_arrive(halo_far + halo_corner)
     for i in range(2):
@@ -614,29 +634,39 @@
         above = far_ref[0, :, pl.ds(c0, 32), :].reshape(192, channels)
         below = far_ref[1, :, pl.ds(c0, 32), :].reshape(192, channels)
         keys, values = keys_values(jnp.concatenate([above[128:], below[:64], above, below], axis=0))
-        for down, seg in ((0, slice(128, 320)), (1, slice(0, 128)), (2, slice(256, 512))):
+        keys_ref[...] = keys
+        values_ref[...] = values
+
+        @pl.loop(0, out_rows // 4)
+        def _(down):
+            seg = pl.ds(pl.multiple_of(lax.rem(2 * down + 1, 3) * 128, 128), 256)
             spot = down * (half // 16) + across
-            count = seg.stop - seg.start
             parts = []
             for g in range(2):
                 lanes = slice(g * half_ch, (g + 1) * half_ch)
-                scores = dot_t(keys[seg, lanes], queries(down, c0, lanes)) + rim_ref[down, :count, lanes]
+                scores = dot_t(keys_ref[seg, lanes], queries(down, c0, lanes)) + rim_ref[down, :, lanes]
                 old_peak, old_norm = stat_ref[spot, 0:1, lanes], stat_ref[spot, 1:2, lanes]
                 peak = jnp.maximum(old_peak, jnp.max(scores, axis=0, keepdims=True))
-                weight = jnp.exp(scores - peak)
-                fade = jnp.exp(old_peak - peak)
+                weight = jnp.exp2(scores - peak)
+                fade = jnp.exp2(old_peak - peak)
                 inverse = 1.0 / (old_norm * fade + jnp.sum(weight, axis=0, keepdims=True))
                 fade = fade * inverse
-                mixed = dot(values[lanes, seg], weight.astype(BF16))
+                mixed = dot(values_ref[lanes, seg], weight.astype(BF16))
                 for p in range(2):
                     cut = slice(p * 128, p * 128 + 128)
                     held = held_ref[spot, g * half_ch + p * 128 : g * half_ch + p * 128 + 128, :]
                     total = held * fade[:, cut] + mixed[cut, cut] * inverse[:, cut]
                     parts.append(jnp.where(same_half, total, 0.0).T.astype(BF16))
             lifted = dot(jnp.concatenate(parts, axis=1), wout_ref[...])
-            base = coarse_ref[down * 4 : down * 4 + 4, pl.ds(c0, 16), :].astype(F32)
+            base = coarse_ref[pl.ds(down * 4, 4), pl.ds(c0, 16), :].astype(F32)
             result = base + (lifted[:64] + lifted[64:]).reshape(4, 16, channels)
-            out_ref[down * 4 : down * 4 + 4, pl.ds(c0, 16), :] = result.astype(BF16)
+            out_ref[pl.ds(down * 4, 4), pl.ds(c0, 16), :] = result.astype(BF16)
+
+        out_copy(across).start()
+
+    @pl.loop(0, half // 16)
+    def _(across):
+        out_copy(across).wait()
 
     rest = pl.ds(0, owners - 1)
     for i, (src, dst) in enumerate(((sendf_ref, recvf_ref), (sendm_ref, recvm_ref))):
@@ -656,6 +686,9 @@
     vmem = pl.BlockSpec(memory_space=pltpu.VMEM)
     hbm = pl.BlockSpec(memory_space=pl.ANY)
     scratch = [
+        ((obs, width), BF16),
+        ((width, channels), BF16),
+        ((out_rows, half, channels), BF16),
         ((rows, cols, channels), BF16),
         ((4, 4 * channels, channels), BF16),
         ((channels, 3 * channels), BF16),
@@ -696,15 +729,17 @@
         ((out_rows * half // 64, channels, 128), F32),
         ((out_rows * half // 64, 8, channels), F32),
         ((HEADS, 640), F32),
+        ((512, channels), BF16),
+        ((channels, 512), BF16),
     ]
-    sems = [pltpu.SemaphoreType.DMA((n,)) for n in (4, 2, 8, 2, 38, 38)]
+    sems = [pltpu.SemaphoreType.DMA((n,)) for n in (6, 2, 8, 2, half // 16, 38, 38)]
     sems.append(pltpu.SemaphoreType.REGULAR)
     return pl.pallas_call(
         main_kernel,
         name="main",
         out_shape=jax.ShapeDtypeStruct((out_rows, half, channels), BF16),
-        in_specs=[vmem, vmem, vmem, vmem, hbm, vmem, vmem, hbm, vmem, vmem, hbm, vmem, hbm],
-        out_specs=vmem,
+        in_specs=[vmem, vmem, vmem, hbm, hbm, hbm, vmem, hbm, vmem, vmem, hbm, vmem, hbm],
+        out_specs=hbm,
         scratch_shapes=[pltpu.VMEM(shape, dtype) for shape, dtype in scratch] + sems,
         compiler_params=pltpu.CompilerParams(
             collective_id=0, has_side_effects=True, vmem_limit_bytes=62 << 20
@@ -721,7 +756,7 @@
         conv_b.reshape(1, channels),
         norm_gain.reshape(1, channels),
         w_qkv,
-        rel_bias,
+        jnp.transpose(rel_bias, (1, 0, 2)),
         w_out,
     )
 

time: 76.9 us -> 78.6 us (1.022)
  Pallas kernels: 73.2 us -> 76.3 us
  local copies, waits for them, and re-layouts: 3.51 us -> 2.06 us
    pallas_call x1, Pallas kernels: 73.2 us -> 76.3 us  [body(): pl.pallas_call(main_kernel, name='main', out_shape=jax.ShapeDtypeStruct((...]
    unnamed x2 -> x1, local copies, waits for them, and re-layouts: 3.51 us -> 2.06 us
where the time goes in v7:
time: 78.6 us; the launch traced here: 78.4 us
  Pallas kernels  76.3 us (97%)
  local copies, waits for them, and re-layouts  2.06 us (3%)
    pallas_call x1, Pallas kernels, body(): pl.pallas_call(main_kernel, name='main', out_shape=jax.ShapeDtypeStruct((...  76.3 us
    unnamed x1, local copies, waits for them, and re-layouts  2.06 us

profile of v7, /device:TPU:9, one launch (start us, length us, event | category | flops | bytes accessed | tf_op | source)
XLA Modules:
  0.0 78.4 jit_solution(9331958234786834385)
XLA Ops:
  0.0 76.3 %main.1 = bf16[12,64,512]{2,1,0:T(8,128)(2,1)} custom-call(s32[1,2048]{1,0:T(1,128)} %bitcast.10, s32[1,2048]{1,0:T(1,128)} %bitcast.11, s32[1,2048]{1,0:T(1,128)} %bitcast.12, bf16[2048,128]{1,0:T(8,128)(2,1)} %feat_hbm.1, bf16[24,128,512]{2,1,0:T(8,128)(2,1)} %back_hbm.1, bf16[128,512]{1,0:T(8,128)(2,1)} %win_hbm.1, f32[1,512]{1,0:T(1,128)} %bitcast.13, ...), custom_call_target="tpu_custom_call" | custom-call | tf_op jit(solution)/shard_map/main/pallas_call | solution.py:737
  76.4 2.1 %copy.15 = bf16[12,64,512]{2,1,0:T(8,128)(2,1)} copy(bf16[12,64,512]{2,1,0:T(8,128)(2,1)} %main.1) | data formatting | bytes 1572864

commit v8 on v6

--- a/solution.py
+++ b/solution.py
@@ -10,6 +10,7 @@
 BF16 = jnp.bfloat16
 I32 = jnp.int32
 NEG = -1e30
+LOG2E = 1.4426950408889634
 MESH = pl.DeviceIdType.MESH
 WAYS = ((-1, 0), (1, 0), (0, -1), (0, 1), (-1, -1), (-1, 1), (1, -1), (1, 1))
 
@@ -45,16 +46,16 @@
 
 
 def main_kernel(
-    dest_ref, cell_ref, sub_ref, feat_ref, back_hbm, win_ref, dens_ref, conv_hbm, bias_in_ref,
+    dest_ref, cell_ref, sub_ref, feat_hbm, back_hbm, win_hbm, dens_ref, conv_hbm, bias_in_ref,
     gain_ref, wqkv_hbm, rel_ref, wout_hbm,
-    out_ref,
-    back_ref, conv_ref, wqkv_ref, wout_ref,
+    out_hbm,
+    feat_ref, win_ref, out_ref, back_ref, conv_ref, wqkv_ref, wout_ref,
     sendf_ref, sendm_ref, recvf_ref, recvm_ref, pick_ref, group_ref, local_ref,
     edge_ref, brow_ref, bside_ref, line_ref, taps_ref, acc_ref, comp_ref,
     codes_ref, spread_ref, sums_ref, oedge_ref, oline_ref, orow_ref, oside_ref, otaps_ref,
     own_ref, coarse_ref, vert_ref, side_ref, sside_ref, query_ref, ext_ref, bias_ref, rim_ref,
     far_ref, turned_ref, held_ref, stat_ref, strip_ref,
-    load_sem, route_sem, arrive_sem, own_sem, halo_send, halo_recv, meet_sem,
+    load_sem, route_sem, arrive_sem, own_sem, out_sem, halo_send, halo_recv, meet_sem,
 ):
     obs, width = feat_ref.shape
     owners = sendf_ref.shape[0]
@@ -70,11 +71,18 @@
     loads = [
         pltpu.make_async_copy(src, dst, load_sem.at[i])
         for i, (src, dst) in enumerate(
-            ((back_hbm, back_ref), (conv_hbm, conv_ref), (wqkv_hbm, wqkv_ref), (wout_hbm, wout_ref))
+            (
+                (back_hbm, back_ref),
+                (conv_hbm, conv_ref),
+                (wqkv_hbm, wqkv_ref),
+                (wout_hbm, wout_ref),
+                (feat_hbm, feat_ref),
+                (win_hbm, win_ref),
+            )
         )
     ]
-    for load in loads:
-        load.start()
+    for i in (0, 4, 5, 1, 2, 3):
+        loads[i].start()
 
     def inside(da):
         return (lat + da >= 0) & (lat + da < lat_count)
@@ -198,6 +206,8 @@
     kind = lax.rem(lat + lon, 4)
     home = kind * 32 + lat
 
+    loads[4].wait()
+
     @pl.loop(0, owners // 32)
     def _(turn):
         part = lax.rem(turn + kind, 4)
@@ -319,6 +329,7 @@
     tail = jnp.where(
         line16 == 0, dens_hi.astype(F32), jnp.where(line16 == 1, dens_lo.astype(F32), 0.0)
     ).astype(BF16)
+    loads[5].wait()
     lift = jnp.concatenate([win_ref[...], tail], axis=0)
 
     @pl.loop(0, 4)
@@ -427,8 +438,8 @@
     no_up = jnp.where(lat == 0, NEG, 0.0)
     no_down = jnp.where(lat == lat_count - 1, NEG, 0.0)
     strip_ref[...] = jnp.full(strip_ref.shape, NEG, F32)
-    for r in range(rel_ref.shape[1]):
-        strip_ref[:, r * 32 : r * 32 + rel_ref.shape[2]] = rel_ref[:, r, :]
+    for r in range(rel_ref.shape[0]):
+        strip_ref[:, r * 32 : r * 32 + rel_ref.shape[2]] = rel_ref[r] * LOG2E
     lane256 = iota((16, 256), 1)
     for pair in range(HEADS // 2):
         places = slice(pair * 128, pair * 128 + 128)
@@ -544,7 +555,7 @@
     @pl.loop(0, out_rows // 4)
     def _(part):
         own = own_ref[pl.ds(part * 4, 4)].reshape(block, channels)
-        query = dot(own, wqkv_ref[:, :channels]).astype(BF16) * 0.125
+        query = dot(own, wqkv_ref[:, :channels]) * (0.125 * LOG2E)
         query_ref[pl.ds(part * 4, 4)] = query.astype(BF16).reshape(4, half, channels)
 
     half_ch = channels // 2
@@ -570,7 +581,7 @@
                 lanes = slice(g * half_ch, (g + 1) * half_ch)
                 scores = dot_t(keys[:, lanes], queries(down, c0, lanes)) + bias_ref[down, :, lanes]
                 peak = jnp.max(scores, axis=0, keepdims=True)
-                weight = jnp.exp(scores - peak)
+                weight = jnp.exp2(scores - peak)
                 stat_ref[spot, 0:1, lanes] = peak
                 stat_ref[spot, 1:2, lanes] = jnp.sum(weight, axis=0, keepdims=True)
                 mixed = dot(values[lanes], weight.astype(BF16))
@@ -599,6 +610,10 @@
     @pl.loop(0, 2)
     def _(end):
         attend_near(end * (half // 16 - 1))
+
+    def out_copy(across):
+        some = pl.ds(pl.multiple_of(across * 16, 16), 16)
+        return pltpu.make_async_copy(out_ref.at[:, some], out_hbm.at[:, some], out_sem.at[across])
 
     halo_arrive(halo_far + halo_corner)
     for i in range(2):
@@ -623,8 +638,8 @@
                 scores = dot_t(keys[seg, lanes], queries(down, c0, lanes)) + rim_ref[down, :count, lanes]
                 old_peak, old_norm = stat_ref[spot, 0:1, lanes], stat_ref[spot, 1:2, lanes]
                 peak = jnp.maximum(old_peak, jnp.max(scores, axis=0, keepdims=True))
-                weight = jnp.exp(scores - peak)
-                fade = jnp.exp(old_peak - peak)
+                weight = jnp.exp2(scores - peak)
+                fade = jnp.exp2(old_peak - peak)
                 inverse = 1.0 / (old_norm * fade + jnp.sum(weight, axis=0, keepdims=True))
                 fade = fade * inverse
                 mixed = dot(values[lanes, seg], weight.astype(BF16))
@@ -637,6 +652,11 @@
             base = coarse_ref[down * 4 : down * 4 + 4, pl.ds(c0, 16), :].astype(F32)
             result = base + (lifted[:64] + lifted[64:]).reshape(4, 16, channels)
             out_ref[down * 4 : down * 4 + 4, pl.ds(c0, 16), :] = result.astype(BF16)
+        out_copy(across).start()
+
+    @pl.loop(0, half // 16)
+    def _(across):
+        out_copy(across).wait()
 
     rest = pl.ds(0, owners - 1)
     for i, (src, dst) in enumerate(((sendf_ref, recvf_ref), (sendm_ref, recvm_ref))):
@@ -656,6 +676,9 @@
     vmem = pl.BlockSpec(memory_space=pltpu.VMEM)
     hbm = pl.BlockSpec(memory_space=pl.ANY)
     scratch = [
+        ((obs, width), BF16),
+        ((width, channels), BF16),
+        ((out_rows, half, channels), BF16),
         ((rows, cols, channels), BF16),
         ((4, 4 * channels, channels), BF16),
         ((channels, 3 * channels), BF16),
@@ -697,14 +720,14 @@
         ((out_rows * half // 64, 8, channels), F32),
         ((HEADS, 640), F32),
     ]
-    sems = [pltpu.SemaphoreType.DMA((n,)) for n in (4, 2, 8, 2, 38, 38)]
+    sems = [pltpu.SemaphoreType.DMA((n,)) for n in (6, 2, 8, 2, half // 16, 38, 38)]
     sems.append(pltpu.SemaphoreType.REGULAR)
     return pl.pallas_call(
         main_kernel,
         name="main",
         out_shape=jax.ShapeDtypeStruct((out_rows, half, channels), BF16),
-        in_specs=[vmem, vmem, vmem, vmem, hbm, vmem, vmem, hbm, vmem, vmem, hbm, vmem, hbm],
-        out_specs=vmem,
+        in_specs=[vmem, vmem, vmem, hbm, hbm, hbm, vmem, hbm, vmem, vmem, hbm, vmem, hbm],
+        out_specs=hbm,
         scratch_shapes=[pltpu.VMEM(shape, dtype) for shape, dtype in scratch] + sems,
         compiler_params=pltpu.CompilerParams(
             collective_id=0, has_side_effects=True, vmem_limit_bytes=62 << 20
@@ -721,7 +744,7 @@
         conv_b.reshape(1, channels),
         norm_gain.reshape(1, channels),
         w_qkv,
-        rel_bias,
+        jnp.transpose(rel_bias, (1, 0, 2)),
         w_out,
     )
 

time: 76.9 us -> 74.8 us (0.973)
  local copies, waits for them, and re-layouts: 3.51 us -> 2.06 us
    unnamed x2 -> x1, local copies, waits for them, and re-layouts: 3.51 us -> 2.06 us
where the time goes in v8:
time: 74.8 us; the launch traced here: 74.6 us
  Pallas kernels  72.6 us (97%)
  local copies, waits for them, and re-layouts  2.06 us (3%)
    pallas_call x1, Pallas kernels, body(): pl.pallas_call(main_kernel, name='main', out_shape=jax.ShapeDtypeStruct((...  72.6 us
    unnamed x1, local copies, waits for them, and re-layouts  2.06 us

profile of v8, /device:TPU:9, one launch (start us, length us, event | category | flops | bytes accessed | tf_op | source)
XLA Modules:
  0.0 74.6 jit_solution(17636686792342254989)
XLA Ops:
  0.0 72.6 %main.1 = bf16[12,64,512]{2,1,0:T(8,128)(2,1)} custom-call(s32[1,2048]{1,0:T(1,128)} %bitcast.10, s32[1,2048]{1,0:T(1,128)} %bitcast.11, s32[1,2048]{1,0:T(1,128)} %bitcast.12, bf16[2048,128]{1,0:T(8,128)(2,1)} %feat_hbm.1, bf16[24,128,512]{2,1,0:T(8,128)(2,1)} %back_hbm.1, bf16[128,512]{1,0:T(8,128)(2,1)} %win_hbm.1, f32[1,512]{1,0:T(1,128)} %bitcast.13, ...), custom_call_target="tpu_custom_call" | custom-call | tf_op jit(solution)/shard_map/main/pallas_call | solution.py:725
  72.6 2.1 %copy.15 = bf16[12,64,512]{2,1,0:T(8,128)(2,1)} copy(bf16[12,64,512]{2,1,0:T(8,128)(2,1)} %main.1) | data formatting | bytes 1572864
